TPU v7x, 128 devices: a whole 4x4x4 slice. The times are simulated.
128 devices in a mesh: prow: 4 (over x), pcol: 32 (over z, y, core).
Axes of the slice: x: 4, y: 4, z: 4, core: 2. Of those that a mesh axis runs over, the one named last changes fastest.
Arguments:
- trail_u: bfloat16 [8, 32, 2048, 256], P('prow', 'pcol'), may hold values from -6 to 6
- trail_v: bfloat16 [8, 32, 2048, 256], P('prow', 'pcol'), may hold values from -6 to 6
- tile_rank: int32 [8, 32], P('prow', 'pcol'), may hold values from 32 to 256
- new_rank: int32 [8, 32], P('prow', 'pcol'), may hold values from 32 to 256, as said below
- row_u: bfloat16 [8, 2048, 256], P('prow', 'pcol'), may hold values from -6 to 6
- row_v: bfloat16 [8, 2048, 256], P('prow', 'pcol'), may hold values from -0.23925781 to 0.23925781
- row_rank: int32 [8], replicated, may hold values from 32 to 256
- col_u: bfloat16 [32, 2048, 256], P('prow', 'pcol'), may hold values from -6 to 6
- col_v: bfloat16 [32, 2048, 256], P('prow', 'pcol'), may hold values from -0.23925781 to 0.23925781
- col_rank: int32 [32], replicated, may hold values from 32 to 256
- diag_inv: float32 [2048, 2048], P('pcol'), as said below
- sketch: bfloat16 [2048, 256], replicated, may hold values from -0.125 to 0.125
Outputs:
- fresh_u: bfloat16 [8, 32, 2048, 256], P('prow', 'pcol')
- fresh_v: bfloat16 [8, 32, 2048, 256], P('prow', 'pcol')
Inputs may be any that keep to these rules, and one draw needn't show every extreme that they name: new_rank[i, j] is at most tile_rank[i, j]. `diag_inv`: lower triangular with diagonal entries between 1 and 2.
All inputs are finite; a program needn't handle non-finite values.
Results may differ from a plain program's by a relative error of at most 0.015.
Values may be sent and summed in bfloat16 or wider, within the bound.
No kernel may reach another device: no remote copies, remote signals or barrier semaphores. Data moves between devices by JAX's collectives and lax.ppermute only.
A program may use at most 128 MiB of HBM per device.

v0:
```python
import math

import jax
import jax.numpy as jnp
from jax import lax
from jax.sharding import PartitionSpec as P


def keep_columns(factor, rank):
    columns = jnp.arange(factor.shape[-1], dtype=jnp.int32)
    keep = (columns[None, :] < rank[:, None]).astype(factor.dtype)
    return factor * keep[:, None, :]


def on_device(
    trail_u,
    trail_v,
    tile_rank,
    new_rank,
    row_u,
    row_v,
    row_rank,
    col_u,
    col_v,
    col_rank,
    diag_inv,
    sketch,
):
    trow, tcol, width, rmax = trail_u.shape
    cslab = col_u.shape[0]
    here_row = lax.axis_index("prow")
    own_row_rank = lax.dynamic_slice_in_dim(row_rank, here_row * trow, trow)
    own_col_rank = lax.dynamic_slice_in_dim(col_rank, here_row * cslab, cslab)
    rows_u = keep_columns(row_u, own_row_rank)
    cols_u = keep_columns(col_u, own_col_rank)
    stacked = jnp.concatenate(
        [keep_columns(row_v, own_row_rank), keep_columns(col_v, own_col_rank)], axis=0
    )
    solved = jnp.einsum(
        "ab,tbk->tak",
        diag_inv,
        lax.all_gather(stacked, "pcol", axis=1, tiled=True).astype(jnp.float32),
        precision=lax.Precision.HIGHEST,
    ).astype(jnp.bfloat16)
    row_w = solved[:trow]
    col_w = solved[trow:]
    row_u_full, row_w_full = (
        lax.all_gather(rows_u, "pcol", axis=1, tiled=True),
        lax.all_gather(row_w, "pcol", axis=1, tiled=True),
    )
    col_u_all, col_w_all = (
        lax.all_gather(cols_u, "prow", axis=0, tiled=True),
        lax.all_gather(col_w, "prow", axis=0, tiled=True),
    )
    col_u_own, col_w_own = (
        lax.all_to_all(col_u_all, "pcol", split_axis=0, concat_axis=1, tiled=True),
        lax.all_to_all(col_w_all, "pcol", split_axis=0, concat_axis=1, tiled=True),
    )
    coupling = jnp.einsum(
        "rbk,cbl->crkl", row_w_full, col_w_own, preferred_element_type=jnp.float32
    ).astype(jnp.bfloat16)
    columns = jnp.arange(rmax, dtype=jnp.int32)
    alive = (columns[None, None, :] < tile_rank[:, :, None]).astype(jnp.bfloat16)
    left = trail_u * alive[:, :, None, :]
    right = trail_v * alive[:, :, None, :]
    shift = jnp.einsum(
        "cbl,crkl->rcbk", col_u_own, coupling, preferred_element_type=jnp.float32
    ).astype(jnp.bfloat16)
    left_cat = jnp.concatenate([left, row_u_full[:, None]], axis=3)
    right_cat = jnp.concatenate([right, -shift], axis=3)
    keep = columns[None, None, :] < new_rank[:, :, None]
    probe_in = sketch[None, None] * keep.astype(jnp.bfloat16)[:, :, None, :]
    probe = jnp.einsum(
        "rcbm,rcbk->rcmk", right_cat, probe_in, preferred_element_type=jnp.float32
    ).astype(jnp.bfloat16)
    range_y = jnp.einsum("rcbm,rcmk->rcbk", left_cat, probe, preferred_element_type=jnp.float32)
    gram = jnp.einsum("rcbk,rcbl->rckl", range_y, range_y, precision=lax.Precision.HIGHEST)
    gram = gram + (1.0 - keep.astype(jnp.float32))[:, :, :, None] * jnp.eye(rmax, dtype=jnp.float32)
    lower = jnp.linalg.cholesky(gram)
    basis = lax.linalg.triangular_solve(
        lower, range_y, left_side=False, lower=True, transpose_a=True
    )
    fresh_u = (basis * math.sqrt(width)).astype(jnp.bfloat16)
    back = jnp.einsum(
        "rcbm,rcbk->rcmk", left_cat, fresh_u, preferred_element_type=jnp.float32
    ).astype(jnp.bfloat16)
    fresh_v = (
        jnp.einsum("rcbm,rcmk->rcbk", right_cat, back, preferred_element_type=jnp.float32) / width
    ).astype(jnp.bfloat16)
    return (fresh_u, fresh_v)


def solution(mesh):
    return jax.shard_map(
        on_device,
        mesh=mesh,
        in_specs=(
            P("prow", "pcol", None, None),
            P("prow", "pcol", None, None),
            P("prow", "pcol"),
            P("prow", "pcol"),
            P("prow", "pcol", None),
            P("prow", "pcol", None),
            P(),
            P("prow", "pcol", None),
            P("prow", "pcol", None),
            P(),
            P("pcol", None),
            P(),
        ),
        out_specs=(P("prow", "pcol", None, None), P("prow", "pcol", None, None)),
        check_vma=False,
    )
```

profile of v0, /device:TPU:1, one launch (start us, length us, event | category | flops | bytes accessed | tf_op | source)
XLA Modules:
  0.0 385.2 jit_solution(11781857096204658299)
XLA Ops:
  7.2 0.8 dynamic_slice.6
  8.1 0.7 dynamic_slice.7
  8.9 1.5 broadcast_multiply_fusion.2
  10.4 1.8 broadcast_multiply_fusion.1
  12.2 0.8 pad_maximum_fusion
  13.8 60.9 %all-gather.8.cloned.1.call-done = bf16[10,2048,256]{2,1,0:T(8,128)(2,1)} async-done(((bf16[10,64,256]{2,1,0:T(8,128)(2,1)}), bf16[10,2048,256]{2,1,0:T(8,128)(2,1)}) %all-gather.8.cloned.1.call-update) | async-done | bytes 10485776 | tf_op jit(solution)/shard_map/all_gather | solution.py:42
  74.7 8.1 %fusion.20 = bf16[10,64,256]{2,1,0:T(8,128)(2,1)S(1)} fusion(bf16[10,2048,256]{2,1,0:T(8,128)(2,1)} %all-gather.8.cloned.1.call-done, f32[64,2048]{1,0:T(8,128)S(1)} %copy-done), kind=kOutput, calls=%fused_computation.30 | convolution fusion | flops 4026695680 | bytes 11337728 | tf_op jit(solution)/shard_map/ab,tbk->tak/dot_general | solution.py:39
  82.8 0.7 slice.65
  84.9 14.2 %all-gather.14.cloned.1.call-done = bf16[32,64,256]{2,1,0:T(8,128)(2,1)} async-done(((bf16[8,64,256]{2,1,0:T(8,128)(2,1)}), bf16[32,64,256]{2,1,0:T(8,128)(2,1)}) %all-gather.14.cloned.1.call-update) | async-done | bytes 1048592 | tf_op jit(solution)/shard_map/all_gather | solution.py:52
  99.0 8.7 %all-to-all-start.1 = ((bf16[32,64,256]{2,1,0:T(8,128)(2,1)}), bf16[32,64,256]{2,1,0:T(8,128)(2,1)}, u32[]{:S(2)}, u32[]{:S(2)}) async-start(bf16[32,64,256]{2,1,0:T(8,128)(2,1)} %all-gather.14.cloned.1.call-done), calls=%async_computation.1 | async-start | bytes 2097152 | tf_op jit(solution)/shard_map/all_to_all | solution.py:56
  107.9 17.0 %all-to-all-done.1 = bf16[32,64,256]{2,1,0:T(8,128)(2,1)} async-done(((bf16[32,64,256]{2,1,0:T(8,128)(2,1)}), bf16[32,64,256]{2,1,0:T(8,128)(2,1)}, u32[]{:S(2)}, u32[]{:S(2)}) %all-to-all-start.1) | async-done | bytes 1048608 | tf_op jit(solution)/shard_map/all_to_all | solution.py:56
  125.6 8.7 %all-to-all-start = ((bf16[32,64,256]{2,1,0:T(8,128)(2,1)}), bf16[32,64,256]{2,1,0:T(8,128)(2,1)}, u32[]{:S(2)}, u32[]{:S(2)}) async-start(bf16[32,64,256]{2,1,0:T(8,128)(2,1)} %all-gather.10.cloned.1.call-done), calls=%async_computation | async-start | bytes 2097152 | tf_op jit(solution)/shard_map/all_to_all | solution.py:57
  134.4 3.9 %bitcast_multiply_fusion = (bf16[2,1,2048,256]{3,2,0,1:T(8,128)(2,1)}, bf16[2,1,2048,256]{3,2,0,1:T(8,128)(2,1)}) fusion(bf16[2,1,2048,256]{3,2,1,0:T(8,128)(2,1)S(1)} %copy-done.2, bf16[2,256]{1,0:T(2,128)(2,1)S(1)} %compare_convert_fusion.1, bf16[2,1,2048,256]{3,2,1,0:T(8,128)(2,1)} %param.12), kind=kLoop, calls=%fused_computation.21 | loop fusion | flops 2097152 | bytes 8389632 | tf_op jit(solution)/shard_map/mul | solution.py:65
  138.3 14.0 %all-to-all-done = bf16[32,64,256]{2,1,0:T(8,128)(2,1)} async-done(((bf16[32,64,256]{2,1,0:T(8,128)(2,1)}), bf16[32,64,256]{2,1,0:T(8,128)(2,1)}, u32[]{:S(2)}, u32[]{:S(2)}) %all-to-all-start) | async-done | bytes 1048608 | tf_op jit(solution)/shard_map/all_to_all | solution.py:57
  152.3 23.9 %all-gather.12.cloned.1.call-done = bf16[2,2048,256]{2,1,0:T(8,128)(2,1)} async-done(((bf16[2,64,256]{2,1,0:T(8,128)(2,1)}), bf16[2,2048,256]{2,1,0:T(8,128)(2,1)}) %all-gather.12.cloned.1.call-update) | async-done | bytes 2097168 | tf_op jit(solution)/shard_map/all_gather | solution.py:49
  176.2 5.2 %fusion.3 = bf16[2,1,2048,256]{3,2,0,1:T(8,128)(2,1)} fusion(bf16[2048,256,1]{1,0,2:T(8,128)(2,1)} %bitcast.13, bf16[2048,256,1]{1,0,2:T(8,128)(2,1)} %bitcast.8, bf16[2,2048,256]{2,1,0:T(8,128)(2,1)} %all-gather.12.cloned.1.call-done), kind=kOutput, calls=%fused_computation.11 | convolution fusion | flops 1078067200 | bytes 6291456 | tf_op jit(solution)/shard_map/cbl,crkl->rcbk/dot_general | solution.py:66
  181.3 40.3 %all-gather.6.cloned.1.call-done = bf16[2,2048,256]{2,1,0:T(8,128)(2,1)} async-done(((bf16[2,64,256]{2,1,0:T(8,128)(2,1)}), bf16[2,2048,256]{2,1,0:T(8,128)(2,1)}) %all-gather.6.cloned.1.call-update) | async-done | bytes 2097168 | tf_op jit(solution)/shard_map/all_gather | solution.py:48
  221.6 7.5 %fusion.7 = f32[2,2048,256]{2,1,0:T(8,128)} fusion(bf16[2,1,2048,256]{3,2,0,1:T(8,128)(2,1)} %bitcast.129, bf16[2,1,2048,256]{3,2,0,1:T(8,128)(2,1)} %get-tuple-element.34, bf16[2,1,2048,256]{3,2,0,1:T(8,128)(2,1)} %fusion.3, bf16[2,1,2048,256]{3,2,0,1:T(8,128)(2,1)S(1)} %copy-done.3, bf16[2,256]{1,0:T(2,128)(2,1)S(1)} %fusion.36, bf16[2048,256]{1,0:T(8,128)(2,1)} %param.23), kind=kOutput, calls=%fused_computation.16 | convolution fusion | flops 2165571584 | bytes 13632512 | tf_op jit(solution)/shard_map/rcbm,rcmk->rcbk/dot_general | solution.py:76
  229.1 10.5 %convolution_add_fusion = f32[2,256,256]{1,2,0:T(8,128)S(1)} fusion(f32[2,2048,256]{2,1,0:T(8,128)} %fusion.7, f32[256,256]{0,1:T(8,128)S(1)} %fusion.31, f32[2,256]{1,0:T(2,128)S(1)} %convert_subtract_fusion), kind=kOutput, calls=%fused_computation.27 | convolution fusion | flops 3221487616 | bytes 4982784 | tf_op jit(solution)/shard_map/rcbk,rcbl->rckl/dot_general | solution.py:77
  239.8 23.5 %custom-call.16 = f32[2,1,128,128]{3,2,1,0:T(8,128)S(1)} custom-call(f32[2,1,128,128]{3,2,1,0:T(8,128)S(1)} %cholesky.125), custom_call_target="Cholesky" | custom-call | tf_op jit(solution)/shard_map/jit(cholesky)/cholesky | solution.py:79
  263.3 19.9 %custom-call.17 = f32[2,1,1,128,128]{3,4,2,1,0:T(8,128)S(1)} custom-call(f32[2,1,1,128,128]{4,3,2,1,0:T(8,128)S(1)} %select_bitcast_fusion), custom_call_target="InvertDiagBlocksLowerTriangular" | custom-call | tf_op jit(solution)/shard_map/jit(cholesky)/cholesky | solution.py:79
  283.9 23.5 %custom-call.18 = f32[2,1,128,128]{3,2,1,0:T(8,128)S(1)} custom-call(f32[2,1,128,128]{3,2,1,0:T(8,128)S(1)} %fusion.22), custom_call_target="Cholesky" | custom-call | tf_op jit(solution)/shard_map/jit(cholesky)/cholesky | solution.py:79
  307.8 4.0 %while.1 = (s32[]{:T(128)}, f32[2,1,256,256]{3,2,1,0:T(8,128)S(1)}, s32[2,2]{1,0:T(2,128)S(1)}, f32[2,2,1,128,128]{4,3,0,2,1:T(8,128)S(1)}, s32[]{:T(128)}) while((s32[]{:T(128)}, f32[2,1,256,256]{3,2,1,0:T(8,128)S(1)}, s32[2,2]{1,0:T(2,128)S(1)}, f32[2,2,1,128,128]{4,3,0,2,1:T(8,128)S(1)}, s32[]{:T(128)}) %tuple.34), condition=%wide.while_cond, body=%wide.while_body.sunk | while | flops 2 | bytes 262261 | solution.py:80
  308.4 1.4 bitcast_dynamic-update-slice_fusion.3
  310.4 1.4 bitcast_dynamic-update-slice_fusion.3
  312.5 40.4 %custom-call.19 = f32[2,1,2,128,128]{3,4,2,1,0:T(8,128)S(1)} custom-call(f32[2,1,2,128,128]{4,3,2,1,0:T(8,128)} %bitcast.131), custom_call_target="InvertDiagBlocksLowerTriangular" | custom-call | tf_op jit(solution)/shard_map/triangular_solve | solution.py:80
  352.9 3.7 fusion.11
  356.7 3.5 fusion.9
  360.1 3.4 fusion.32
  363.5 7.8 %fusion.4 = bf16[2,1,2048,256]{3,2,1,0:T(8,128)(2,1)} fusion(bf16[2,1,2048,256]{3,2,0,1:T(8,128)(2,1)} %fusion.3, bf16[2,1,2048,256]{3,2,0,1:T(8,128)(2,1)} %get-tuple-element.33, f32[2,2048,128]{1,2,0:T(8,128)} %fusion.32, f32[2,2048,128]{1,2,0:T(8,128)S(1)} %fusion.11, bf16[2,1,2048,256]{3,2,0,1:T(8,128)(2,1)} %bitcast.130, ...), kind=kOutput, calls=%fused_computation.12 | convolution fusion | flops 2169765888 | bytes 14680064 | tf_op jit(solution)/shard_map/rcbm,rcmk->rcbk/dot_general | solution.py:88
  371.3 3.4 fusion
  374.7 3.9 %copy.82 = bf16[2,1,2048,256]{3,2,1,0:T(8,128)(2,1)} copy(bf16[2,1,2048,256]{2,3,0,1:T(8,128)(2,1)} %fusion) | data formatting | bytes 4194304
  (53 shorter events, 6.5 us)
Async XLA Ops:
  7.2 67.5 %copy-start = (f32[64,2048]{1,0:T(8,128)S(1)}, f32[64,2048]{1,0:T(8,128)}, u32[]{:S(2)}) copy-start(f32[64,2048]{1,0:T(8,128)} %param.22) | copy-start | bytes 1572868
  7.2 67.5 %all-gather.8.cloned.1.call-start = ((), (), s32[]{:S(2)}) async-start(), calls=%async_computation.3 | async-start | bytes 10813440 | tf_op jit(solution)/shard_map/all_gather | solution.py:42
  13.0 86.1 %all-gather.14.cloned.1.call-start = ((), (), s32[]{:S(2)}) async-start(), calls=%async_computation.6 | async-start | bytes 1310720 | tf_op jit(solution)/shard_map/all_gather | solution.py:52
  13.7 111.9 %all-gather.10.cloned.1.call-start = ((), (), s32[]{:S(2)}) async-start(), calls=%async_computation.4 | async-start | bytes 1310720 | tf_op jit(solution)/shard_map/all_gather | solution.py:53
  82.8 25.0 %copy-start.6 = (s32[2,1]{0,1:T(1,128)S(1)}, s32[2,1]{0,1:T(1,128)}, u32[]{:S(2)}) copy-start(s32[2,1]{0,1:T(1,128)} %param.14) | copy-start | bytes 28
  82.8 25.1 %copy-start.4 = (s32[2,1]{0,1:T(1,128)S(1)}, s32[2,1]{0,1:T(1,128)}, u32[]{:S(2)}) copy-start(s32[2,1]{0,1:T(1,128)} %param.15) | copy-start | bytes 28
  83.6 92.6 %all-gather.12.cloned.1.call-start = ((), (), s32[]{:S(2)}) async-start(), calls=%async_computation.5 | async-start | bytes 2162688 | tf_op jit(solution)/shard_map/all_gather | solution.py:49
  84.3 137.3 %all-gather.6.cloned.1.call-start = ((), (), s32[]{:S(2)}) async-start(), calls=%async_computation.2 | async-start | bytes 2162688 | tf_op jit(solution)/shard_map/all_gather | solution.py:48
  84.9 49.5 %copy-start.2 = (bf16[2,1,2048,256]{3,2,1,0:T(8,128)(2,1)S(1)}, bf16[2,1,2048,256]{3,2,1,0:T(8,128)(2,1)}, u32[]{:S(2)}) copy-start(bf16[2,1,2048,256]{3,2,1,0:T(8,128)(2,1)} %param.13) | copy-start | bytes 6291460
  99.0 25.9 %all-to-all-start.1 = ((bf16[32,64,256]{2,1,0:T(8,128)(2,1)}), bf16[32,64,256]{2,1,0:T(8,128)(2,1)}, u32[]{:S(2)}, u32[]{:S(2)}) async-start(bf16[32,64,256]{2,1,0:T(8,128)(2,1)} %all-gather.14.cloned.1.call-done), calls=%async_computation.1 | async-start | bytes 2097152 | tf_op jit(solution)/shard_map/all_to_all | solution.py:56
  125.6 26.7 %all-to-all-start = ((bf16[32,64,256]{2,1,0:T(8,128)(2,1)}), bf16[32,64,256]{2,1,0:T(8,128)(2,1)}, u32[]{:S(2)}, u32[]{:S(2)}) async-start(bf16[32,64,256]{2,1,0:T(8,128)(2,1)} %all-gather.10.cloned.1.call-done), calls=%async_computation | async-start | bytes 2097152 | tf_op jit(solution)/shard_map/all_to_all | solution.py:57
  176.2 45.4 %copy-start.3 = (bf16[2,1,2048,256]{3,2,0,1:T(8,128)(2,1)S(1)}, bf16[2,1,2048,256]{3,2,0,1:T(8,128)(2,1)}, u32[]{:S(2)}) copy-start(bf16[2,1,2048,256]{3,2,0,1:T(8,128)(2,1)} %get-tuple-element.33) | copy-start | bytes 6291460
  311.8 0.7 copy-start.5
  352.9 3.8 copy-start.1
Sparse Core Ops, SparseCore 0:
  13.1 61.5 all-gather.7
  76.9 22.0 all-gather.13
  101.3 24.2 all-gather.9
  127.7 48.3 all-gather.11
  178.3 43.2 all-gather.5
where the time goes:
time: 386 us; the launch traced here: 385 us
  waiting for transfers between devices  172 us (45%)
  other arithmetic  119 us (31%)
  matrix products  50.3 us (13%)
  starting transfers between devices  17.5 us (5%)
  between operations  14 us (4%)
  local copies, waits for them, and re-layouts  11.8 us (3%)
    another operation x9, other arithmetic, on_device(): lower = jnp.linalg.cholesky(gram)  67.1 us
    all_gather x1, waiting for transfers between devices, on_device(): lax.all_gather(stacked, 'pcol', axis=1, tiled=True).astype(jnp.float32)  60.9 us
    another operation x4, other arithmetic, on_device(): lax.linalg.triangular_solve(lower, range_y, left_side=False, lower=True,...  40.6 us
    all_gather x1, waiting for transfers between devices, on_device(): lax.all_gather(rows_u, 'pcol', axis=1, tiled=True)  40.3 us
    all_gather x1, waiting for transfers between devices, on_device(): lax.all_gather(row_w, 'pcol', axis=1, tiled=True)  23.9 us
    all_to_all x1, waiting for transfers between devices, on_device(): lax.all_to_all(col_u_all, 'pcol', split_axis=0, concat_axis=1, tiled=True)  17 us
    all_gather x1, waiting for transfers between devices, on_device(): lax.all_gather(cols_u, 'prow', axis=0, tiled=True)  14.2 us
    all_to_all x1, waiting for transfers between devices, on_device(): lax.all_to_all(col_w_all, 'pcol', split_axis=0, concat_axis=1, tiled=True)  14 us
  transfers between devices with their start and end apart: 7, of which 7 were waited for; matrix products, arithmetic and copies ran while one was open for 5% of the time, Pallas kernels for 0%

commit v1 on v0

v1 whole, which is shorter than its diff:
```python
import functools
import math

import jax
import jax.numpy as jnp
from jax import lax
from jax.experimental import pallas as pl
from jax.experimental.pallas import tpu as pltpu
from jax.sharding import Mesh, PartitionSpec as P

F32 = jnp.float32
BF16 = jnp.bfloat16
HALF = 128


def dot(a, b, ca=1, cb=0, precision=None):
    return lax.dot_general(
        a, b, (((ca,), (cb,)), ((), ())), preferred_element_type=F32, precision=precision
    )


def exact(a, b, ca=1, cb=0):
    return dot(a, b, ca, cb, lax.Precision.HIGHEST)


def pieces(x, count):
    out = []
    for _ in range(count):
        piece = x.astype(BF16)
        out.append(piece)
        x = x - piece.astype(F32)
    return out


def eliminate(blocks):
    n = HALF
    lane = lax.broadcasted_iota(jnp.int32, (8, n), 1)
    sub = lax.broadcasted_iota(jnp.int32, (8, n), 0)
    tiles = [[m[8 * i : 8 * i + 8] for i in range(n // 8)] for m in blocks]
    for k in range(0, n, 2):
        g, at = divmod(k, 8)
        first, second = lane == k, lane == k + 1
        pair = first | second
        for x in tiles:
            c0 = [jnp.broadcast_to(x[i][:, k : k + 1], (8, n)) for i in range(g, n // 8)]
            c1 = [jnp.broadcast_to(x[i][:, k + 1 : k + 2], (8, n)) for i in range(g, n // 8)]
            r0 = jnp.broadcast_to(x[g][at : at + 1], (8, n))
            r1 = jnp.broadcast_to(x[g][at + 1 : at + 2], (8, n))
            a = jnp.broadcast_to(c0[0][at : at + 1], (8, n))
            b = jnp.broadcast_to(c1[0][at : at + 1], (8, n))
            c = jnp.broadcast_to(c1[0][at + 1 : at + 2], (8, n))
            inv = 1.0 / (a * c - b * b)
            ai, bi, ci = a * inv, b * inv, c * inv
            r0 = jnp.where(first, 1.0, jnp.where(second, 0.0, r0))
            r1 = jnp.where(second, 1.0, jnp.where(first, 0.0, r1))
            q0 = ci * r0 - bi * r1
            q1 = ai * r1 - bi * r0
            for m, i in enumerate(range(g, n // 8)):
                if i == g and at == 6:
                    continue
                new = (jnp.where(pair, 0.0, x[i]) - c0[m] * q0) - c1[m] * q1
                x[i] = jnp.where(sub > at + 1, new, x[i]) if i == g else new
    odd = (sub % 2) == 1
    out = []
    for x in tiles:
        done = []
        for i in range(n // 8):
            row = sub + 8 * i
            pivot_start = row - row % 2
            here = jnp.sum(jnp.where(lane == row, x[i], 0.0), axis=1, keepdims=True)
            above = jnp.sum(jnp.where((lane == row + 1) & ~odd, x[i], 0.0), axis=1, keepdims=True)
            here = jnp.broadcast_to(here, (8, n))
            above = jnp.broadcast_to(above, (8, n))
            unit = jnp.where(lane < pivot_start, x[i], jnp.where(lane == row, 1.0, 0.0))
            ratio = jnp.where(odd, pltpu.roll(above / here, 1, axis=0), 0.0)
            above = jnp.where(odd, pltpu.roll(above, 1, axis=0), 0.0)
            scale = lax.rsqrt(here - ratio * above)
            done.append((unit - ratio * pltpu.roll(unit, 1, axis=0)) * scale)
        out.append(jnp.concatenate(done, axis=0))
    return out


def inverse_factors(grams):
    h = HALF
    m1 = eliminate([g[:h, :h] for g in grams])
    u12 = [exact(m, g[:h, h:]) for m, g in zip(m1, grams)]
    m2 = eliminate([g[h:, h:] - exact(u, u, 0, 0) for u, g in zip(u12, grams)])
    m21 = [-exact(b, exact(u, a, 0, 0)) for a, b, u in zip(m1, m2, u12)]
    zero = jnp.zeros((h, h), F32)
    return [
        jnp.concatenate(
            [jnp.concatenate([a, zero], axis=1), jnp.concatenate([c, b], axis=1)], axis=0
        )
        for a, b, c in zip(m1, m2, m21)
    ]


def tail_kernel(
    ranks,
    guu,
    pt,
    sk,
    gathered,
    vp0,
    vp1,
    vp2,
    vp3,
    up0,
    up1,
    up2,
    up3,
    trail_u,
    trail_v,
    fresh_u,
    fresh_v,
    dinv,
    vall,
    ui,
    uj,
    tu,
    tv,
    zs,
    bs,
    ou,
    ov,
    load_sem,
    out_sem,
):
    width, rmax = 2048, 256
    part = width // 4
    here = ranks[7]

    loads = []

    def load(src, dst):
        copy = pltpu.make_async_copy(src, dst, load_sem.at[len(loads)])
        copy.start()
        loads.append(copy)
        return copy

    need_v = [load(gathered.at[8 + t], vall.at[:, pl.ds(rmax * t, rmax)]) for t in range(2)]
    for k, src in enumerate((vp0, vp1, vp2, vp3)):
        at = pl.multiple_of(lax.rem(here + 4 - k, 4) * part, part)
        need_v.append(load(src, vall.at[pl.ds(at, part), pl.ds(2 * rmax, rmax)]))
    need_d = []
    for q in range(4):
        chunks, rows = pl.ds(0, 2 * q + 2), pl.ds(part * q, part)
        need_d.append(load(gathered.at[chunks, rows], dinv.at[chunks, rows]))
    need_u = [load(gathered.at[10 + t], ui.at[t]) for t in range(2)]
    need_u.append(load(trail_u, tu))
    need_uj = []
    for k, src in enumerate((up0, up1, up2, up3)):
        at = pl.multiple_of(lax.rem(here + 4 - k, 4) * part, part)
        need_uj.append(load(src, uj.at[pl.ds(at, part)]))
    need_tv = load(trail_v, tv)

    for copy in need_v:
        copy.wait()
    coupling = [jnp.zeros((rmax, rmax), F32)] * 2
    for q in range(4):
        need_d[q].wait()
        depth = part * (q + 1)
        for n in range(2):
            at = part * q + rmax * n
            lhs = jnp.concatenate([dinv[c, at : at + rmax] for c in range(2 * q + 2)], axis=1)
            w = dot(lhs, vall[:depth]).astype(BF16)
            wj = w[:, 2 * rmax :]
            coupling = [
                coupling[t] + dot(w[:, rmax * t : rmax * (t + 1)], wj, 0, 0) for t in range(2)
            ]
    for copy in need_u:
        copy.wait()
    gur = [dot(tu[t], ui[t], 0, 0) for t in range(2)]
    grr = [dot(ui[t], ui[t], 0, 0) for t in range(2)]
    for copy in need_uj:
        copy.wait()
    reach = dot(uj[...], sk[...], 0, 0).astype(BF16)

    row = lax.broadcasted_iota(jnp.int32, (rmax, rmax), 0)
    col = lax.broadcasted_iota(jnp.int32, (rmax, rmax), 1)
    couplings, grams, probes, whole, heads = [], [], [], [], []
    for t in range(2):
        tile_rank, new_rank, row_rank, col_rank = ranks[t], ranks[2 + t], ranks[4 + t], ranks[6]
        keep = col < new_rank
        c = jnp.where((row < row_rank) & (col < col_rank), coupling[t], 0.0).astype(BF16)
        top = jnp.where((row < tile_rank) & keep, pt[t], 0.0)
        bottom = jnp.where(keep, -dot(c, reach), 0.0)
        probe = jnp.concatenate([top, bottom], axis=0).astype(BF16)
        g = jnp.concatenate(
            [
                jnp.concatenate([guu[t], gur[t]], axis=1),
                jnp.concatenate([gur[t].T, grr[t]], axis=1),
            ],
            axis=0,
        )
        parts = pieces(g, 3)
        gp = dot(parts[0], probe) + (dot(parts[1], probe) + dot(parts[2], probe))
        gp = pieces(gp, 3)
        gram = dot(probe, gp[0], 0, 0) + (dot(probe, gp[1], 0, 0) + dot(probe, gp[2], 0, 0))
        grams.append(gram + jnp.where((row == col) & ~keep, 1.0, 0.0))
        couplings.append(c)
        probes.append(probe)
        whole.append(parts)
    inverses = inverse_factors(grams)
    need_tv.wait()
    for t in range(2):
        mp = pieces(inverses[t] * math.sqrt(width), 3)
        z = dot(probes[t], mp[0], 1, 1) + (dot(probes[t], mp[1], 1, 1) + dot(probes[t], mp[2], 1, 1))
        z = z.astype(BF16)
        back = dot(whole[t][0], z) + dot(whole[t][1], z)
        top = jnp.where(row < ranks[t], back[:rmax], 0.0)
        bottom = -dot(couplings[t], back[rmax:].astype(BF16), 0, 0)
        zs[t] = z
        bs[t] = (jnp.concatenate([top, bottom], axis=0) / width).astype(BF16)

    copies = []
    for t in range(2):
        for n in range(4):
            rows = pl.ds(part * n, part)
            left = jnp.concatenate([tu[t, rows], ui[t, rows]], axis=1)
            ou[t, rows] = dot(left, zs[t]).astype(BF16)
            right = jnp.concatenate([tv[t, rows], uj[rows]], axis=1)
            ov[t, rows] = dot(right, bs[t]).astype(BF16)
            for src, dst in ((ou, fresh_u), (ov, fresh_v)):
                copy = pltpu.make_async_copy(
                    src.at[t, rows], dst.at[t, rows], out_sem.at[len(copies)]
                )
                copy.start()
                copies.append(copy)
    for copy in copies:
        copy.wait()


def tail(ranks, guu, pt, sketch, gathered, vparts, uparts, trail_u, trail_v):
    width, rmax = sketch.shape
    vmem = pl.BlockSpec(memory_space=pltpu.VMEM)
    hbm = pl.BlockSpec(memory_space=pl.ANY)
    tile = jax.ShapeDtypeStruct(trail_u.shape, BF16)
    return pl.pallas_call(
        tail_kernel,
        name="tail",
        out_shape=(tile, tile),
        in_specs=[pl.BlockSpec(memory_space=pltpu.SMEM)] + [vmem] * 3 + [hbm] * 11,
        out_specs=(hbm, hbm),
        scratch_shapes=[
            pltpu.VMEM((8, width, rmax), BF16),
            pltpu.VMEM((width, 3 * rmax), BF16),
            pltpu.VMEM((2, width, rmax), BF16),
            pltpu.VMEM((width, rmax), BF16),
            pltpu.VMEM((2, width, rmax), BF16),
            pltpu.VMEM((2, width, rmax), BF16),
            pltpu.VMEM((2, 2 * rmax, rmax), BF16),
            pltpu.VMEM((2, 2 * rmax, rmax), BF16),
            pltpu.VMEM((2, width, rmax), BF16),
            pltpu.VMEM((2, width, rmax), BF16),
            pltpu.SemaphoreType.DMA((20,)),
            pltpu.SemaphoreType.DMA((16,)),
        ],
        compiler_params=pltpu.CompilerParams(vmem_limit_bytes=56 * 1024 * 1024),
        cost_estimate=pl.CostEstimate(
            flops=16_000_000_000, bytes_accessed=20_000_000, transcendentals=0
        ),
    )(ranks, guu, pt, sketch, gathered, *vparts, *uparts, trail_u, trail_v)


def on_device(
    trail_u,
    trail_v,
    tile_rank,
    new_rank,
    row_u,
    row_v,
    row_rank,
    col_u,
    col_v,
    col_rank,
    diag_inv,
    sketch,
):
    trow, _, width, rmax = trail_u.shape
    x, z = lax.axis_index("x"), lax.axis_index("z")
    yc = lax.axis_index(("y", "c"))
    pcol = z * 8 + yc
    trail_u, trail_v = trail_u[:, 0], trail_v[:, 0]

    slab = diag_inv.shape[0]
    factor = jnp.swapaxes(diag_inv.astype(BF16).reshape(slab, width // rmax, rmax), 0, 1)
    mine = jnp.concatenate([factor, row_v, row_u], axis=0)
    gathered = lax.all_gather(mine, ("z", "y", "c"), axis=1, tiled=True)

    both = jnp.stack([col_v, col_u], axis=1)
    quarter = lax.all_to_all(both, ("y", "c"), split_axis=0, concat_axis=2, tiled=True)[0]
    swap = [(a * 4 + b, b * 4 + a) for a in range(4) for b in range(4)]
    quarter = lax.ppermute(quarter, ("x", "z"), swap)

    def spread(block):
        return [block] + [
            lax.ppermute(block, "x", [(a, (a + k) % 4) for a in range(4)]) for k in (1, 3, 2)
        ]

    vparts = spread(quarter[0])
    uparts = spread(quarter[1])
    vparts = [vparts[0], vparts[1], vparts[3], vparts[2]]
    uparts = [uparts[0], uparts[1], uparts[3], uparts[2]]

    guu = jnp.einsum("tbm,tbn->tmn", trail_u, trail_u, preferred_element_type=F32)
    pt = jnp.einsum("tbm,bn->tmn", trail_v, sketch, preferred_element_type=F32)
    own_row = lax.dynamic_slice_in_dim(row_rank, x * trow, trow)
    own_col = lax.dynamic_slice_in_dim(col_rank, pcol, 1)
    ranks = jnp.concatenate([tile_rank[:, 0], new_rank[:, 0], own_row, own_col, x[None]])
    fresh_u, fresh_v = tail(ranks, guu, pt, sketch, gathered, vparts, uparts, trail_u, trail_v)
    return fresh_u[:, None], fresh_v[:, None]


def solution(mesh):
    split = Mesh(mesh.devices.reshape(4, 4, 4, 2), ("x", "z", "y", "c"))
    cols = ("z", "y", "c")
    tiles = P("x", cols, None, None)
    panel = P("x", cols, None)
    return jax.shard_map(
        on_device,
        mesh=split,
        in_specs=(
            tiles,
            tiles,
            P("x", cols),
            P("x", cols),
            panel,
            panel,
            P(),
            panel,
            panel,
            P(),
            P(cols, None),
            P(),
        ),
        out_specs=(tiles, tiles),
        check_vma=False,
    )
```

time: 386 us -> 148 us (0.38)
  waiting for transfers between devices: 172 us -> 30.2 us
  other arithmetic: 119 us -> 3.94 us
  matrix products: 50.3 us -> 3.38 us
  Pallas kernels: 0 us -> 41.7 us
  starting transfers between devices: 17.5 us -> 34.2 us
  blocking collectives: 0 us -> 15.1 us
  local copies, waits for them, and re-layouts: 11.8 us -> 4.66 us
    all_gather x5 -> x1, waiting for transfers between devices: 140 us -> 13.8 us  [on_device(): gathered = lax.all_gather(mine, ('z', 'y', 'c'), axis=1, tiled=True)]
    another operation x13 -> x1, other arithmetic: 108 us -> 1.16 us  [on_device(): both = jnp.stack([col_v, col_u], axis=1)]
    pallas_call x0 -> x1, Pallas kernels: none -> 41.7 us  [tail(): pl.pallas_call(tail_kernel, name='tail', out_shape=(tile, tile), in_specs...]
    dot_general x5 -> x2, matrix products: 39.1 us -> 3.38 us  [the longest x1 1.83 us: on_device(): jnp.einsum('tbm,tbn->tmn', trail_u, trail_u, preferred_element_type=F32)]
    ppermute x0 -> x7, starting transfers between devices: none -> 34.1 us  [the longest x6 28.8 us: spread(): lax.ppermute(block, 'x', [(a, (a + k) % 4) for a in range(4)])]
    all_to_all x2 -> x0, waiting for transfers between devices: 31 us -> none  [the longest x1 17 us: on_device(): lax.all_to_all(col_u_all, 'pcol', split_axis=0, concat_axis=1, tiled=True)]
    all_to_all x2 -> x0, starting transfers between devices: 17.3 us -> none  [the longest x1 8.68 us: on_device(): lax.all_to_all(col_w_all, 'pcol', split_axis=0, concat_axis=1, tiled=True)]
    ppermute x0 -> x7, waiting for transfers between devices: none -> 16.4 us  [the longest x6 16.4 us: spread(): lax.ppermute(block, 'x', [(a, (a + k) % 4) for a in range(4)])]
  transfers between devices with their start and end apart: 7 -> 8, of which waited for: 7 -> 5; matrix products, arithmetic and copies ran while one was open for 5% -> 6% of each run, Pallas kernels for 0% -> 0%
where the time goes in v1:
time: 148 us; the launch traced here: 147 us
  Pallas kernels  41.7 us (28%)
  starting transfers between devices  34.2 us (23%)
  waiting for transfers between devices  30.2 us (20%)
  blocking collectives  15.1 us (10%)
  between operations  14.2 us (10%)
  local copies, waits for them, and re-layouts  4.66 us (3%)
  other arithmetic  3.94 us (3%)
  matrix products  3.38 us (2%)
    pallas_call x1, Pallas kernels, tail(): pl.pallas_call(tail_kernel, name='tail', out_shape=(tile, tile), in_specs...  41.7 us
    ppermute x6, starting transfers between devices, spread(): lax.ppermute(block, 'x', [(a, (a + k) % 4) for a in range(4)])  28.8 us
    ppermute x6, waiting for transfers between devices, spread(): lax.ppermute(block, 'x', [(a, (a + k) % 4) for a in range(4)])  16.4 us
    all_to_all x1, blocking collectives, on_device(): lax.all_to_all(both, ('y', 'c'), split_axis=0, concat_axis=2, tiled=True)[0]  15.1 us
    all_gather x1, waiting for transfers between devices, on_device(): gathered = lax.all_gather(mine, ('z', 'y', 'c'), axis=1, tiled=True)  13.8 us
    ppermute x1, starting transfers between devices, on_device(): quarter = lax.ppermute(quarter, ('x', 'z'), swap)  5.38 us
  transfers between devices with their start and end apart: 8, of which 5 were waited for; matrix products, arithmetic and copies ran while one was open for 6% of the time, Pallas kernels for 0%

profile of v1, /device:TPU:1, one launch (start us, length us, event | category | flops | bytes accessed | tf_op | source)
XLA Modules:
  0.0 147.4 jit_solution(5016159362578215722)
XLA Ops:
  7.2 0.0 all-gather.2.cloned.1.call-start
  7.2 1.1 convert_element_type.3
  8.4 0.0 copy-start.14
  8.4 0.0 copy-start.15
  8.4 0.0 copy-start.5
  8.4 0.0 copy-start.6
  8.4 1.7 %pad_maximum_fusion.1 = bf16[12,64,256]{2,1,0:T(8,128)(2,1)} fusion(bf16[2,64,256]{2,1,0:T(8,128)(2,1)} %param.16, bf16[2,64,256]{2,1,0:T(8,128)(2,1)} %param.17, bf16[8,64,256]{2,1,0:T(8,128)(2,1)S(1)} %bitcast.37), kind=kLoop, calls=%fused_computation.3 | loop fusion | flops 393216 | bytes 786432 | tf_op jit(solution)/shard_map/concatenate | solution.py:288
  10.1 0.0 all-gather.2.cloned.1.call-update
  10.1 0.0 copy-start
  10.1 0.0 copy-start.1
  10.1 1.2 pad_maximum_fusion
  11.3 15.1 %all_to_all.15 = bf16[8,2,64,256]{3,2,1,0:T(8,128)(2,1)S(1)} all-to-all(bf16[8,2,64,256]{3,2,1,0:T(8,128)(2,1)S(1)} %pad_maximum_fusion), channel_id=1, replica_groups=mesh['x'=4,'z'=4,'y'=4,'c'=2] {'y','c'}, dimensions={0} | all-to-all | bytes 1048576 | tf_op jit(solution)/shard_map/all_to_all | solution.py:292
  26.4 0.8 copy.26
  27.3 5.4 %collective-permute-start = (bf16[2,512,256]{2,1,0:T(8,128)(2,1)}, bf16[2,512,256]{2,1,0:T(8,128)(2,1)}, u32[]{:S(2)}, u32[]{:S(2)}) collective-permute-start(bf16[2,512,256]{2,1,0:T(8,128)(2,1)} %bitcast.11), channel_id=1, source_target_pairs={{0,0},{8,32},{16,64},{24,96},{32,8},{40,40},{48,72},{56,104},{64,1... | collective-permute-start | bytes 1572872 | tf_op jit(solution)/shard_map/ppermute | solution.py:294
  32.6 0.6 dynamic_slice.7
  33.2 0.1 dynamic_slice.6
  33.3 1.3 concatenate.6.ranks
  34.6 1.1 slice_bitcast_fusion
  35.7 0.0 copy-start.7
  35.7 24.3 %collective-permute-start.6 = (bf16[512,256]{1,0:T(8,128)(2,1)S(1)}, bf16[512,256]{1,0:T(8,128)(2,1)S(1)}, u32[]{:S(2)}, u32[]{:S(2)}) collective-permute-start(bf16[512,256]{1,0:T(8,128)(2,1)S(1)} %get-tuple-element.12.up0), channel_id=1, source_target_pairs={{0,96},{32,0},{64,32},{96,64},{1,97},{33,1},{65,33},{97,65},{2,98}... | collective-permute-start | bytes 786440 | tf_op jit(solution)/shard_map/ppermute | solution.py:298
  60.0 1.5 %fusion.pt = f32[2,256,256]{2,1,0:T(8,128)} fusion(bf16[2048,256]{1,0:T(8,128)(2,1)S(1)} %copy-done.1, bf16[2,1,2048,256]{3,2,1,0:T(8,128)(2,1)S(1)} %copy-done), kind=kOutput, calls=%fused_computation | convolution fusion | flops 536870912 | bytes 3670016 | tf_op jit(solution)/shard_map/tbm,bn->tmn/dot_general | solution.py:307
  61.6 0.6 collective-permute-start.4
  62.2 2.1 %collective-permute-start.3 = (bf16[512,256]{1,0:T(8,128)(2,1)S(1)}, bf16[512,256]{1,0:T(8,128)(2,1)S(1)}, u32[]{:S(2)}, u32[]{:S(2)}) collective-permute-start(bf16[512,256]{1,0:T(8,128)(2,1)S(1)} %get-tuple-element.13.vp0), channel_id=1, source_target_pairs={{0,96},{32,0},{64,32},{96,64},{1,97},{33,1},{65,33},{97,65},{2,98}... | collective-permute-start | bytes 786440 | tf_op jit(solution)/shard_map/ppermute | solution.py:298
  64.3 1.8 %collective-permute-start.2 = (bf16[512,256]{1,0:T(8,128)(2,1)S(1)}, bf16[512,256]{1,0:T(8,128)(2,1)S(1)}, u32[]{:S(2)}, u32[]{:S(2)}) collective-permute-start(bf16[512,256]{1,0:T(8,128)(2,1)S(1)} %get-tuple-element.13.vp0), channel_id=1, source_target_pairs={{0,64},{32,96},{64,0},{96,32},{1,65},{33,97},{65,1},{97,33},{2,66}... | collective-permute-start | bytes 786440 | tf_op jit(solution)/shard_map/ppermute | solution.py:298
  66.0 2.4 %collective-permute-done.6.up3 = bf16[512,256]{1,0:T(8,128)(2,1)S(1)} collective-permute-done((bf16[512,256]{1,0:T(8,128)(2,1)S(1)}, bf16[512,256]{1,0:T(8,128)(2,1)S(1)}, u32[]{:S(2)}, u32[]{:S(2)}) %collective-permute-start.6) | collective-permute-done | bytes 262176 | tf_op jit(solution)/shard_map/ppermute | solution.py:298
  68.4 0.7 copy-done.8
  69.2 1.8 %fusion.3.guu = f32[2,256,256]{2,1,0:T(8,128)} fusion(bf16[2,1,2048,256]{3,2,1,0:T(8,128)(2,1)S(1)} %copy-done.7), kind=kOutput, calls=%fused_computation.8 | convolution fusion | flops 536870912 | bytes 2621440 | tf_op jit(solution)/shard_map/tbm,tbn->tmn/dot_general | solution.py:306
  71.0 7.3 %collective-permute-done.4.up1 = bf16[512,256]{1,0:T(8,128)(2,1)S(1)} collective-permute-done((bf16[512,256]{1,0:T(8,128)(2,1)S(1)}, bf16[512,256]{1,0:T(8,128)(2,1)S(1)}, u32[]{:S(2)}, u32[]{:S(2)}) %collective-permute-start.4) | collective-permute-done | bytes 262176 | tf_op jit(solution)/shard_map/ppermute | solution.py:298
  78.3 2.6 %collective-permute-done.3.vp3 = bf16[512,256]{1,0:T(8,128)(2,1)S(1)} collective-permute-done((bf16[512,256]{1,0:T(8,128)(2,1)S(1)}, bf16[512,256]{1,0:T(8,128)(2,1)S(1)}, u32[]{:S(2)}, u32[]{:S(2)}) %collective-permute-start.3) | collective-permute-done | bytes 262176 | tf_op jit(solution)/shard_map/ppermute | solution.py:298
  81.0 4.1 %collective-permute-done.1.vp1 = bf16[512,256]{1,0:T(8,128)(2,1)S(1)} collective-permute-done((bf16[512,256]{1,0:T(8,128)(2,1)S(1)}, bf16[512,256]{1,0:T(8,128)(2,1)S(1)}, u32[]{:S(2)}, u32[]{:S(2)}) %collective-permute-start.1) | collective-permute-done | bytes 262176 | tf_op jit(solution)/shard_map/ppermute | solution.py:298
  85.0 13.8 %all-gather.2.cloned.1.call-done.gathered = bf16[12,2048,256]{2,1,0:T(8,128)(2,1)} async-done(((bf16[12,64,256]{2,1,0:T(8,128)(2,1)}), bf16[12,2048,256]{2,1,0:T(8,128)(2,1)}) %all-gather.2.cloned.1.call-update) | async-done | bytes 12582928 | tf_op jit(solution)/shard_map/all_gather | solution.py:289
  98.8 41.7 %tail.1 = (bf16[2,2048,256]{2,1,0:T(8,128)(2,1)}, bf16[2,2048,256]{2,1,0:T(8,128)(2,1)}) custom-call(s32[8]{0:T(128)} %concatenate.6.ranks, f32[2,256,256]{2,1,0:T(8,128)} %fusion.3.guu, f32[2,256,256]{2,1,0:T(8,128)} %fusion.pt, bf16[2048,256]{1,0:T(8,128)(2,1)} %sk.1, bf16[12,2048,256]{2,1,0:T(8,128)(2,1)} %all-gather.2.cloned.1.call-done.gathered, ...), custom_call_target="tpu_custom_call" | custom-call | flops 16000000000 | bytes 20000000 | tf_op jit(solution)/shard_map/tail/pallas_call | solution.py:239
  (30 shorter events, 0.1 us)
Async XLA Ops:
  7.2 2.9 %copy-start.2 = (bf16[8,64,256]{2,1,0:T(8,128)(2,1)S(1)}, bf16[8,64,256]{2,1,0:T(8,128)(2,1)}, u32[]{:S(2)}) copy-start(bf16[8,64,256]{2,1,0:T(8,128)(2,1)} %param.19) | copy-start | bytes 786436
  7.2 91.6 %all-gather.2.cloned.1.call-start = ((), (), s32[]{:S(2)}) async-start(), calls=%async_computation.1 | async-start | bytes 12976128 | tf_op jit(solution)/shard_map/all_gather | solution.py:289
  8.4 24.3 %copy-start.14 = (s32[32]{0:T(128)S(1)}, s32[32]{0:T(128)}, u32[]{:S(2)}) copy-start(s32[32]{0:T(128)} %param.21) | copy-start | bytes 388
  8.4 24.9 %copy-start.15 = (s32[8]{0:T(128)S(1)}, s32[8]{0:T(128)}, u32[]{:S(2)}) copy-start(s32[8]{0:T(128)} %param.18) | copy-start | bytes 100
  8.4 24.9 %copy-start.5 = (s32[2,1]{0,1:T(1,128)S(1)}, s32[2,1]{0,1:T(1,128)}, u32[]{:S(2)}) copy-start(s32[2,1]{0,1:T(1,128)} %param.14) | copy-start | bytes 28
  8.4 24.9 %copy-start.6 = (s32[2,1]{0,1:T(1,128)S(1)}, s32[2,1]{0,1:T(1,128)}, u32[]{:S(2)}) copy-start(s32[2,1]{0,1:T(1,128)} %param.15) | copy-start | bytes 28
  10.1 49.9 %copy-start = (bf16[2,1,2048,256]{3,2,1,0:T(8,128)(2,1)S(1)}, bf16[2,1,2048,256]{3,2,1,0:T(8,128)(2,1)}, u32[]{:S(2)}) copy-start(bf16[2,1,2048,256]{3,2,1,0:T(8,128)(2,1)} %param.13) | copy-start | bytes 6291460
  10.1 49.9 %copy-start.1 = (bf16[2048,256]{1,0:T(8,128)(2,1)S(1)}, bf16[2048,256]{1,0:T(8,128)(2,1)}, u32[]{:S(2)}) copy-start(bf16[2048,256]{1,0:T(8,128)(2,1)} %sk.1) | copy-start | bytes 3145732
  27.3 7.4 %collective-permute-start = (bf16[2,512,256]{2,1,0:T(8,128)(2,1)}, bf16[2,512,256]{2,1,0:T(8,128)(2,1)}, u32[]{:S(2)}, u32[]{:S(2)}) collective-permute-start(bf16[2,512,256]{2,1,0:T(8,128)(2,1)} %bitcast.11), channel_id=1, source_target_pairs={{0,0},{8,32},{16,64},{24,96},{32,8},{40,40},{48,72},{56,104},{64,1... | collective-permute-start | bytes 1572872 | tf_op jit(solution)/shard_map/ppermute | solution.py:294
  35.7 35.3 %copy-start.3 = (bf16[512,256]{1,0:T(8,128)(2,1)}, bf16[512,256]{1,0:T(8,128)(2,1)S(1)}, u32[]{:S(2)}) copy-start(bf16[512,256]{1,0:T(8,128)(2,1)S(1)} %get-tuple-element.12.up0) | copy-start | bytes 786436
  35.7 35.3 %copy-start.4 = (bf16[512,256]{1,0:T(8,128)(2,1)}, bf16[512,256]{1,0:T(8,128)(2,1)S(1)}, u32[]{:S(2)}) copy-start(bf16[512,256]{1,0:T(8,128)(2,1)S(1)} %get-tuple-element.13.vp0) | copy-start | bytes 786436
  35.7 33.5 %copy-start.7 = (bf16[2,1,2048,256]{3,2,1,0:T(8,128)(2,1)S(1)}, bf16[2,1,2048,256]{3,2,1,0:T(8,128)(2,1)}, u32[]{:S(2)}) copy-start(bf16[2,1,2048,256]{3,2,1,0:T(8,128)(2,1)} %param.12) | copy-start | bytes 6291460
  35.7 32.7 %collective-permute-start.6 = (bf16[512,256]{1,0:T(8,128)(2,1)S(1)}, bf16[512,256]{1,0:T(8,128)(2,1)S(1)}, u32[]{:S(2)}, u32[]{:S(2)}) collective-permute-start(bf16[512,256]{1,0:T(8,128)(2,1)S(1)} %get-tuple-element.12.up0), channel_id=1, source_target_pairs={{0,96},{32,0},{64,32},{96,64},{1,97},{33,1},{65,33},{97,65},{2,98}... | collective-permute-start | bytes 786440 | tf_op jit(solution)/shard_map/ppermute | solution.py:298
  61.6 9.4 %collective-permute-start.5 = (bf16[512,256]{1,0:T(8,128)(2,1)S(1)}, bf16[512,256]{1,0:T(8,128)(2,1)S(1)}, u32[]{:S(2)}, u32[]{:S(2)}) collective-permute-start(bf16[512,256]{1,0:T(8,128)(2,1)S(1)} %get-tuple-element.12.up0), channel_id=1, source_target_pairs={{0,64},{32,96},{64,0},{96,32},{1,65},{33,97},{65,1},{97,33},{2,66}... | collective-permute-start | bytes 786440 | tf_op jit(solution)/shard_map/ppermute | solution.py:298
  61.6 16.7 %collective-permute-start.4 = (bf16[512,256]{1,0:T(8,128)(2,1)S(1)}, bf16[512,256]{1,0:T(8,128)(2,1)S(1)}, u32[]{:S(2)}, u32[]{:S(2)}) collective-permute-start(bf16[512,256]{1,0:T(8,128)(2,1)S(1)} %get-tuple-element.12.up0), channel_id=1, source_target_pairs={{0,32},{32,64},{64,96},{96,0},{1,33},{33,65},{65,97},{97,1},{2,34}... | collective-permute-start | bytes 786440 | tf_op jit(solution)/shard_map/ppermute | solution.py:298
  62.2 18.8 %collective-permute-start.3 = (bf16[512,256]{1,0:T(8,128)(2,1)S(1)}, bf16[512,256]{1,0:T(8,128)(2,1)S(1)}, u32[]{:S(2)}, u32[]{:S(2)}) collective-permute-start(bf16[512,256]{1,0:T(8,128)(2,1)S(1)} %get-tuple-element.13.vp0), channel_id=1, source_target_pairs={{0,96},{32,0},{64,32},{96,64},{1,97},{33,1},{65,33},{97,65},{2,98}... | collective-permute-start | bytes 786440 | tf_op jit(solution)/shard_map/ppermute | solution.py:298
  64.3 16.7 %collective-permute-start.2 = (bf16[512,256]{1,0:T(8,128)(2,1)S(1)}, bf16[512,256]{1,0:T(8,128)(2,1)S(1)}, u32[]{:S(2)}, u32[]{:S(2)}) collective-permute-start(bf16[512,256]{1,0:T(8,128)(2,1)S(1)} %get-tuple-element.13.vp0), channel_id=1, source_target_pairs={{0,64},{32,96},{64,0},{96,32},{1,65},{33,97},{65,1},{97,33},{2,66}... | collective-permute-start | bytes 786440 | tf_op jit(solution)/shard_map/ppermute | solution.py:298
  68.4 0.7 copy-start.8
  69.1 15.9 %collective-permute-start.1 = (bf16[512,256]{1,0:T(8,128)(2,1)S(1)}, bf16[512,256]{1,0:T(8,128)(2,1)S(1)}, u32[]{:S(2)}, u32[]{:S(2)}) collective-permute-start(bf16[512,256]{1,0:T(8,128)(2,1)S(1)} %get-tuple-element.13.vp0), channel_id=1, source_target_pairs={{0,32},{32,64},{64,96},{96,0},{1,33},{33,65},{65,97},{97,1},{2,34}... | collective-permute-start | bytes 786440 | tf_op jit(solution)/shard_map/ppermute | solution.py:298
  71.0 27.8 %copy-start.9 = (bf16[512,256]{1,0:T(8,128)(2,1)}, bf16[512,256]{1,0:T(8,128)(2,1)S(1)}, u32[]{:S(2)}) copy-start(bf16[512,256]{1,0:T(8,128)(2,1)S(1)} %collective-permute-done.5.up2) | copy-start | bytes 786436
  78.3 20.5 %copy-start.10 = (bf16[512,256]{1,0:T(8,128)(2,1)}, bf16[512,256]{1,0:T(8,128)(2,1)S(1)}, u32[]{:S(2)}) copy-start(bf16[512,256]{1,0:T(8,128)(2,1)S(1)} %collective-permute-done.4.up1) | copy-start | bytes 786436
  81.0 17.8 %copy-start.11 = (bf16[512,256]{1,0:T(8,128)(2,1)}, bf16[512,256]{1,0:T(8,128)(2,1)S(1)}, u32[]{:S(2)}) copy-start(bf16[512,256]{1,0:T(8,128)(2,1)S(1)} %collective-permute-done.3.vp3) | copy-start | bytes 786436
  81.0 17.8 %copy-start.12 = (bf16[512,256]{1,0:T(8,128)(2,1)}, bf16[512,256]{1,0:T(8,128)(2,1)S(1)}, u32[]{:S(2)}) copy-start(bf16[512,256]{1,0:T(8,128)(2,1)S(1)} %collective-permute-done.2.vp2) | copy-start | bytes 786436
  85.0 13.8 %copy-start.13 = (bf16[512,256]{1,0:T(8,128)(2,1)}, bf16[512,256]{1,0:T(8,128)(2,1)S(1)}, u32[]{:S(2)}) copy-start(bf16[512,256]{1,0:T(8,128)(2,1)S(1)} %collective-permute-done.1.vp1) | copy-start | bytes 786436
Sparse Core Ops, SparseCore 0:
  10.9 87.8 all-gather.1

commit v2 on v1

v2 whole, which is shorter than its diff:
```python
import functools
import math

import jax
import jax.numpy as jnp
from jax import lax
from jax.experimental import pallas as pl
from jax.experimental.pallas import tpu as pltpu
from jax.sharding import Mesh, PartitionSpec as P

F32 = jnp.float32
BF16 = jnp.bfloat16
HALF = 128


def dot(a, b, ca=1, cb=0, precision=None):
    return lax.dot_general(
        a, b, (((ca,), (cb,)), ((), ())), preferred_element_type=F32, precision=precision
    )


def exact(a, b, ca=1, cb=0):
    return dot(a, b, ca, cb, lax.Precision.HIGHEST)


def pieces(x, count):
    out = []
    for _ in range(count):
        piece = x.astype(BF16)
        out.append(piece)
        x = x - piece.astype(F32)
    return out


def reciprocal(x):
    r = pl.reciprocal(x, approx=True)
    return r * (2.0 - x * r)

def tree(terms):
    while len(terms) > 1:
        terms = [a + b for a, b in zip(terms[::2], terms[1::2])] + (terms[-1:] if len(terms) % 2 else [])
    return terms[0]

def eliminate(blocks):
    n = HALF
    groups = n // 8
    lane = lax.broadcasted_iota(jnp.int32, (8, n), 1)
    sub = lax.broadcasted_iota(jnp.int32, (8, n), 0)
    spread = lambda v, r: jnp.broadcast_to(v[r : r + 1], (8, n))
    tiles = [[m[8 * i : 8 * i + 8] for i in range(groups)] for m in blocks]
    for g in range(groups):
        panel = (lane >= 8 * g) & (lane < 8 * g + 8)
        for x in tiles:
            cols = [[jnp.broadcast_to(x[i][:, 8 * g + j : 8 * g + j + 1], (8, n)) for i in range(g, groups)] for j in range(8)]
            top = x[g]
            factors = []
            for m in range(0, 8, 2):
                c0, c1 = cols[m], cols[m + 1]
                a, b, c = spread(c0[0], m), spread(c1[0], m), spread(c1[0], m + 1)
                inv = reciprocal(a * c - b * b)
                ai, bi, ci = a * inv, b * inv, c * inv
                for j in range(m + 2, 8):
                    s0, s1 = spread(c0[0], j), spread(c1[0], j)
                    g0, g1 = ci * s0 - bi * s1, ai * s1 - bi * s0
                    cols[j] = [v - (p * g0 + q * g1) for v, p, q in zip(cols[j], c0, c1)]
                k = 8 * g + m
                later = (lane > k + 1) & (lane < 8 * g + 8)
                r0, r1 = spread(top, m), spread(top, m + 1)
                first, second = lane == k, lane == k + 1
                r0 = jnp.where(first, 1.0, jnp.where(second, 0.0, r0))
                r1 = jnp.where(second, 1.0, jnp.where(first, 0.0, r1))
                q0, q1 = ci * r0 - bi * r1, ai * r1 - bi * r0
                if m < 6:
                    new = jnp.where(first | second, 0.0, top) - (c0[0] * q0 + c1[0] * q1)
                    top = jnp.where(sub > m + 1, new, top)
                factors.append((jnp.where(later, 0.0, q0), jnp.where(later, 0.0, q1)))
            x[g] = top
            for t in range(1, groups - g):
                terms = [cols[2 * p][t] * q0 + cols[2 * p + 1][t] * q1 for p, (q0, q1) in enumerate(factors)]
                x[g + t] = jnp.where(panel, 0.0, x[g + t]) - tree(terms)
    odd = (sub % 2) == 1
    out = []
    for x in tiles:
        done = []
        for i in range(groups):
            row = sub + 8 * i
            pivot_start = row - row % 2
            here = jnp.sum(jnp.where(lane == row, x[i], 0.0), axis=1, keepdims=True)
            above = jnp.sum(jnp.where((lane == row + 1) & ~odd, x[i], 0.0), axis=1, keepdims=True)
            here = jnp.broadcast_to(here, (8, n))
            above = jnp.broadcast_to(above, (8, n))
            unit = jnp.where(lane < pivot_start, x[i], jnp.where(lane == row, 1.0, 0.0))
            ratio = jnp.where(odd, pltpu.roll(above / here, 1, axis=0), 0.0)
            above = jnp.where(odd, pltpu.roll(above, 1, axis=0), 0.0)
            scale = lax.rsqrt(here - ratio * above)
            done.append((unit - ratio * pltpu.roll(unit, 1, axis=0)) * scale)
        out.append(jnp.concatenate(done, axis=0))
    return out


def inverse_factors(grams):
    h = HALF
    m1 = eliminate([g[:h, :h] for g in grams])
    u12 = [exact(m, g[:h, h:]) for m, g in zip(m1, grams)]
    m2 = eliminate([g[h:, h:] - exact(u, u, 0, 0) for u, g in zip(u12, grams)])
    m21 = [-exact(b, exact(u, a, 0, 0)) for a, b, u in zip(m1, m2, u12)]
    zero = jnp.zeros((h, h), F32)
    return [
        jnp.concatenate(
            [jnp.concatenate([a, zero], axis=1), jnp.concatenate([c, b], axis=1)], axis=0
        )
        for a, b, c in zip(m1, m2, m21)
    ]


def prepare_kernel(ranks, tu, tv, sk, probe, upper, gram):
    rmax = sk.shape[1]
    t = pl.program_id(0)
    row = lax.broadcasted_iota(jnp.int32, (rmax, rmax), 0)
    col = lax.broadcasted_iota(jnp.int32, (rmax, rmax), 1)
    p = dot(tv[0], sk[...], 0, 0)
    p = jnp.where((row < ranks[t]) & (col < ranks[2 + t]), p, 0.0).astype(BF16)
    h = sum(dot(piece, p) for piece in pieces(dot(tu[0], tu[0], 0, 0), 3))
    probe[0] = p
    upper[0] = h
    gram[0] = 0.5 * sum(dot(p, piece, 0, 0) for piece in pieces(h, 3))


def prepare(ranks, trail_u, trail_v, sketch):
    width, rmax = sketch.shape
    square = lambda kind: jax.ShapeDtypeStruct((2, rmax, rmax), kind)
    tile = pl.BlockSpec((1, width, rmax), lambda t: (t, 0, 0))
    small = pl.BlockSpec((1, rmax, rmax), lambda t: (t, 0, 0))
    return pl.pallas_call(
        prepare_kernel,
        name="prepare",
        grid=(2,),
        out_shape=(square(BF16), square(F32), square(F32)),
        in_specs=[
            pl.BlockSpec(memory_space=pltpu.SMEM),
            tile,
            tile,
            pl.BlockSpec((width, rmax), lambda t: (0, 0)),
        ],
        out_specs=(small, small, small),
        compiler_params=pltpu.CompilerParams(vmem_limit_bytes=24 * 1024 * 1024),
        cost_estimate=pl.CostEstimate(
            flops=2_000_000_000, bytes_accessed=6_000_000, transcendentals=0
        ),
    )(ranks, trail_u, trail_v, sketch)


def reach_kernel(ranks, sk, up0, up1, up2, up3, out):
    part = up0.shape[0]
    total = None
    for k, block in enumerate((up0, up1, up2, up3)):
        at = pl.multiple_of(ranks[7 + k] * part, part)
        term = dot(block[...], sk[pl.ds(at, part)], 0, 0)
        total = term if total is None else total + term
    out[...] = total.astype(BF16)


def reach_of(ranks, sketch, uparts):
    rmax = sketch.shape[1]
    vmem = pl.BlockSpec(memory_space=pltpu.VMEM)
    return pl.pallas_call(
        reach_kernel,
        name="reach",
        out_shape=jax.ShapeDtypeStruct((rmax, rmax), BF16),
        in_specs=[pl.BlockSpec(memory_space=pltpu.SMEM)] + [vmem] * 5,
        out_specs=vmem,
        compiler_params=pltpu.CompilerParams(vmem_limit_bytes=12 * 1024 * 1024),
        cost_estimate=pl.CostEstimate(
            flops=300_000_000, bytes_accessed=2_200_000, transcendentals=0
        ),
    )(ranks, sketch, *uparts)


def tail_kernel(
    ranks,
    probe,
    upper,
    half,
    reach,
    gathered,
    vp0,
    vp1,
    vp2,
    vp3,
    up0,
    up1,
    up2,
    up3,
    trail_u,
    trail_v,
    fresh_u,
    fresh_v,
    dinv,
    vall,
    ui,
    uj,
    tu,
    tv,
    zs,
    bs,
    ou,
    ov,
    load_sem,
    out_sem,
):
    width, rmax = uj.shape
    part = width // 4
    loads = []

    def load(src, dst):
        copy = pltpu.make_async_copy(src, dst, load_sem.at[len(loads)])
        copy.start()
        loads.append(copy)
        return copy

    def spots():
        return [pl.multiple_of(ranks[7 + k] * part, part) for k in range(4)]

    need_v = [load(gathered.at[8 + t], vall.at[:, pl.ds(rmax * t, rmax)]) for t in range(2)]
    for at, src in zip(spots(), (vp0, vp1, vp2, vp3)):
        need_v.append(load(src, vall.at[pl.ds(at, part), pl.ds(2 * rmax, rmax)]))
    need_d = []
    for q in range(4):
        chunks, rows = pl.ds(0, 2 * q + 2), pl.ds(part * q, part)
        need_d.append(load(gathered.at[chunks, rows], dinv.at[chunks, rows]))
    need_u = [load(gathered.at[10 + t], ui.at[t]) for t in range(2)]
    need_u.append(load(trail_u, tu))
    rest = [load(src, uj.at[pl.ds(at, part)]) for at, src in zip(spots(), (up0, up1, up2, up3))]
    rest.append(load(trail_v, tv))

    for copy in need_v:
        copy.wait()
    coupling = [jnp.zeros((rmax, rmax), F32)] * 2
    for q in range(4):
        need_d[q].wait()
        for n in range(2):
            at = part * q + rmax * n
            count = 2 * q + 1 + n
            lhs = jnp.concatenate([dinv[c, at : at + rmax] for c in range(count)], axis=1)
            w = dot(lhs, vall[: rmax * count]).astype(BF16)
            wj = w[:, 2 * rmax :]
            coupling = [
                coupling[t] + dot(w[:, rmax * t : rmax * (t + 1)], wj, 0, 0) for t in range(2)
            ]
    for copy in need_u:
        copy.wait()

    row = lax.broadcasted_iota(jnp.int32, (rmax, rmax), 0)
    col = lax.broadcasted_iota(jnp.int32, (rmax, rmax), 1)
    couplings, grams, probes, products = [], [], [], []
    for t in range(2):
        new_rank, row_rank, col_rank = ranks[2 + t], ranks[4 + t], ranks[6]
        keep = col < new_rank
        top = probe[t]
        c = jnp.where((row < row_rank) & (col < col_rank), coupling[t], 0.0).astype(BF16)
        bottom = jnp.where(keep, -dot(c, reach[...]), 0.0).astype(BF16)
        gur = pieces(dot(tu[t], ui[t], 0, 0), 3)
        grr = pieces(dot(ui[t], ui[t], 0, 0), 3)
        cross = sum(dot(piece, top, 0, 0) for piece in gur)
        own = sum(dot(piece, bottom) for piece in grr)
        mixed = pieces(cross + 0.5 * own, 3)
        gram = half[t] + sum(dot(bottom, piece, 0, 0) for piece in mixed)
        grams.append(gram + gram.T + jnp.where((row == col) & ~keep, 1.0, 0.0))
        couplings.append(c)
        probes.append(jnp.concatenate([top, bottom], axis=0))
        above = upper[t] + sum(dot(piece, bottom) for piece in gur[:2])
        products.append(pieces(jnp.concatenate([above, cross + own], axis=0), 2))
    inverses = inverse_factors(grams)
    for t in range(2):
        m = pieces(inverses[t] * math.sqrt(width), 2)
        zs[t] = (dot(probes[t], m[0], 1, 1) + dot(probes[t], m[1], 1, 1)).astype(BF16)
        g = products[t]
        back = dot(g[0], m[0], 1, 1) + (dot(g[0], m[1], 1, 1) + dot(g[1], m[0], 1, 1))
        top = jnp.where(row < ranks[t], back[:rmax], 0.0)
        bottom = -dot(couplings[t], back[rmax:].astype(BF16), 0, 0)
        bs[t] = (jnp.concatenate([top, bottom], axis=0) / width).astype(BF16)
    for copy in rest:
        copy.wait()

    copies = []
    for t in range(2):
        for n in range(4):
            rows = pl.ds(part * n, part)
            left = jnp.concatenate([tu[t, rows], ui[t, rows]], axis=1)
            ou[t, rows] = dot(left, zs[t]).astype(BF16)
            right = jnp.concatenate([tv[t, rows], uj[rows]], axis=1)
            ov[t, rows] = dot(right, bs[t]).astype(BF16)
            for src, dst in ((ou, fresh_u), (ov, fresh_v)):
                copy = pltpu.make_async_copy(
                    src.at[t, rows], dst.at[t, rows], out_sem.at[len(copies)]
                )
                copy.start()
                copies.append(copy)
    for copy in copies:
        copy.wait()


def tail(ranks, probe, upper, half, reach, gathered, vparts, uparts, trail_u, trail_v):
    _, width, rmax = trail_u.shape
    vmem = pl.BlockSpec(memory_space=pltpu.VMEM)
    hbm = pl.BlockSpec(memory_space=pl.ANY)
    tile = jax.ShapeDtypeStruct(trail_u.shape, BF16)
    return pl.pallas_call(
        tail_kernel,
        name="tail",
        out_shape=(tile, tile),
        in_specs=[pl.BlockSpec(memory_space=pltpu.SMEM)] + [vmem] * 4 + [hbm] * 11,
        out_specs=(hbm, hbm),
        scratch_shapes=[
            pltpu.VMEM((8, width, rmax), BF16),
            pltpu.VMEM((width, 3 * rmax), BF16),
            pltpu.VMEM((2, width, rmax), BF16),
            pltpu.VMEM((width, rmax), BF16),
            pltpu.VMEM((2, width, rmax), BF16),
            pltpu.VMEM((2, width, rmax), BF16),
            pltpu.VMEM((2, 2 * rmax, rmax), BF16),
            pltpu.VMEM((2, 2 * rmax, rmax), BF16),
            pltpu.VMEM((2, width, rmax), BF16),
            pltpu.VMEM((2, width, rmax), BF16),
            pltpu.SemaphoreType.DMA((18,)),
            pltpu.SemaphoreType.DMA((16,)),
        ],
        compiler_params=pltpu.CompilerParams(vmem_limit_bytes=44 * 1024 * 1024),
        cost_estimate=pl.CostEstimate(
            flops=16_000_000_000, bytes_accessed=20_000_000, transcendentals=0
        ),
    )(ranks, probe, upper, half, reach, gathered, *vparts, *uparts, trail_u, trail_v)


def on_device(
    trail_u,
    trail_v,
    tile_rank,
    new_rank,
    row_u,
    row_v,
    row_rank,
    col_u,
    col_v,
    col_rank,
    diag_inv,
    sketch,
):
    trow, _, width, rmax = trail_u.shape
    x, z = lax.axis_index("x"), lax.axis_index("z")
    yc = lax.axis_index(("y", "c"))
    pcol = z * 8 + yc
    trail_u, trail_v = trail_u[:, 0], trail_v[:, 0]

    slab = diag_inv.shape[0]
    factor = jnp.swapaxes(diag_inv.astype(BF16).reshape(slab, width // rmax, rmax), 0, 1)
    mine = jnp.concatenate([factor, row_v, row_u], axis=0)
    gathered = lax.all_gather(mine, ("z", "y", "c"), axis=1, tiled=True)

    both = jnp.stack([col_v, col_u], axis=1)
    quarter = lax.all_to_all(both, ("y", "c"), split_axis=0, concat_axis=2, tiled=True)[0]
    times = (0, 2, 3, 1)
    swap = [(a * 4 + q, (times[a] ^ q) * 4 + a) for a in range(4) for q in range(4)]
    quarter = lax.ppermute(quarter, ("x", "z"), swap)

    def spread(block):
        return [block] + [
            lax.ppermute(block, "x", [(a, (a + k) % 4) for a in range(4)]) for k in (1, 3, 2)
        ]

    vparts = spread(quarter[0])
    uparts = spread(quarter[1])
    vparts = [vparts[0], vparts[1], vparts[3], vparts[2]]
    uparts = [uparts[0], uparts[1], uparts[3], uparts[2]]

    own_row = lax.dynamic_slice_in_dim(row_rank, x * trow, trow)
    own_col = lax.dynamic_slice_in_dim(col_rank, pcol, 1)
    turn = jnp.array(times, jnp.int32)[z]
    quarters = [(turn ^ lax.rem(x + 4 - k, 4))[None] for k in range(4)]
    ranks = jnp.concatenate([tile_rank[:, 0], new_rank[:, 0], own_row, own_col] + quarters)
    probe, upper, half = prepare(ranks, trail_u, trail_v, sketch)
    reach = reach_of(ranks, sketch, uparts)
    fresh_u, fresh_v = tail(
        ranks, probe, upper, half, reach, gathered, vparts, uparts, trail_u, trail_v
    )
    return fresh_u[:, None], fresh_v[:, None]


def solution(mesh):
    split = Mesh(mesh.devices.reshape(4, 4, 4, 2), ("x", "z", "y", "c"))
    cols = ("z", "y", "c")
    tiles = P("x", cols, None, None)
    panel = P("x", cols, None)
    return jax.shard_map(
        on_device,
        mesh=split,
        in_specs=(
            tiles,
            tiles,
            P("x", cols),
            P("x", cols),
            panel,
            panel,
            P(),
            panel,
            panel,
            P(),
            P(cols, None),
            P(),
        ),
        out_specs=(tiles, tiles),
        check_vma=False,
    )
```

time: 148 us -> 132 us (0.89)
  starting transfers between devices: 34.2 us -> 24.6 us
  local copies, waits for them, and re-layouts: 4.66 us -> 10.6 us
  Pallas kernels: 41.7 us -> 36 us
  waiting for transfers between devices: 30.2 us -> 25.6 us
  matrix products: 3.38 us -> 0 us
  between operations: 14.2 us -> 16.9 us
    pallas_call x1, Pallas kernels: 41.7 us -> 31.7 us  [tail(): pl.pallas_call(tail_kernel, name='tail', out_shape=(tile, tile), in_specs...]
    ppermute x6, waiting for transfers between devices: 16.4 us -> 7.3 us  [spread(): lax.ppermute(block, 'x', [(a, (a + k) % 4) for a in range(4)])]
    unnamed x32, local copies, waits for them, and re-layouts: 0.78 us -> 8.5 us
    ppermute x6, starting transfers between devices: 28.8 us -> 23.9 us  [spread(): lax.ppermute(block, 'x', [(a, (a + k) % 4) for a in range(4)])]
    ppermute x1, starting transfers between devices: 5.38 us -> 0.69 us  [on_device(): quarter = lax.ppermute(quarter, ('x', 'z'), swap)]
    all_gather x1, waiting for transfers between devices: 13.8 us -> 18.3 us  [on_device(): gathered = lax.all_gather(mine, ('z', 'y', 'c'), axis=1, tiled=True)]
    pallas_call x0 -> x2, Pallas kernels: none -> 4.35 us  [the longest x1 3.32 us: prepare(): pl.pallas_call(prepare_kernel, name='prepare', grid=(2,), out_shape=(squa...]
    dot_general x2 -> x0, matrix products: 3.38 us -> none  [the longest x1 1.83 us: on_device(): jnp.einsum('tbm,tbn->tmn', trail_u, trail_u, preferred_element_type=F32)]
  transfers between devices with their start and end apart: 8 -> 8, of which waited for: 5 -> 3; matrix products, arithmetic and copies ran while one was open for 6% -> 2% of each run, Pallas kernels for 0% -> 3%
where the time goes in v2:
time: 132 us
  Pallas kernels  36 us (27%)
  waiting for transfers between devices  25.6 us (19%)
  starting transfers between devices  24.6 us (19%)
  between operations  16.9 us (13%)
  blocking collectives  15.3 us (12%)
  local copies, waits for them, and re-layouts  10.6 us (8%)
  other arithmetic  2.87 us (2%)
    pallas_call x1, Pallas kernels, tail(): pl.pallas_call(tail_kernel, name='tail', out_shape=(tile, tile), in_specs...  31.7 us
    ppermute x6, starting transfers between devices, spread(): lax.ppermute(block, 'x', [(a, (a + k) % 4) for a in range(4)])  23.9 us
    all_gather x1, waiting for transfers between devices, on_device(): gathered = lax.all_gather(mine, ('z', 'y', 'c'), axis=1, tiled=True)  18.3 us
    all_to_all x1, blocking collectives, on_device(): lax.all_to_all(both, ('y', 'c'), split_axis=0, concat_axis=2, tiled=True)[0]  15.3 us
    unnamed x32, local copies, waits for them, and re-layouts  8.5 us
    ppermute x6, waiting for transfers between devices, spread(): lax.ppermute(block, 'x', [(a, (a + k) % 4) for a in range(4)])  7.3 us
    pallas_call x1, Pallas kernels, prepare(): pl.pallas_call(prepare_kernel, name='prepare', grid=(2,), out_shape=(squa...  3.32 us
  transfers between devices with their start and end apart: 8, of which 3 were waited for; matrix products, arithmetic and copies ran while one was open for 2% of the time, Pallas kernels for 3%

profile of v2, /device:TPU:1, one launch (start us, length us, event | category | flops | bytes accessed | tf_op | source)
XLA Modules:
  0.0 131.8 jit_solution(14261719883856761429)
XLA Ops:
  7.2 0.0 all-gather.2.cloned.1.call-start
  7.2 1.1 convert_element_type.3
  8.4 1.7 %pad_maximum_fusion.1 = bf16[12,64,256]{2,1,0:T(8,128)(2,1)} fusion(bf16[2,64,256]{2,1,0:T(8,128)(2,1)} %param.17, bf16[2,64,256]{2,1,0:T(8,128)(2,1)} %param.18, bf16[8,64,256]{2,1,0:T(8,128)(2,1)S(1)} %bitcast.37), kind=kLoop, calls=%fused_computation.1 | loop fusion | flops 393216 | bytes 786432 | tf_op jit(solution)/shard_map/concatenate | solution.py:357
  10.1 0.0 all-gather.2.cloned.1.call-update
  10.1 0.0 copy-start.15
  10.2 0.0 copy-start.11
  10.2 0.0 copy-start.12
  10.2 0.1 pad_maximum_fusion
  10.3 15.3 %all_to_all.15 = bf16[8,2,64,256]{3,2,1,0:T(8,128)(2,1)S(1)} all-to-all(bf16[8,2,64,256]{3,2,1,0:T(8,128)(2,1)S(1)} %pad_maximum_fusion), channel_id=1, replica_groups=mesh['x'=4,'z'=4,'y'=4,'c'=2] {'y','c'}, dimensions={0} | all-to-all | bytes 1048576 | tf_op jit(solution)/shard_map/all_to_all | solution.py:361
  25.6 0.7 collective-permute-start
  26.3 19.5 %collective-permute-start.3 = (bf16[512,256]{1,0:T(8,128)(2,1)S(1)}, bf16[512,256]{1,0:T(8,128)(2,1)S(1)}, u32[]{:S(2)}, u32[]{:S(2)}) collective-permute-start(bf16[512,256]{1,0:T(8,128)(2,1)S(1)} %get-tuple-element.19.up0), channel_id=1, source_target_pairs={{0,96},{32,0},{64,32},{96,64},{1,97},{33,1},{65,33},{97,65},{2,98}... | collective-permute-start | bytes 786440 | tf_op jit(solution)/shard_map/ppermute | solution.py:368
  45.8 0.9 collective-permute-start.2
  46.7 0.8 collective-permute-start.1
  47.5 1.9 %collective-permute-start.6 = (bf16[512,256]{1,0:T(8,128)(2,1)S(1)}, bf16[512,256]{1,0:T(8,128)(2,1)S(1)}, u32[]{:S(2)}, u32[]{:S(2)}) collective-permute-start(bf16[512,256]{1,0:T(8,128)(2,1)S(1)} %get-tuple-element.18.vp0), channel_id=1, source_target_pairs={{0,96},{32,0},{64,32},{96,64},{1,97},{33,1},{65,33},{97,65},{2,98}... | collective-permute-start | bytes 786440 | tf_op jit(solution)/shard_map/ppermute | solution.py:368
  49.4 0.9 collective-permute-start.5
  50.2 4.5 %collective-permute-done.3.up3 = bf16[512,256]{1,0:T(8,128)(2,1)S(1)} collective-permute-done((bf16[512,256]{1,0:T(8,128)(2,1)S(1)}, bf16[512,256]{1,0:T(8,128)(2,1)S(1)}, u32[]{:S(2)}, u32[]{:S(2)}) %collective-permute-start.3) | collective-permute-done | bytes 262176 | tf_op jit(solution)/shard_map/ppermute | solution.py:368
  54.7 0.6 dynamic_slice.11
  57.9 0.6 dynamic_slice.10
  58.5 0.1 dynamic_slice.9
  58.6 0.7 concatenate.6.ranks
  59.3 1.6 %copy-done.1 = bf16[2,1,2048,256]{3,2,1,0:T(8,128)(2,1)S(1)} copy-done((bf16[2,1,2048,256]{3,2,1,0:T(8,128)(2,1)S(1)}, bf16[2,1,2048,256]{3,2,1,0:T(8,128)(2,1)}, u32[]{:S(2)}) %copy-start.1) | copy-done | bytes 2097176
  60.9 1.6 %copy-done.3 = bf16[2,1,2048,256]{3,2,1,0:T(8,128)(2,1)S(1)} copy-done((bf16[2,1,2048,256]{3,2,1,0:T(8,128)(2,1)S(1)}, bf16[2,1,2048,256]{3,2,1,0:T(8,128)(2,1)}, u32[]{:S(2)}) %copy-start.3) | copy-done | bytes 2097176
  62.5 3.3 %prepare.1 = (bf16[2,256,256]{2,1,0:T(8,128)(2,1)S(1)}, f32[2,256,256]{2,1,0:T(8,128)S(1)}, f32[2,256,256]{2,1,0:T(8,128)S(1)}) custom-call(s32[11]{0:T(128)S(1)} %concatenate.6.ranks, bf16[2,2048,256]{2,1,0:T(8,128)(2,1)S(1)} %bitcast.32, bf16[2,2048,256]{2,1,0:T(8,128)(2,1)S(1)} %bitcast.34, bf16[2048,256]{1,0:T(8,128)(2,1)S(1)} %copy-done), custom_call_target="tpu_custom_call" | custom-call | flops 2000000000 | bytes 6000000 | tf_op jit(solution)/shard_map/prepare/pallas_call | solution.py:134
  65.9 1.0 reach.1
  66.9 0.0 collective-permute-done.6.vp3
  67.0 2.8 %collective-permute-done.4.vp1 = bf16[512,256]{1,0:T(8,128)(2,1)S(1)} collective-permute-done((bf16[512,256]{1,0:T(8,128)(2,1)S(1)}, bf16[512,256]{1,0:T(8,128)(2,1)S(1)}, u32[]{:S(2)}, u32[]{:S(2)}) %collective-permute-start.4) | collective-permute-done | bytes 262176 | tf_op jit(solution)/shard_map/ppermute | solution.py:368
  69.7 18.3 %all-gather.2.cloned.1.call-done.gathered = bf16[12,2048,256]{2,1,0:T(8,128)(2,1)} async-done(((bf16[12,64,256]{2,1,0:T(8,128)(2,1)}), bf16[12,2048,256]{2,1,0:T(8,128)(2,1)}) %all-gather.2.cloned.1.call-update) | async-done | bytes 12582928 | tf_op jit(solution)/shard_map/all_gather | solution.py:358
  88.0 1.6 %copy-done.2 = bf16[2,1,2048,256]{3,2,1,0:T(8,128)(2,1)S(1)} copy-done((bf16[2,1,2048,256]{3,2,1,0:T(8,128)(2,1)S(1)}, bf16[2,1,2048,256]{3,2,1,0:T(8,128)(2,1)}, u32[]{:S(2)}) %copy-start.2) | copy-done | bytes 2097176
  89.6 1.6 %copy-done.4 = bf16[2,1,2048,256]{3,2,1,0:T(8,128)(2,1)S(1)} copy-done((bf16[2,1,2048,256]{3,2,1,0:T(8,128)(2,1)S(1)}, bf16[2,1,2048,256]{3,2,1,0:T(8,128)(2,1)}, u32[]{:S(2)}) %copy-start.4) | copy-done | bytes 2097176
  91.2 1.0 copy-done.6
  92.2 1.0 copy-done.8
  93.3 31.7 %tail.1 = (bf16[2,2048,256]{2,1,0:T(8,128)(2,1)}, bf16[2,2048,256]{2,1,0:T(8,128)(2,1)}) custom-call(s32[11]{0:T(128)S(1)} %concatenate.6.ranks, bf16[2,256,256]{2,1,0:T(8,128)(2,1)S(1)} %get-tuple-element.7.probe, f32[2,256,256]{2,1,0:T(8,128)S(1)} %copy-done.6, f32[2,256,256]{2,1,0:T(8,128)S(1)} %copy-done.8, bf16[256,256]{1,0:T(8,128)(2,1)S(1)} %reach.1, ...), custom_call_target="tpu_custom_call" | custom-call | flops 16000000000 | bytes 20000000 | tf_op jit(solution)/shard_map/tail/pallas_call | solution.py:308
  (31 shorter events, 0.2 us)
Async XLA Ops:
  7.2 2.9 %copy-start.10 = (bf16[8,64,256]{2,1,0:T(8,128)(2,1)S(1)}, bf16[8,64,256]{2,1,0:T(8,128)(2,1)}, u32[]{:S(2)}) copy-start(bf16[8,64,256]{2,1,0:T(8,128)(2,1)} %param.21) | copy-start | bytes 786436
  7.2 2.9 %copy-start.9 = (bf16[8,64,256]{2,1,0:T(8,128)(2,1)S(1)}, bf16[8,64,256]{2,1,0:T(8,128)(2,1)}, u32[]{:S(2)}) copy-start(bf16[8,64,256]{2,1,0:T(8,128)(2,1)} %param.20) | copy-start | bytes 786436
  7.2 80.8 %all-gather.2.cloned.1.call-start = ((), (), s32[]{:S(2)}) async-start(), calls=%async_computation.1 | async-start | bytes 12976128 | tf_op jit(solution)/shard_map/all_gather | solution.py:358
  10.1 44.6 %copy-start.15 = (s32[4]{0:T(128)S(1)}, s32[4]{0:T(128)}, u32[]{:S(2)}) copy-start(s32[4]{0:T(128)} %constant.45.clone) | copy-start | bytes 52
  10.1 47.8 %copy-start.13 = (s32[32]{0:T(128)S(1)}, s32[32]{0:T(128)}, u32[]{:S(2)}) copy-start(s32[32]{0:T(128)} %param.22) | copy-start | bytes 388
  10.1 48.4 %copy-start.14 = (s32[8]{0:T(128)S(1)}, s32[8]{0:T(128)}, u32[]{:S(2)}) copy-start(s32[8]{0:T(128)} %param.19) | copy-start | bytes 100
  10.2 48.4 %copy-start.11 = (s32[2,1]{0,1:T(1,128)S(1)}, s32[2,1]{0,1:T(1,128)}, u32[]{:S(2)}) copy-start(s32[2,1]{0,1:T(1,128)} %param.15) | copy-start | bytes 28
  10.2 48.4 %copy-start.12 = (s32[2,1]{0,1:T(1,128)S(1)}, s32[2,1]{0,1:T(1,128)}, u32[]{:S(2)}) copy-start(s32[2,1]{0,1:T(1,128)} %param.16) | copy-start | bytes 28
  10.2 49.1 %copy-start = (bf16[2048,256]{1,0:T(8,128)(2,1)S(1)}, bf16[2048,256]{1,0:T(8,128)(2,1)}, u32[]{:S(2)}) copy-start(bf16[2048,256]{1,0:T(8,128)(2,1)} %sk.3) | copy-start | bytes 3145732
  25.6 0.7 collective-permute-start
  26.3 28.4 %collective-permute-start.3 = (bf16[512,256]{1,0:T(8,128)(2,1)S(1)}, bf16[512,256]{1,0:T(8,128)(2,1)S(1)}, u32[]{:S(2)}, u32[]{:S(2)}) collective-permute-start(bf16[512,256]{1,0:T(8,128)(2,1)S(1)} %get-tuple-element.19.up0), channel_id=1, source_target_pairs={{0,96},{32,0},{64,32},{96,64},{1,97},{33,1},{65,33},{97,65},{2,98}... | collective-permute-start | bytes 786440 | tf_op jit(solution)/shard_map/ppermute | solution.py:368
  45.8 20.1 %collective-permute-start.2 = (bf16[512,256]{1,0:T(8,128)(2,1)S(1)}, bf16[512,256]{1,0:T(8,128)(2,1)S(1)}, u32[]{:S(2)}, u32[]{:S(2)}) collective-permute-start(bf16[512,256]{1,0:T(8,128)(2,1)S(1)} %get-tuple-element.19.up0), channel_id=1, source_target_pairs={{0,64},{32,96},{64,0},{96,32},{1,65},{33,97},{65,1},{97,33},{2,66}... | collective-permute-start | bytes 786440 | tf_op jit(solution)/shard_map/ppermute | solution.py:368
  46.7 19.2 %collective-permute-start.1 = (bf16[512,256]{1,0:T(8,128)(2,1)S(1)}, bf16[512,256]{1,0:T(8,128)(2,1)S(1)}, u32[]{:S(2)}, u32[]{:S(2)}) collective-permute-start(bf16[512,256]{1,0:T(8,128)(2,1)S(1)} %get-tuple-element.19.up0), channel_id=1, source_target_pairs={{0,32},{32,64},{64,96},{96,0},{1,33},{33,65},{65,97},{97,1},{2,34}... | collective-permute-start | bytes 786440 | tf_op jit(solution)/shard_map/ppermute | solution.py:368
  47.5 19.5 %collective-permute-start.6 = (bf16[512,256]{1,0:T(8,128)(2,1)S(1)}, bf16[512,256]{1,0:T(8,128)(2,1)S(1)}, u32[]{:S(2)}, u32[]{:S(2)}) collective-permute-start(bf16[512,256]{1,0:T(8,128)(2,1)S(1)} %get-tuple-element.18.vp0), channel_id=1, source_target_pairs={{0,96},{32,0},{64,32},{96,64},{1,97},{33,1},{65,33},{97,65},{2,98}... | collective-permute-start | bytes 786440 | tf_op jit(solution)/shard_map/ppermute | solution.py:368
  49.4 17.6 %collective-permute-start.5 = (bf16[512,256]{1,0:T(8,128)(2,1)S(1)}, bf16[512,256]{1,0:T(8,128)(2,1)S(1)}, u32[]{:S(2)}, u32[]{:S(2)}) collective-permute-start(bf16[512,256]{1,0:T(8,128)(2,1)S(1)} %get-tuple-element.18.vp0), channel_id=1, source_target_pairs={{0,64},{32,96},{64,0},{96,32},{1,65},{33,97},{65,1},{97,33},{2,66}... | collective-permute-start | bytes 786440 | tf_op jit(solution)/shard_map/ppermute | solution.py:368
  54.7 15.0 %collective-permute-start.4 = (bf16[512,256]{1,0:T(8,128)(2,1)S(1)}, bf16[512,256]{1,0:T(8,128)(2,1)S(1)}, u32[]{:S(2)}, u32[]{:S(2)}) collective-permute-start(bf16[512,256]{1,0:T(8,128)(2,1)S(1)} %get-tuple-element.18.vp0), channel_id=1, source_target_pairs={{0,32},{32,64},{64,96},{96,0},{1,33},{33,65},{65,97},{97,1},{2,34}... | collective-permute-start | bytes 786440 | tf_op jit(solution)/shard_map/ppermute | solution.py:368
  59.3 1.6 %copy-start.1 = (bf16[2,1,2048,256]{3,2,1,0:T(8,128)(2,1)S(1)}, bf16[2,1,2048,256]{3,2,1,0:T(8,128)(2,1)}, u32[]{:S(2)}) copy-start(bf16[2,1,2048,256]{3,2,1,0:T(8,128)(2,1)} %param.13) | copy-start | bytes 6291460
  60.9 1.6 %copy-start.3 = (bf16[2,1,2048,256]{3,2,1,0:T(8,128)(2,1)S(1)}, bf16[2,1,2048,256]{3,2,1,0:T(8,128)(2,1)}, u32[]{:S(2)}) copy-start(bf16[2,1,2048,256]{3,2,1,0:T(8,128)(2,1)} %param.14) | copy-start | bytes 6291460
  65.8 1.1 copy-start.5
  65.9 1.1 copy-start.7
  88.0 1.6 %copy-start.2 = (bf16[2,1,2048,256]{3,2,1,0:T(8,128)(2,1)S(1)}, bf16[2,1,2048,256]{3,2,1,0:T(8,128)(2,1)}, u32[]{:S(2)}) copy-start(bf16[2,1,2048,256]{3,2,1,0:T(8,128)(2,1)} %param.13) | copy-start | bytes 6291460
  89.6 1.6 %copy-start.4 = (bf16[2,1,2048,256]{3,2,1,0:T(8,128)(2,1)S(1)}, bf16[2,1,2048,256]{3,2,1,0:T(8,128)(2,1)}, u32[]{:S(2)}) copy-start(bf16[2,1,2048,256]{3,2,1,0:T(8,128)(2,1)} %param.14) | copy-start | bytes 6291460
  91.2 1.0 copy-start.6
  92.2 1.0 copy-start.8
Sparse Core Ops, SparseCore 0:
  10.3 77.6 all-gather.1

commit v3 on v2

--- a/solution.py
+++ b/solution.py
@@ -48,36 +48,41 @@
     sub = lax.broadcasted_iota(jnp.int32, (8, n), 0)
     spread = lambda v, r: jnp.broadcast_to(v[r : r + 1], (8, n))
     tiles = [[m[8 * i : 8 * i + 8] for i in range(groups)] for m in blocks]
+
+    def column(v, at):
+        return jnp.broadcast_to(jnp.sum(jnp.where(lane == at, v, 0.0), axis=1, keepdims=True), (8, n))
+
     for g in range(groups):
         panel = (lane >= 8 * g) & (lane < 8 * g + 8)
         for x in tiles:
-            cols = [[jnp.broadcast_to(x[i][:, 8 * g + j : 8 * g + j + 1], (8, n)) for i in range(g, groups)] for j in range(8)]
-            top = x[g]
-            factors = []
+            cols = [[column(x[i], 8 * g + j) for j in range(8)] for i in range(g, groups)]
+            top, own, kept = x[g], cols[0], x[g]
             for m in range(0, 8, 2):
-                c0, c1 = cols[m], cols[m + 1]
-                a, b, c = spread(c0[0], m), spread(c1[0], m), spread(c1[0], m + 1)
+                c0, c1 = own[m], own[m + 1]
+                a, b, c = spread(c0, m), spread(c1, m), spread(c1, m + 1)
                 inv = reciprocal(a * c - b * b)
                 ai, bi, ci = a * inv, b * inv, c * inv
+                upper, lower = sub == m, sub == m + 1
                 for j in range(m + 2, 8):
-                    s0, s1 = spread(c0[0], j), spread(c1[0], j)
+                    s0, s1 = spread(own[j], m), spread(own[j], m + 1)
                     g0, g1 = ci * s0 - bi * s1, ai * s1 - bi * s0
-                    cols[j] = [v - (p * g0 + q * g1) for v, p, q in zip(cols[j], c0, c1)]
+                    own[j] = jnp.where(upper, g0, jnp.where(lower, g1, own[j] - (c0 * g0 + c1 * g1)))
                 k = 8 * g + m
-                later = (lane > k + 1) & (lane < 8 * g + 8)
+                first, second = lane == k, lane == k + 1
+                if m:
+                    kept = jnp.where(upper | lower, top, kept)
                 r0, r1 = spread(top, m), spread(top, m + 1)
-                first, second = lane == k, lane == k + 1
                 r0 = jnp.where(first, 1.0, jnp.where(second, 0.0, r0))
                 r1 = jnp.where(second, 1.0, jnp.where(first, 0.0, r1))
                 q0, q1 = ci * r0 - bi * r1, ai * r1 - bi * r0
-                if m < 6:
-                    new = jnp.where(first | second, 0.0, top) - (c0[0] * q0 + c1[0] * q1)
-                    top = jnp.where(sub > m + 1, new, top)
-                factors.append((jnp.where(later, 0.0, q0), jnp.where(later, 0.0, q1)))
-            x[g] = top
-            for t in range(1, groups - g):
-                terms = [cols[2 * p][t] * q0 + cols[2 * p + 1][t] * q1 for p, (q0, q1) in enumerate(factors)]
-                x[g + t] = jnp.where(panel, 0.0, x[g + t]) - tree(terms)
+                new = jnp.where(first | second, 0.0, top) - (c0 * q0 + c1 * q1)
+                top = jnp.where(upper, q0, jnp.where(lower, q1, new))
+            x[g] = kept
+            if g + 1 < groups:
+                solved = [spread(top, m) for m in range(8)]
+                for t in range(1, groups - g):
+                    terms = [cols[t][m] * solved[m] for m in range(8)]
+                    x[g + t] = jnp.where(panel, 0.0, x[g + t]) - tree(terms)
     odd = (sub % 2) == 1
     out = []
     for x in tiles:
@@ -111,6 +116,26 @@
         )
         for a, b, c in zip(m1, m2, m21)
     ]
+
+
+def pack_kernel(diag, row_v, row_u, out):
+    chunks = out.shape[0] - 4
+    rmax = out.shape[2]
+    for c in range(chunks):
+        out[c] = diag[:, rmax * c : rmax * (c + 1)].astype(BF16)
+    out[chunks : chunks + 2] = row_v[...]
+    out[chunks + 2 :] = row_u[...]
+
+
+def pack(diag_inv, row_v, row_u):
+    count, slab, rmax = row_v.shape
+    chunks = diag_inv.shape[1] // rmax
+    return pl.pallas_call(
+        pack_kernel,
+        name="pack",
+        out_shape=jax.ShapeDtypeStruct((chunks + 2 * count, slab, rmax), BF16),
+        cost_estimate=pl.CostEstimate(flops=0, bytes_accessed=1_100_000, transcendentals=0),
+    )(diag_inv, row_v, row_u)
 
 
 def prepare_kernel(ranks, tu, tv, sk, probe, upper, gram):
@@ -205,11 +230,16 @@
     bs,
     ou,
     ov,
+    pv,
+    hv,
+    gv,
+    rv,
     load_sem,
     out_sem,
 ):
     width, rmax = uj.shape
     part = width // 4
+    smalls = (pv, hv, gv, rv)
     loads = []
 
     def load(src, dst):
@@ -221,23 +251,27 @@
     def spots():
         return [pl.multiple_of(ranks[7 + k] * part, part) for k in range(4)]
 
+    def load_d(q):
+        chunks, rows = pl.ds(0, 2 * q + 2), pl.ds(part * q, part)
+        return load(gathered.at[chunks, rows], dinv.at[chunks, rows])
+
     need_v = [load(gathered.at[8 + t], vall.at[:, pl.ds(rmax * t, rmax)]) for t in range(2)]
     for at, src in zip(spots(), (vp0, vp1, vp2, vp3)):
         need_v.append(load(src, vall.at[pl.ds(at, part), pl.ds(2 * rmax, rmax)]))
-    need_d = []
-    for q in range(4):
-        chunks, rows = pl.ds(0, 2 * q + 2), pl.ds(part * q, part)
-        need_d.append(load(gathered.at[chunks, rows], dinv.at[chunks, rows]))
-    need_u = [load(gathered.at[10 + t], ui.at[t]) for t in range(2)]
-    need_u.append(load(trail_u, tu))
-    rest = [load(src, uj.at[pl.ds(at, part)]) for at, src in zip(spots(), (up0, up1, up2, up3))]
-    rest.append(load(trail_v, tv))
-
+    need_d = [load_d(0), load_d(1)]
     for copy in need_v:
         copy.wait()
+    need_d += [load_d(2), load_d(3)]
     coupling = [jnp.zeros((rmax, rmax), F32)] * 2
     for q in range(4):
         need_d[q].wait()
+        if q == 1:
+            need_u = [load(gathered.at[10 + t], ui.at[t]) for t in range(2)]
+            need_u.append(load(trail_u, tu))
+            need_u += [load(a, b) for a, b in zip((probe, upper, half, reach), smalls)]
+        if q == 2:
+            rest = [load(a, uj.at[pl.ds(at, part)]) for at, a in zip(spots(), (up0, up1, up2, up3))]
+            rest.append(load(trail_v, tv))
         for n in range(2):
             at = part * q + rmax * n
             count = 2 * q + 1 + n
@@ -249,6 +283,7 @@
             ]
     for copy in need_u:
         copy.wait()
+    probe, upper, half, reach = smalls
 
     row = lax.broadcasted_iota(jnp.int32, (rmax, rmax), 0)
     col = lax.broadcasted_iota(jnp.int32, (rmax, rmax), 1)
@@ -302,14 +337,13 @@
 
 def tail(ranks, probe, upper, half, reach, gathered, vparts, uparts, trail_u, trail_v):
     _, width, rmax = trail_u.shape
-    vmem = pl.BlockSpec(memory_space=pltpu.VMEM)
     hbm = pl.BlockSpec(memory_space=pl.ANY)
     tile = jax.ShapeDtypeStruct(trail_u.shape, BF16)
     return pl.pallas_call(
         tail_kernel,
         name="tail",
         out_shape=(tile, tile),
-        in_specs=[pl.BlockSpec(memory_space=pltpu.SMEM)] + [vmem] * 4 + [hbm] * 11,
+        in_specs=[pl.BlockSpec(memory_space=pltpu.SMEM)] + [hbm] * 15,
         out_specs=(hbm, hbm),
         scratch_shapes=[
             pltpu.VMEM((8, width, rmax), BF16),
@@ -322,10 +356,14 @@
             pltpu.VMEM((2, 2 * rmax, rmax), BF16),
             pltpu.VMEM((2, width, rmax), BF16),
             pltpu.VMEM((2, width, rmax), BF16),
-            pltpu.SemaphoreType.DMA((18,)),
+            pltpu.VMEM((2, rmax, rmax), BF16),
+            pltpu.VMEM((2, rmax, rmax), F32),
+            pltpu.VMEM((2, rmax, rmax), F32),
+            pltpu.VMEM((rmax, rmax), BF16),
+            pltpu.SemaphoreType.DMA((22,)),
             pltpu.SemaphoreType.DMA((16,)),
         ],
-        compiler_params=pltpu.CompilerParams(vmem_limit_bytes=44 * 1024 * 1024),
+        compiler_params=pltpu.CompilerParams(vmem_limit_bytes=56 * 1024 * 1024),
         cost_estimate=pl.CostEstimate(
             flops=16_000_000_000, bytes_accessed=20_000_000, transcendentals=0
         ),
@@ -352,16 +390,12 @@
     pcol = z * 8 + yc
     trail_u, trail_v = trail_u[:, 0], trail_v[:, 0]
 
-    slab = diag_inv.shape[0]
-    factor = jnp.swapaxes(diag_inv.astype(BF16).reshape(slab, width // rmax, rmax), 0, 1)
-    mine = jnp.concatenate([factor, row_v, row_u], axis=0)
-    gathered = lax.all_gather(mine, ("z", "y", "c"), axis=1, tiled=True)
-
-    both = jnp.stack([col_v, col_u], axis=1)
-    quarter = lax.all_to_all(both, ("y", "c"), split_axis=0, concat_axis=2, tiled=True)[0]
+    gathered = lax.all_gather(pack(diag_inv, row_v, row_u), ("z", "y", "c"), axis=1, tiled=True)
+
     times = (0, 2, 3, 1)
     swap = [(a * 4 + q, (times[a] ^ q) * 4 + a) for a in range(4) for q in range(4)]
-    quarter = lax.ppermute(quarter, ("x", "z"), swap)
+    quarter = lax.ppermute(jnp.stack([col_v, col_u], axis=1), ("x", "z"), swap)
+    quarter = lax.all_to_all(quarter, ("y", "c"), split_axis=0, concat_axis=2, tiled=True)[0]
 
     def spread(block):
         return [block] + [

time: 132 us -> 117 us (0.89)
  waiting for transfers between devices: 25.6 us -> 16.2 us
  local copies, waits for them, and re-layouts: 10.6 us -> 6.34 us
  starting transfers between devices: 24.6 us -> 27.5 us
  Pallas kernels: 36 us -> 33.5 us
  other arithmetic: 2.87 us -> 1.17 us
    all_gather x1, waiting for transfers between devices: 18.3 us -> 7.58 us  [on_device(): lax.all_gather(pack(diag_inv, row_v, row_u), ('z', 'y', 'c'), axis=1, til...]
    pallas_call x1, Pallas kernels: 31.7 us -> 27.1 us  [tail(): pl.pallas_call(tail_kernel, name='tail', out_shape=(tile, tile), in_specs...]
    unnamed x32 -> x42, local copies, waits for them, and re-layouts: 8.5 us -> 4.32 us
    ppermute x6, starting transfers between devices: 23.9 us -> 26.8 us  [spread(): lax.ppermute(block, 'x', [(a, (a + k) % 4) for a in range(4)])]
    pallas_call x0 -> x1, Pallas kernels: none -> 1.86 us  [pack(): pl.pallas_call(pack_kernel, name='pack', out_shape=jax.ShapeDtypeStruct((...]
    concatenate x1 -> x0, other arithmetic: 1.7 us -> none  [on_device(): mine = jnp.concatenate([factor, row_v, row_u], axis=0)]
  transfers between devices with their start and end apart: 8 -> 8, of which waited for: 3 -> 3; matrix products, arithmetic and copies ran while one was open for 2% -> 3% of each run, Pallas kernels for 3% -> 4%
where the time goes in v3:
time: 117 us
  Pallas kernels  33.5 us (29%)
  starting transfers between devices  27.5 us (24%)
  between operations  16.9 us (14%)
  waiting for transfers between devices  16.2 us (14%)
  blocking collectives  15.1 us (13%)
  local copies, waits for them, and re-layouts  6.34 us (5%)
  other arithmetic  1.17 us (1%)
    pallas_call x1, Pallas kernels, tail(): pl.pallas_call(tail_kernel, name='tail', out_shape=(tile, tile), in_specs...  27.1 us
    ppermute x6, starting transfers between devices, spread(): lax.ppermute(block, 'x', [(a, (a + k) % 4) for a in range(4)])  26.8 us
    all_to_all x1, blocking collectives, on_device(): lax.all_to_all(quarter, ('y', 'c'), split_axis=0, concat_axis=2, tiled=True)  15.1 us
    ppermute x6, waiting for transfers between devices, spread(): lax.ppermute(block, 'x', [(a, (a + k) % 4) for a in range(4)])  8.58 us
    all_gather x1, waiting for transfers between devices, on_device(): lax.all_gather(pack(diag_inv, row_v, row_u), ('z', 'y', 'c'), axis=1, til...  7.58 us
    unnamed x42, local copies, waits for them, and re-layouts  4.32 us
    pallas_call x1, Pallas kernels, prepare(): pl.pallas_call(prepare_kernel, name='prepare', grid=(2,), out_shape=(squa...  3.5 us
  transfers between devices with their start and end apart: 8, of which 3 were waited for; matrix products, arithmetic and copies ran while one was open for 3% of the time, Pallas kernels for 4%

profile of v3, /device:TPU:1, one launch (start us, length us, event | category | flops | bytes accessed | tf_op | source)
XLA Modules:
  0.0 116.7 jit_solution(14233781615938370055)
XLA Ops:
  7.2 0.0 copy-start.20
  7.2 0.0 all-gather.2.cloned.1.call-start
  7.2 1.9 %pack.1 = bf16[12,64,256]{2,1,0:T(8,128)(2,1)} custom-call(f32[64,2048]{1,0:T(8,128)} %diag.1, bf16[2,64,256]{2,1,0:T(8,128)(2,1)} %row_v.1, bf16[2,64,256]{2,1,0:T(8,128)(2,1)} %row_u.1), custom_call_target="tpu_custom_call" | custom-call | bytes 1100000 | tf_op jit(solution)/shard_map/pack/pallas_call | solution.py:133
  9.1 0.0 copy-start
  9.1 0.0 all-gather.2.cloned.1.call-update
  9.1 1.2 %pad_maximum_fusion = bf16[8,2,64,256]{3,2,1,0:T(8,128)(2,1)S(1)} fusion(bf16[8,1,64,256]{3,2,1,0:T(8,128)(2,1)} %bitcast.32, bf16[8,1,64,256]{3,2,1,0:T(8,128)(2,1)} %bitcast.33), kind=kLoop, calls=%fused_computation | loop fusion | flops 262144 | bytes 1048576 | tf_op jit(solution)/shard_map/stack | solution.py:397
  10.3 0.7 collective-permute-start
  11.0 0.0 collective-permute-done
  11.0 15.1 %all_to_all.15 = bf16[8,2,64,256]{3,2,1,0:T(8,128)(2,1)S(1)} all-to-all(bf16[8,2,64,256]{3,2,1,0:T(8,128)(2,1)S(1)} %collective-permute-done), channel_id=1, replica_groups=mesh['x'=4,'z'=4,'y'=4,'c'=2] {'y','c'}, dimensions={0} | all-to-all | bytes 1048576 | tf_op jit(solution)/shard_map/all_to_all | solution.py:398
  26.2 22.3 %collective-permute-start.3 = (bf16[512,256]{1,0:T(8,128)(2,1)S(1)}, bf16[512,256]{1,0:T(8,128)(2,1)S(1)}, u32[]{:S(2)}, u32[]{:S(2)}) collective-permute-start(bf16[512,256]{1,0:T(8,128)(2,1)S(1)} %bitcast.22), channel_id=1, source_target_pairs={{0,96},{32,0},{64,32},{96,64},{1,97},{33,1},{65,33},{97,65},{2,98}... | collective-permute-start | bytes 786440 | tf_op jit(solution)/shard_map/ppermute | solution.py:402
  48.5 0.4 collective-permute-start.2
  49.0 0.8 collective-permute-start.1
  49.8 1.9 %collective-permute-start.6 = (bf16[512,256]{1,0:T(8,128)(2,1)S(1)}, bf16[512,256]{1,0:T(8,128)(2,1)S(1)}, u32[]{:S(2)}, u32[]{:S(2)}) collective-permute-start(bf16[512,256]{1,0:T(8,128)(2,1)S(1)} %bitcast.34), channel_id=1, source_target_pairs={{0,96},{32,0},{64,32},{96,64},{1,97},{33,1},{65,33},{97,65},{2,98}... | collective-permute-start | bytes 786440 | tf_op jit(solution)/shard_map/ppermute | solution.py:402
  51.7 1.3 %collective-permute-start.5 = (bf16[512,256]{1,0:T(8,128)(2,1)S(1)}, bf16[512,256]{1,0:T(8,128)(2,1)S(1)}, u32[]{:S(2)}, u32[]{:S(2)}) collective-permute-start(bf16[512,256]{1,0:T(8,128)(2,1)S(1)} %bitcast.35), channel_id=1, source_target_pairs={{0,64},{32,96},{64,0},{96,32},{1,65},{33,97},{65,1},{97,33},{2,66}... | collective-permute-start | bytes 786440 | tf_op jit(solution)/shard_map/ppermute | solution.py:402
  53.0 6.2 %collective-permute-done.3.up3 = bf16[512,256]{1,0:T(8,128)(2,1)S(1)} collective-permute-done((bf16[512,256]{1,0:T(8,128)(2,1)S(1)}, bf16[512,256]{1,0:T(8,128)(2,1)S(1)}, u32[]{:S(2)}, u32[]{:S(2)}) %collective-permute-start.3) | collective-permute-done | bytes 262176 | tf_op jit(solution)/shard_map/ppermute | solution.py:402
  59.2 0.0 collective-permute-start.4
  59.2 0.6 dynamic_slice.11
  62.4 0.6 dynamic_slice.10
  63.0 0.1 dynamic_slice.9
  63.1 0.7 concatenate.3.ranks
  63.8 0.0 copy-start.7
  63.8 1.8 %copy-done.7 = bf16[2,1,2048,256]{3,2,1,0:T(8,128)(2,1)S(1)} copy-done((bf16[2,1,2048,256]{3,2,1,0:T(8,128)(2,1)S(1)}, bf16[2,1,2048,256]{3,2,1,0:T(8,128)(2,1)}, u32[]{:S(2)}) %copy-start.7) | copy-done | bytes 2097176
  65.7 1.8 %copy-done.8 = bf16[2,1,2048,256]{3,2,1,0:T(8,128)(2,1)S(1)} copy-done((bf16[2,1,2048,256]{3,2,1,0:T(8,128)(2,1)S(1)}, bf16[2,1,2048,256]{3,2,1,0:T(8,128)(2,1)}, u32[]{:S(2)}) %copy-start.8) | copy-done | bytes 2097176
  67.4 3.5 %prepare.1 = (bf16[2,256,256]{2,1,0:T(8,128)(2,1)S(1)}, f32[2,256,256]{2,1,0:T(8,128)S(1)}, f32[2,256,256]{2,1,0:T(8,128)S(1)}) custom-call(s32[11]{0:T(128)S(1)} %concatenate.3.ranks, bf16[2,2048,256]{2,1,0:T(8,128)(2,1)S(1)} %bitcast.28, bf16[2,2048,256]{2,1,0:T(8,128)(2,1)S(1)} %bitcast.30, bf16[2048,256]{1,0:T(8,128)(2,1)S(1)} %copy-done), custom_call_target="tpu_custom_call" | custom-call | flops 2000000000 | bytes 6000000 | tf_op jit(solution)/shard_map/prepare/pallas_call | solution.py:159
  71.0 0.0 collective-permute-done.2.up2
  71.0 0.0 collective-permute-done.1.up1
  71.1 1.0 reach.1
  72.1 0.6 copy-done.5
  72.8 0.0 collective-permute-done.5.vp2
  72.8 2.3 %collective-permute-done.4.vp1 = bf16[512,256]{1,0:T(8,128)(2,1)S(1)} collective-permute-done((bf16[512,256]{1,0:T(8,128)(2,1)S(1)}, bf16[512,256]{1,0:T(8,128)(2,1)S(1)}, u32[]{:S(2)}, u32[]{:S(2)}) %collective-permute-start.4) | collective-permute-done | bytes 262176 | tf_op jit(solution)/shard_map/ppermute | solution.py:402
  75.1 7.6 %all-gather.2.cloned.1.call-done.gathered = bf16[12,2048,256]{2,1,0:T(8,128)(2,1)} async-done(((bf16[12,64,256]{2,1,0:T(8,128)(2,1)}), bf16[12,2048,256]{2,1,0:T(8,128)(2,1)}) %all-gather.2.cloned.1.call-update) | async-done | bytes 12582928 | tf_op jit(solution)/shard_map/all_gather | solution.py:393
  82.7 27.1 %tail.1 = (bf16[2,2048,256]{2,1,0:T(8,128)(2,1)}, bf16[2,2048,256]{2,1,0:T(8,128)(2,1)}) custom-call(s32[11]{0:T(128)} %copy-done.6, bf16[2,256,256]{2,1,0:T(8,128)(2,1)} %copy-done.11, f32[2,256,256]{2,1,0:T(8,128)} %copy-done.9, f32[2,256,256]{2,1,0:T(8,128)} %copy-done.10, bf16[256,256]{1,0:T(8,128)(2,1)} %copy-done.5, ...), custom_call_target="tpu_custom_call" | custom-call | flops 16000000000 | bytes 20000000 | tf_op jit(solution)/shard_map/tail/pallas_call | solution.py:342
  (38 shorter events, 0.1 us)
Async XLA Ops:
  7.2 52.1 %copy-start.20 = (s32[4]{0:T(128)S(1)}, s32[4]{0:T(128)}, u32[]{:S(2)}) copy-start(s32[4]{0:T(128)} %constant.45.clone) | copy-start | bytes 52
  7.2 75.5 %all-gather.2.cloned.1.call-start = ((), (), s32[]{:S(2)}) async-start(), calls=%async_computation.1 | async-start | bytes 12976128 | tf_op jit(solution)/shard_map/all_gather | solution.py:393
  9.1 53.3 %copy-start.18 = (s32[32]{0:T(128)S(1)}, s32[32]{0:T(128)}, u32[]{:S(2)}) copy-start(s32[32]{0:T(128)} %param.22) | copy-start | bytes 388
  9.1 53.9 %copy-start.19 = (s32[8]{0:T(128)S(1)}, s32[8]{0:T(128)}, u32[]{:S(2)}) copy-start(s32[8]{0:T(128)} %param.19) | copy-start | bytes 100
  9.1 54.0 %copy-start.13 = (s32[2,1]{0,1:T(1,128)S(1)}, s32[2,1]{0,1:T(1,128)}, u32[]{:S(2)}) copy-start(s32[2,1]{0,1:T(1,128)} %param.15) | copy-start | bytes 28
  9.1 54.0 %copy-start.14 = (s32[2,1]{0,1:T(1,128)S(1)}, s32[2,1]{0,1:T(1,128)}, u32[]{:S(2)}) copy-start(s32[2,1]{0,1:T(1,128)} %param.16) | copy-start | bytes 28
  9.1 54.7 %copy-start = (bf16[2048,256]{1,0:T(8,128)(2,1)S(1)}, bf16[2048,256]{1,0:T(8,128)(2,1)}, u32[]{:S(2)}) copy-start(bf16[2048,256]{1,0:T(8,128)(2,1)} %sk.3) | copy-start | bytes 3145732
  10.3 0.7 collective-permute-start
  26.2 44.8 %copy-start.12 = (bf16[1,1,8,64,256]{4,3,1,2,0:T(8,128)(2,1)}, bf16[1,1,8,64,256]{4,3,1,2,0:T(8,128)(2,1)S(1)}, u32[]{:S(2)}) copy-start(bf16[1,1,8,64,256]{4,3,1,2,0:T(8,128)(2,1)S(1)} %get-tuple-element.16) | copy-start | bytes 786436
  26.2 44.8 %copy-start.1 = (bf16[1,1,8,64,256]{4,3,1,2,0:T(8,128)(2,1)}, bf16[1,1,8,64,256]{4,3,1,2,0:T(8,128)(2,1)S(1)}, u32[]{:S(2)}) copy-start(bf16[1,1,8,64,256]{4,3,1,2,0:T(8,128)(2,1)S(1)} %get-tuple-element.17) | copy-start | bytes 786436
  26.2 33.0 %collective-permute-start.3 = (bf16[512,256]{1,0:T(8,128)(2,1)S(1)}, bf16[512,256]{1,0:T(8,128)(2,1)S(1)}, u32[]{:S(2)}, u32[]{:S(2)}) collective-permute-start(bf16[512,256]{1,0:T(8,128)(2,1)S(1)} %bitcast.22), channel_id=1, source_target_pairs={{0,96},{32,0},{64,32},{96,64},{1,97},{33,1},{65,33},{97,65},{2,98}... | collective-permute-start | bytes 786440 | tf_op jit(solution)/shard_map/ppermute | solution.py:402
  48.5 22.5 %collective-permute-start.2 = (bf16[512,256]{1,0:T(8,128)(2,1)S(1)}, bf16[512,256]{1,0:T(8,128)(2,1)S(1)}, u32[]{:S(2)}, u32[]{:S(2)}) collective-permute-start(bf16[512,256]{1,0:T(8,128)(2,1)S(1)} %bitcast.23), channel_id=1, source_target_pairs={{0,64},{32,96},{64,0},{96,32},{1,65},{33,97},{65,1},{97,33},{2,66}... | collective-permute-start | bytes 786440 | tf_op jit(solution)/shard_map/ppermute | solution.py:402
  49.0 22.0 %collective-permute-start.1 = (bf16[512,256]{1,0:T(8,128)(2,1)S(1)}, bf16[512,256]{1,0:T(8,128)(2,1)S(1)}, u32[]{:S(2)}, u32[]{:S(2)}) collective-permute-start(bf16[512,256]{1,0:T(8,128)(2,1)S(1)} %bitcast.24), channel_id=1, source_target_pairs={{0,32},{32,64},{64,96},{96,0},{1,33},{33,65},{65,97},{97,1},{2,34}... | collective-permute-start | bytes 786440 | tf_op jit(solution)/shard_map/ppermute | solution.py:402
  49.8 23.0 %collective-permute-start.6 = (bf16[512,256]{1,0:T(8,128)(2,1)S(1)}, bf16[512,256]{1,0:T(8,128)(2,1)S(1)}, u32[]{:S(2)}, u32[]{:S(2)}) collective-permute-start(bf16[512,256]{1,0:T(8,128)(2,1)S(1)} %bitcast.34), channel_id=1, source_target_pairs={{0,96},{32,0},{64,32},{96,64},{1,97},{33,1},{65,33},{97,65},{2,98}... | collective-permute-start | bytes 786440 | tf_op jit(solution)/shard_map/ppermute | solution.py:402
  51.7 21.1 %collective-permute-start.5 = (bf16[512,256]{1,0:T(8,128)(2,1)S(1)}, bf16[512,256]{1,0:T(8,128)(2,1)S(1)}, u32[]{:S(2)}, u32[]{:S(2)}) collective-permute-start(bf16[512,256]{1,0:T(8,128)(2,1)S(1)} %bitcast.35), channel_id=1, source_target_pairs={{0,64},{32,96},{64,0},{96,32},{1,65},{33,97},{65,1},{97,33},{2,66}... | collective-permute-start | bytes 786440 | tf_op jit(solution)/shard_map/ppermute | solution.py:402
  59.2 11.8 %copy-start.2 = (bf16[512,256]{1,0:T(8,128)(2,1)}, bf16[512,256]{1,0:T(8,128)(2,1)S(1)}, u32[]{:S(2)}) copy-start(bf16[512,256]{1,0:T(8,128)(2,1)S(1)} %collective-permute-done.3.up3) | copy-start | bytes 786436
  59.2 15.9 %collective-permute-start.4 = (bf16[512,256]{1,0:T(8,128)(2,1)S(1)}, bf16[512,256]{1,0:T(8,128)(2,1)S(1)}, u32[]{:S(2)}, u32[]{:S(2)}) collective-permute-start(bf16[512,256]{1,0:T(8,128)(2,1)S(1)} %bitcast.36), channel_id=1, source_target_pairs={{0,32},{32,64},{64,96},{96,0},{1,33},{33,65},{65,97},{97,1},{2,34}... | collective-permute-start | bytes 786440 | tf_op jit(solution)/shard_map/ppermute | solution.py:402
  63.8 7.2 %copy-start.6 = (s32[11]{0:T(128)}, s32[11]{0:T(128)S(1)}, u32[]{:S(2)}) copy-start(s32[11]{0:T(128)S(1)} %concatenate.3.ranks) | copy-start | bytes 136
  63.8 1.8 %copy-start.7 = (bf16[2,1,2048,256]{3,2,1,0:T(8,128)(2,1)S(1)}, bf16[2,1,2048,256]{3,2,1,0:T(8,128)(2,1)}, u32[]{:S(2)}) copy-start(bf16[2,1,2048,256]{3,2,1,0:T(8,128)(2,1)} %param.13) | copy-start | bytes 6291460
  65.7 1.8 %copy-start.8 = (bf16[2,1,2048,256]{3,2,1,0:T(8,128)(2,1)S(1)}, bf16[2,1,2048,256]{3,2,1,0:T(8,128)(2,1)}, u32[]{:S(2)}) copy-start(bf16[2,1,2048,256]{3,2,1,0:T(8,128)(2,1)} %param.14) | copy-start | bytes 6291460
  71.0 1.1 copy-start.9
  71.0 1.8 %copy-start.10 = (f32[2,256,256]{2,1,0:T(8,128)}, f32[2,256,256]{2,1,0:T(8,128)S(1)}, u32[]{:S(2)}) copy-start(f32[2,256,256]{2,1,0:T(8,128)S(1)} %get-tuple-element.9.half) | copy-start | bytes 1572868
  71.0 1.8 %copy-start.11 = (bf16[2,256,256]{2,1,0:T(8,128)(2,1)}, bf16[2,256,256]{2,1,0:T(8,128)(2,1)S(1)}, u32[]{:S(2)}) copy-start(bf16[2,256,256]{2,1,0:T(8,128)(2,1)S(1)} %get-tuple-element.7.probe) | copy-start | bytes 786436
  71.0 11.7 %copy-start.3 = (bf16[512,256]{1,0:T(8,128)(2,1)}, bf16[512,256]{1,0:T(8,128)(2,1)S(1)}, u32[]{:S(2)}) copy-start(bf16[512,256]{1,0:T(8,128)(2,1)S(1)} %collective-permute-done.2.up2) | copy-start | bytes 786436
  71.1 11.7 %copy-start.4 = (bf16[512,256]{1,0:T(8,128)(2,1)}, bf16[512,256]{1,0:T(8,128)(2,1)S(1)}, u32[]{:S(2)}) copy-start(bf16[512,256]{1,0:T(8,128)(2,1)S(1)} %collective-permute-done.1.up1) | copy-start | bytes 786436
  72.1 0.6 copy-start.5
  72.8 10.0 %copy-start.15 = (bf16[512,256]{1,0:T(8,128)(2,1)}, bf16[512,256]{1,0:T(8,128)(2,1)S(1)}, u32[]{:S(2)}) copy-start(bf16[512,256]{1,0:T(8,128)(2,1)S(1)} %collective-permute-done.6.vp3) | copy-start | bytes 786436
  72.8 9.9 %copy-start.16 = (bf16[512,256]{1,0:T(8,128)(2,1)}, bf16[512,256]{1,0:T(8,128)(2,1)S(1)}, u32[]{:S(2)}) copy-start(bf16[512,256]{1,0:T(8,128)(2,1)S(1)} %collective-permute-done.5.vp2) | copy-start | bytes 786436
  75.1 7.6 %copy-start.17 = (bf16[512,256]{1,0:T(8,128)(2,1)}, bf16[512,256]{1,0:T(8,128)(2,1)S(1)}, u32[]{:S(2)}) copy-start(bf16[512,256]{1,0:T(8,128)(2,1)S(1)} %collective-permute-done.4.vp1) | copy-start | bytes 786436
Sparse Core Ops, SparseCore 0:
  10.9 71.7 all-gather.1

commit v4 on v3

--- a/solution.py
+++ b/solution.py
@@ -13,14 +13,8 @@
 HALF = 128
 
 
-def dot(a, b, ca=1, cb=0, precision=None):
-    return lax.dot_general(
-        a, b, (((ca,), (cb,)), ((), ())), preferred_element_type=F32, precision=precision
-    )
-
-
-def exact(a, b, ca=1, cb=0):
-    return dot(a, b, ca, cb, lax.Precision.HIGHEST)
+def dot(a, b, ca=1, cb=0):
+    return lax.dot_general(a, b, (((ca,), (cb,)), ((), ())), preferred_element_type=F32)
 
 
 def pieces(x, count):
@@ -32,9 +26,19 @@
     return out
 
 
-def reciprocal(x):
-    r = pl.reciprocal(x, approx=True)
-    return r * (2.0 - x * r)
+def joined(a, b, pairs, ca=1, cb=0):
+    left = jnp.concatenate([a[i] for i, _ in pairs], axis=ca)
+    right = jnp.concatenate([b[j] for _, j in pairs], axis=cb)
+    return dot(left, right, ca, cb)
+
+
+ONE = ((0, 0), (1, 0), (2, 0))
+SIX = ((0, 0), (0, 1), (1, 0), (1, 1), (0, 2), (2, 0))
+
+
+def exact(a, b, ca=1, cb=0):
+    return joined(pieces(a, 3), pieces(b, 3), SIX, ca, cb)
+
 
 def tree(terms):
     while len(terms) > 1:
@@ -56,27 +60,28 @@
         panel = (lane >= 8 * g) & (lane < 8 * g + 8)
         for x in tiles:
             cols = [[column(x[i], 8 * g + j) for j in range(8)] for i in range(g, groups)]
-            top, own, kept = x[g], cols[0], x[g]
+            top, own, kept = x[g], list(cols[0]), x[g]
+            raw, fresh = list(own), top
             for m in range(0, 8, 2):
                 c0, c1 = own[m], own[m + 1]
-                a, b, c = spread(c0, m), spread(c1, m), spread(c1, m + 1)
-                inv = reciprocal(a * c - b * b)
-                ai, bi, ci = a * inv, b * inv, c * inv
+                a, b, c = spread(raw[m], m), spread(raw[m + 1], m), spread(raw[m + 1], m + 1)
+                inv = pl.reciprocal(a * c - b * b, approx=True)
                 upper, lower = sub == m, sub == m + 1
                 for j in range(m + 2, 8):
-                    s0, s1 = spread(own[j], m), spread(own[j], m + 1)
-                    g0, g1 = ci * s0 - bi * s1, ai * s1 - bi * s0
-                    own[j] = jnp.where(upper, g0, jnp.where(lower, g1, own[j] - (c0 * g0 + c1 * g1)))
+                    s0, s1 = spread(raw[j], m), spread(raw[j], m + 1)
+                    h0, h1 = c * s0 - b * s1, a * s1 - b * s0
+                    raw[j] = own[j] - inv * (c0 * h0 + c1 * h1)
+                    own[j] = jnp.where(upper, inv * h0, jnp.where(lower, inv * h1, raw[j]))
                 k = 8 * g + m
                 first, second = lane == k, lane == k + 1
                 if m:
-                    kept = jnp.where(upper | lower, top, kept)
-                r0, r1 = spread(top, m), spread(top, m + 1)
+                    kept = jnp.where(upper | lower, fresh, kept)
+                r0, r1 = spread(fresh, m), spread(fresh, m + 1)
                 r0 = jnp.where(first, 1.0, jnp.where(second, 0.0, r0))
                 r1 = jnp.where(second, 1.0, jnp.where(first, 0.0, r1))
-                q0, q1 = ci * r0 - bi * r1, ai * r1 - bi * r0
-                new = jnp.where(first | second, 0.0, top) - (c0 * q0 + c1 * q1)
-                top = jnp.where(upper, q0, jnp.where(lower, q1, new))
+                h0, h1 = c * r0 - b * r1, a * r1 - b * r0
+                fresh = jnp.where(first | second, 0.0, top) - inv * (c0 * h0 + c1 * h1)
+                top = jnp.where(upper, inv * h0, jnp.where(lower, inv * h1, fresh))
             x[g] = kept
             if g + 1 < groups:
                 solved = [spread(top, m) for m in range(8)]
@@ -105,16 +110,28 @@
 
 def inverse_factors(grams):
     h = HALF
-    m1 = eliminate([g[:h, :h] for g in grams])
-    u12 = [exact(m, g[:h, h:]) for m, g in zip(m1, grams)]
-    m2 = eliminate([g[h:, h:] - exact(u, u, 0, 0) for u, g in zip(u12, grams)])
+    n = 2 * h
+    diagonal = lax.broadcasted_iota(jnp.int32, (n, n), 0) == lax.broadcasted_iota(
+        jnp.int32, (n, n), 1
+    )
+    scales, scaled = [], []
+    for g in grams:
+        kept = jnp.where(diagonal, g, 0.0)
+        across = lax.rsqrt(jnp.sum(kept, axis=0, keepdims=True))
+        down = lax.rsqrt(jnp.sum(kept, axis=1, keepdims=True))
+        scales.append(across)
+        scaled.append((g * down) * across)
+    m1 = eliminate([g[:h, :h] for g in scaled])
+    u12 = [exact(m, g[:h, h:]) for m, g in zip(m1, scaled)]
+    m2 = eliminate([g[h:, h:] - exact(u, u, 0, 0) for u, g in zip(u12, scaled)])
     m21 = [-exact(b, exact(u, a, 0, 0)) for a, b, u in zip(m1, m2, u12)]
     zero = jnp.zeros((h, h), F32)
     return [
         jnp.concatenate(
             [jnp.concatenate([a, zero], axis=1), jnp.concatenate([c, b], axis=1)], axis=0
         )
-        for a, b, c in zip(m1, m2, m21)
+        * scale
+        for a, b, c, scale in zip(m1, m2, m21, scales)
     ]
 
 
@@ -222,6 +239,7 @@
     fresh_v,
     dinv,
     vall,
+    wall,
     ui,
     uj,
     tu,
@@ -234,6 +252,7 @@
     hv,
     gv,
     rv,
+    ps,
     load_sem,
     out_sem,
 ):
@@ -255,35 +274,47 @@
         chunks, rows = pl.ds(0, 2 * q + 2), pl.ds(part * q, part)
         return load(gathered.at[chunks, rows], dinv.at[chunks, rows])
 
-    need_v = [load(gathered.at[8 + t], vall.at[:, pl.ds(rmax * t, rmax)]) for t in range(2)]
-    for at, src in zip(spots(), (vp0, vp1, vp2, vp3)):
-        need_v.append(load(src, vall.at[pl.ds(at, part), pl.ds(2 * rmax, rmax)]))
-    need_d = [load_d(0), load_d(1)]
-    for copy in need_v:
+    def load_quarter(q):
+        rows = pl.ds(part * q, part)
+        copies = [
+            load(gathered.at[8 + t, rows], vall.at[rows, pl.ds(rmax * t, rmax)]) for t in range(2)
+        ]
+        chunks = pl.ds(0, 2 * q + 2)
+        return copies + [load(gathered.at[chunks, rows], dinv.at[chunks, rows])]
+
+    need_vj = [
+        load(a, vall.at[pl.ds(at, part), pl.ds(2 * rmax, rmax)])
+        for at, a in zip(spots(), (vp0, vp1, vp2, vp3))
+    ]
+    need = [load_quarter(0), load_quarter(1)]
+    need_u = [load(gathered.at[10 + t], ui.at[t]) for t in range(2)]
+    need_u.append(load(trail_u, tu))
+    need += [load_quarter(2), load_quarter(3)]
+    need_smalls = [load(a, b) for a, b in zip((probe, upper, half, reach), smalls)]
+    rest = [load(a, uj.at[pl.ds(at, part)]) for at, a in zip(spots(), (up0, up1, up2, up3))]
+    rest.append(load(trail_v, tv))
+    for copy in need_vj:
         copy.wait()
-    need_d += [load_d(2), load_d(3)]
-    coupling = [jnp.zeros((rmax, rmax), F32)] * 2
     for q in range(4):
-        need_d[q].wait()
-        if q == 1:
-            need_u = [load(gathered.at[10 + t], ui.at[t]) for t in range(2)]
-            need_u.append(load(trail_u, tu))
-            need_u += [load(a, b) for a, b in zip((probe, upper, half, reach), smalls)]
-        if q == 2:
-            rest = [load(a, uj.at[pl.ds(at, part)]) for at, a in zip(spots(), (up0, up1, up2, up3))]
-            rest.append(load(trail_v, tv))
+        for copy in need[q]:
+            copy.wait()
         for n in range(2):
             at = part * q + rmax * n
             count = 2 * q + 1 + n
             lhs = jnp.concatenate([dinv[c, at : at + rmax] for c in range(count)], axis=1)
-            w = dot(lhs, vall[: rmax * count]).astype(BF16)
-            wj = w[:, 2 * rmax :]
-            coupling = [
-                coupling[t] + dot(w[:, rmax * t : rmax * (t + 1)], wj, 0, 0) for t in range(2)
-            ]
-    for copy in need_u:
+            wall[at : at + rmax] = dot(lhs, vall[: rmax * count]).astype(BF16)
+        if q == 1:
+            for copy in need_u:
+                copy.wait()
+            for t in range(2):
+                sides = jnp.concatenate([tu[t], ui[t]], axis=1)
+                ps[t] = dot(ui[t], sides, 0, 0)
+    for copy in need_smalls:
         copy.wait()
     probe, upper, half, reach = smalls
+    parts = [(pieces(ps[t, :, :rmax], 3), pieces(ps[t, :, rmax:], 3)) for t in range(2)]
+    crosses = [joined(parts[t][0], [probe[t]], ONE) for t in range(2)]
+    coupling = dot(wall[:, : 2 * rmax], wall[:, 2 * rmax :], 0, 0)
 
     row = lax.broadcasted_iota(jnp.int32, (rmax, rmax), 0)
     col = lax.broadcasted_iota(jnp.int32, (rmax, rmax), 1)
@@ -292,25 +323,24 @@
         new_rank, row_rank, col_rank = ranks[2 + t], ranks[4 + t], ranks[6]
         keep = col < new_rank
         top = probe[t]
-        c = jnp.where((row < row_rank) & (col < col_rank), coupling[t], 0.0).astype(BF16)
+        c = coupling[rmax * t : rmax * (t + 1)]
+        c = jnp.where((row < row_rank) & (col < col_rank), c, 0.0).astype(BF16)
         bottom = jnp.where(keep, -dot(c, reach[...]), 0.0).astype(BF16)
-        gur = pieces(dot(tu[t], ui[t], 0, 0), 3)
-        grr = pieces(dot(ui[t], ui[t], 0, 0), 3)
-        cross = sum(dot(piece, top, 0, 0) for piece in gur)
-        own = sum(dot(piece, bottom) for piece in grr)
+        gru, grr = parts[t]
+        cross = crosses[t]
+        own = joined(grr, [bottom], ONE)
         mixed = pieces(cross + 0.5 * own, 3)
-        gram = half[t] + sum(dot(bottom, piece, 0, 0) for piece in mixed)
+        gram = half[t] + joined([bottom], mixed, ((0, 0), (0, 1), (0, 2)), 0, 0)
         grams.append(gram + gram.T + jnp.where((row == col) & ~keep, 1.0, 0.0))
         couplings.append(c)
         probes.append(jnp.concatenate([top, bottom], axis=0))
-        above = upper[t] + sum(dot(piece, bottom) for piece in gur[:2])
+        above = upper[t] + joined(gru, [bottom], ONE[:2], 0, 0)
         products.append(pieces(jnp.concatenate([above, cross + own], axis=0), 2))
     inverses = inverse_factors(grams)
     for t in range(2):
         m = pieces(inverses[t] * math.sqrt(width), 2)
-        zs[t] = (dot(probes[t], m[0], 1, 1) + dot(probes[t], m[1], 1, 1)).astype(BF16)
-        g = products[t]
-        back = dot(g[0], m[0], 1, 1) + (dot(g[0], m[1], 1, 1) + dot(g[1], m[0], 1, 1))
+        zs[t] = joined([probes[t]], m, ((0, 0), (0, 1)), 1, 1).astype(BF16)
+        back = joined(products[t], m, ((0, 0), (0, 1), (1, 0)), 1, 1)
         top = jnp.where(row < ranks[t], back[:rmax], 0.0)
         bottom = -dot(couplings[t], back[rmax:].astype(BF16), 0, 0)
         bs[t] = (jnp.concatenate([top, bottom], axis=0) / width).astype(BF16)
@@ -348,6 +378,7 @@
         scratch_shapes=[
             pltpu.VMEM((8, width, rmax), BF16),
             pltpu.VMEM((width, 3 * rmax), BF16),
+            pltpu.VMEM((width, 3 * rmax), BF16),
             pltpu.VMEM((2, width, rmax), BF16),
             pltpu.VMEM((width, rmax), BF16),
             pltpu.VMEM((2, width, rmax), BF16),
@@ -360,7 +391,8 @@
             pltpu.VMEM((2, rmax, rmax), F32),
             pltpu.VMEM((2, rmax, rmax), F32),
             pltpu.VMEM((rmax, rmax), BF16),
-            pltpu.SemaphoreType.DMA((22,)),
+            pltpu.VMEM((2, rmax, 2 * rmax), F32),
+            pltpu.SemaphoreType.DMA((28,)),
             pltpu.SemaphoreType.DMA((16,)),
         ],
         compiler_params=pltpu.CompilerParams(vmem_limit_bytes=56 * 1024 * 1024),

time: 117 us -> 113 us (0.966)
  Pallas kernels: 33.5 us -> 29.6 us
    pallas_call x1, Pallas kernels: 27.1 us -> 23.2 us  [tail(): pl.pallas_call(tail_kernel, name='tail', out_shape=(tile, tile), in_specs...]
where the time goes in v4:
time: 113 us
  Pallas kernels  29.6 us (26%)
  starting transfers between devices  27.5 us (24%)
  between operations  16.9 us (15%)
  waiting for transfers between devices  16.2 us (14%)
  blocking collectives  15.1 us (13%)
  local copies, waits for them, and re-layouts  6.34 us (6%)
  other arithmetic  1.17 us (1%)
    ppermute x6, starting transfers between devices, spread(): lax.ppermute(block, 'x', [(a, (a + k) % 4) for a in range(4)])  26.8 us
    pallas_call x1, Pallas kernels, tail(): pl.pallas_call(tail_kernel, name='tail', out_shape=(tile, tile), in_specs...  23.2 us
    all_to_all x1, blocking collectives, on_device(): lax.all_to_all(quarter, ('y', 'c'), split_axis=0, concat_axis=2, tiled=True)  15.1 us
    ppermute x6, waiting for transfers between devices, spread(): lax.ppermute(block, 'x', [(a, (a + k) % 4) for a in range(4)])  8.58 us
    all_gather x1, waiting for transfers between devices, on_device(): lax.all_gather(pack(diag_inv, row_v, row_u), ('z', 'y', 'c'), axis=1, til...  7.58 us
    unnamed x42, local copies, waits for them, and re-layouts  4.32 us
    pallas_call x1, Pallas kernels, prepare(): pl.pallas_call(prepare_kernel, name='prepare', grid=(2,), out_shape=(squa...  3.5 us
  transfers between devices with their start and end apart: 8, of which 3 were waited for; matrix products, arithmetic and copies ran while one was open for 3% of the time, Pallas kernels for 4%

profile of v4, /device:TPU:1, one launch (start us, length us, event | category | flops | bytes accessed | tf_op | source)
XLA Modules:
  0.0 112.8 jit_solution(7307662170863305923)
XLA Ops:
  7.2 0.0 copy-start.20
  7.2 0.0 all-gather.2.cloned.1.call-start
  7.2 1.9 %pack.1 = bf16[12,64,256]{2,1,0:T(8,128)(2,1)} custom-call(f32[64,2048]{1,0:T(8,128)} %diag.1, bf16[2,64,256]{2,1,0:T(8,128)(2,1)} %row_v.1, bf16[2,64,256]{2,1,0:T(8,128)(2,1)} %row_u.1), custom_call_target="tpu_custom_call" | custom-call | bytes 1100000 | tf_op jit(solution)/shard_map/pack/pallas_call | solution.py:150
  9.1 0.0 copy-start
  9.1 0.0 all-gather.2.cloned.1.call-update
  9.1 1.2 %pad_maximum_fusion = bf16[8,2,64,256]{3,2,1,0:T(8,128)(2,1)S(1)} fusion(bf16[8,1,64,256]{3,2,1,0:T(8,128)(2,1)} %bitcast.32, bf16[8,1,64,256]{3,2,1,0:T(8,128)(2,1)} %bitcast.33), kind=kLoop, calls=%fused_computation | loop fusion | flops 262144 | bytes 1048576 | tf_op jit(solution)/shard_map/stack | solution.py:429
  10.3 0.7 collective-permute-start
  11.0 0.0 collective-permute-done
  11.0 15.1 %all_to_all.15 = bf16[8,2,64,256]{3,2,1,0:T(8,128)(2,1)S(1)} all-to-all(bf16[8,2,64,256]{3,2,1,0:T(8,128)(2,1)S(1)} %collective-permute-done), channel_id=1, replica_groups=mesh['x'=4,'z'=4,'y'=4,'c'=2] {'y','c'}, dimensions={0} | all-to-all | bytes 1048576 | tf_op jit(solution)/shard_map/all_to_all | solution.py:430
  26.2 22.3 %collective-permute-start.3 = (bf16[512,256]{1,0:T(8,128)(2,1)S(1)}, bf16[512,256]{1,0:T(8,128)(2,1)S(1)}, u32[]{:S(2)}, u32[]{:S(2)}) collective-permute-start(bf16[512,256]{1,0:T(8,128)(2,1)S(1)} %bitcast.22), channel_id=1, source_target_pairs={{0,96},{32,0},{64,32},{96,64},{1,97},{33,1},{65,33},{97,65},{2,98}... | collective-permute-start | bytes 786440 | tf_op jit(solution)/shard_map/ppermute | solution.py:434
  48.5 0.4 collective-permute-start.2
  49.0 0.8 collective-permute-start.1
  49.8 1.9 %collective-permute-start.6 = (bf16[512,256]{1,0:T(8,128)(2,1)S(1)}, bf16[512,256]{1,0:T(8,128)(2,1)S(1)}, u32[]{:S(2)}, u32[]{:S(2)}) collective-permute-start(bf16[512,256]{1,0:T(8,128)(2,1)S(1)} %bitcast.34), channel_id=1, source_target_pairs={{0,96},{32,0},{64,32},{96,64},{1,97},{33,1},{65,33},{97,65},{2,98}... | collective-permute-start | bytes 786440 | tf_op jit(solution)/shard_map/ppermute | solution.py:434
  51.7 1.3 %collective-permute-start.5 = (bf16[512,256]{1,0:T(8,128)(2,1)S(1)}, bf16[512,256]{1,0:T(8,128)(2,1)S(1)}, u32[]{:S(2)}, u32[]{:S(2)}) collective-permute-start(bf16[512,256]{1,0:T(8,128)(2,1)S(1)} %bitcast.35), channel_id=1, source_target_pairs={{0,64},{32,96},{64,0},{96,32},{1,65},{33,97},{65,1},{97,33},{2,66}... | collective-permute-start | bytes 786440 | tf_op jit(solution)/shard_map/ppermute | solution.py:434
  53.0 6.2 %collective-permute-done.3.up3 = bf16[512,256]{1,0:T(8,128)(2,1)S(1)} collective-permute-done((bf16[512,256]{1,0:T(8,128)(2,1)S(1)}, bf16[512,256]{1,0:T(8,128)(2,1)S(1)}, u32[]{:S(2)}, u32[]{:S(2)}) %collective-permute-start.3) | collective-permute-done | bytes 262176 | tf_op jit(solution)/shard_map/ppermute | solution.py:434
  59.2 0.0 collective-permute-start.4
  59.2 0.6 dynamic_slice.11
  62.4 0.6 dynamic_slice.10
  63.0 0.1 dynamic_slice.9
  63.1 0.7 concatenate.3.ranks
  63.8 0.0 copy-start.7
  63.8 1.8 %copy-done.7 = bf16[2,1,2048,256]{3,2,1,0:T(8,128)(2,1)S(1)} copy-done((bf16[2,1,2048,256]{3,2,1,0:T(8,128)(2,1)S(1)}, bf16[2,1,2048,256]{3,2,1,0:T(8,128)(2,1)}, u32[]{:S(2)}) %copy-start.7) | copy-done | bytes 2097176
  65.7 1.8 %copy-done.8 = bf16[2,1,2048,256]{3,2,1,0:T(8,128)(2,1)S(1)} copy-done((bf16[2,1,2048,256]{3,2,1,0:T(8,128)(2,1)S(1)}, bf16[2,1,2048,256]{3,2,1,0:T(8,128)(2,1)}, u32[]{:S(2)}) %copy-start.8) | copy-done | bytes 2097176
  67.4 3.5 %prepare.1 = (bf16[2,256,256]{2,1,0:T(8,128)(2,1)S(1)}, f32[2,256,256]{2,1,0:T(8,128)S(1)}, f32[2,256,256]{2,1,0:T(8,128)S(1)}) custom-call(s32[11]{0:T(128)S(1)} %concatenate.3.ranks, bf16[2,2048,256]{2,1,0:T(8,128)(2,1)S(1)} %bitcast.28, bf16[2,2048,256]{2,1,0:T(8,128)(2,1)S(1)} %bitcast.30, bf16[2048,256]{1,0:T(8,128)(2,1)S(1)} %copy-done), custom_call_target="tpu_custom_call" | custom-call | flops 2000000000 | bytes 6000000 | tf_op jit(solution)/shard_map/prepare/pallas_call | solution.py:176
  71.0 0.0 collective-permute-done.2.up2
  71.0 0.0 collective-permute-done.1.up1
  71.1 1.0 reach.1
  72.1 0.6 copy-done.5
  72.8 0.0 collective-permute-done.6.vp3
  72.8 2.3 %collective-permute-done.4.vp1 = bf16[512,256]{1,0:T(8,128)(2,1)S(1)} collective-permute-done((bf16[512,256]{1,0:T(8,128)(2,1)S(1)}, bf16[512,256]{1,0:T(8,128)(2,1)S(1)}, u32[]{:S(2)}, u32[]{:S(2)}) %collective-permute-start.4) | collective-permute-done | bytes 262176 | tf_op jit(solution)/shard_map/ppermute | solution.py:434
  75.1 7.6 %all-gather.2.cloned.1.call-done.gathered = bf16[12,2048,256]{2,1,0:T(8,128)(2,1)} async-done(((bf16[12,64,256]{2,1,0:T(8,128)(2,1)}), bf16[12,2048,256]{2,1,0:T(8,128)(2,1)}) %all-gather.2.cloned.1.call-update) | async-done | bytes 12582928 | tf_op jit(solution)/shard_map/all_gather | solution.py:425
  82.7 23.2 %tail.1 = (bf16[2,2048,256]{2,1,0:T(8,128)(2,1)}, bf16[2,2048,256]{2,1,0:T(8,128)(2,1)}) custom-call(s32[11]{0:T(128)} %copy-done.6, bf16[2,256,256]{2,1,0:T(8,128)(2,1)} %copy-done.11, f32[2,256,256]{2,1,0:T(8,128)} %copy-done.9, f32[2,256,256]{2,1,0:T(8,128)} %copy-done.10, bf16[256,256]{1,0:T(8,128)(2,1)} %copy-done.5, ...), custom_call_target="tpu_custom_call" | custom-call | flops 16000000000 | bytes 20000000 | tf_op jit(solution)/shard_map/tail/pallas_call | solution.py:372
  (38 shorter events, 0.1 us)
Async XLA Ops:
  7.2 52.1 %copy-start.20 = (s32[4]{0:T(128)S(1)}, s32[4]{0:T(128)}, u32[]{:S(2)}) copy-start(s32[4]{0:T(128)} %constant.45.clone) | copy-start | bytes 52
  7.2 75.5 %all-gather.2.cloned.1.call-start = ((), (), s32[]{:S(2)}) async-start(), calls=%async_computation.1 | async-start | bytes 12976128 | tf_op jit(solution)/shard_map/all_gather | solution.py:425
  9.1 53.3 %copy-start.18 = (s32[32]{0:T(128)S(1)}, s32[32]{0:T(128)}, u32[]{:S(2)}) copy-start(s32[32]{0:T(128)} %param.22) | copy-start | bytes 388
  9.1 53.9 %copy-start.19 = (s32[8]{0:T(128)S(1)}, s32[8]{0:T(128)}, u32[]{:S(2)}) copy-start(s32[8]{0:T(128)} %param.19) | copy-start | bytes 100
  9.1 54.0 %copy-start.13 = (s32[2,1]{0,1:T(1,128)S(1)}, s32[2,1]{0,1:T(1,128)}, u32[]{:S(2)}) copy-start(s32[2,1]{0,1:T(1,128)} %param.15) | copy-start | bytes 28
  9.1 54.0 %copy-start.14 = (s32[2,1]{0,1:T(1,128)S(1)}, s32[2,1]{0,1:T(1,128)}, u32[]{:S(2)}) copy-start(s32[2,1]{0,1:T(1,128)} %param.16) | copy-start | bytes 28
  9.1 54.7 %copy-start = (bf16[2048,256]{1,0:T(8,128)(2,1)S(1)}, bf16[2048,256]{1,0:T(8,128)(2,1)}, u32[]{:S(2)}) copy-start(bf16[2048,256]{1,0:T(8,128)(2,1)} %sk.3) | copy-start | bytes 3145732
  10.3 0.7 collective-permute-start
  26.2 44.8 %copy-start.12 = (bf16[1,1,8,64,256]{4,3,1,2,0:T(8,128)(2,1)}, bf16[1,1,8,64,256]{4,3,1,2,0:T(8,128)(2,1)S(1)}, u32[]{:S(2)}) copy-start(bf16[1,1,8,64,256]{4,3,1,2,0:T(8,128)(2,1)S(1)} %get-tuple-element.16) | copy-start | bytes 786436
  26.2 44.8 %copy-start.1 = (bf16[1,1,8,64,256]{4,3,1,2,0:T(8,128)(2,1)}, bf16[1,1,8,64,256]{4,3,1,2,0:T(8,128)(2,1)S(1)}, u32[]{:S(2)}) copy-start(bf16[1,1,8,64,256]{4,3,1,2,0:T(8,128)(2,1)S(1)} %get-tuple-element.17) | copy-start | bytes 786436
  26.2 33.0 %collective-permute-start.3 = (bf16[512,256]{1,0:T(8,128)(2,1)S(1)}, bf16[512,256]{1,0:T(8,128)(2,1)S(1)}, u32[]{:S(2)}, u32[]{:S(2)}) collective-permute-start(bf16[512,256]{1,0:T(8,128)(2,1)S(1)} %bitcast.22), channel_id=1, source_target_pairs={{0,96},{32,0},{64,32},{96,64},{1,97},{33,1},{65,33},{97,65},{2,98}... | collective-permute-start | bytes 786440 | tf_op jit(solution)/shard_map/ppermute | solution.py:434
  48.5 22.5 %collective-permute-start.2 = (bf16[512,256]{1,0:T(8,128)(2,1)S(1)}, bf16[512,256]{1,0:T(8,128)(2,1)S(1)}, u32[]{:S(2)}, u32[]{:S(2)}) collective-permute-start(bf16[512,256]{1,0:T(8,128)(2,1)S(1)} %bitcast.23), channel_id=1, source_target_pairs={{0,64},{32,96},{64,0},{96,32},{1,65},{33,97},{65,1},{97,33},{2,66}... | collective-permute-start | bytes 786440 | tf_op jit(solution)/shard_map/ppermute | solution.py:434
  49.0 22.0 %collective-permute-start.1 = (bf16[512,256]{1,0:T(8,128)(2,1)S(1)}, bf16[512,256]{1,0:T(8,128)(2,1)S(1)}, u32[]{:S(2)}, u32[]{:S(2)}) collective-permute-start(bf16[512,256]{1,0:T(8,128)(2,1)S(1)} %bitcast.24), channel_id=1, source_target_pairs={{0,32},{32,64},{64,96},{96,0},{1,33},{33,65},{65,97},{97,1},{2,34}... | collective-permute-start | bytes 786440 | tf_op jit(solution)/shard_map/ppermute | solution.py:434
  49.8 23.0 %collective-permute-start.6 = (bf16[512,256]{1,0:T(8,128)(2,1)S(1)}, bf16[512,256]{1,0:T(8,128)(2,1)S(1)}, u32[]{:S(2)}, u32[]{:S(2)}) collective-permute-start(bf16[512,256]{1,0:T(8,128)(2,1)S(1)} %bitcast.34), channel_id=1, source_target_pairs={{0,96},{32,0},{64,32},{96,64},{1,97},{33,1},{65,33},{97,65},{2,98}... | collective-permute-start | bytes 786440 | tf_op jit(solution)/shard_map/ppermute | solution.py:434
  51.7 21.1 %collective-permute-start.5 = (bf16[512,256]{1,0:T(8,128)(2,1)S(1)}, bf16[512,256]{1,0:T(8,128)(2,1)S(1)}, u32[]{:S(2)}, u32[]{:S(2)}) collective-permute-start(bf16[512,256]{1,0:T(8,128)(2,1)S(1)} %bitcast.35), channel_id=1, source_target_pairs={{0,64},{32,96},{64,0},{96,32},{1,65},{33,97},{65,1},{97,33},{2,66}... | collective-permute-start | bytes 786440 | tf_op jit(solution)/shard_map/ppermute | solution.py:434
  59.2 11.8 %copy-start.2 = (bf16[512,256]{1,0:T(8,128)(2,1)}, bf16[512,256]{1,0:T(8,128)(2,1)S(1)}, u32[]{:S(2)}) copy-start(bf16[512,256]{1,0:T(8,128)(2,1)S(1)} %collective-permute-done.3.up3) | copy-start | bytes 786436
  59.2 15.9 %collective-permute-start.4 = (bf16[512,256]{1,0:T(8,128)(2,1)S(1)}, bf16[512,256]{1,0:T(8,128)(2,1)S(1)}, u32[]{:S(2)}, u32[]{:S(2)}) collective-permute-start(bf16[512,256]{1,0:T(8,128)(2,1)S(1)} %bitcast.36), channel_id=1, source_target_pairs={{0,32},{32,64},{64,96},{96,0},{1,33},{33,65},{65,97},{97,1},{2,34}... | collective-permute-start | bytes 786440 | tf_op jit(solution)/shard_map/ppermute | solution.py:434
  63.8 7.2 %copy-start.6 = (s32[11]{0:T(128)}, s32[11]{0:T(128)S(1)}, u32[]{:S(2)}) copy-start(s32[11]{0:T(128)S(1)} %concatenate.3.ranks) | copy-start | bytes 136
  63.8 1.8 %copy-start.7 = (bf16[2,1,2048,256]{3,2,1,0:T(8,128)(2,1)S(1)}, bf16[2,1,2048,256]{3,2,1,0:T(8,128)(2,1)}, u32[]{:S(2)}) copy-start(bf16[2,1,2048,256]{3,2,1,0:T(8,128)(2,1)} %param.13) | copy-start | bytes 6291460
  65.7 1.8 %copy-start.8 = (bf16[2,1,2048,256]{3,2,1,0:T(8,128)(2,1)S(1)}, bf16[2,1,2048,256]{3,2,1,0:T(8,128)(2,1)}, u32[]{:S(2)}) copy-start(bf16[2,1,2048,256]{3,2,1,0:T(8,128)(2,1)} %param.14) | copy-start | bytes 6291460
  71.0 1.1 %copy-start.9 = (f32[2,256,256]{2,1,0:T(8,128)}, f32[2,256,256]{2,1,0:T(8,128)S(1)}, u32[]{:S(2)}) copy-start(f32[2,256,256]{2,1,0:T(8,128)S(1)} %get-tuple-element.8.upper) | copy-start | bytes 1572868
  71.0 1.8 %copy-start.10 = (f32[2,256,256]{2,1,0:T(8,128)}, f32[2,256,256]{2,1,0:T(8,128)S(1)}, u32[]{:S(2)}) copy-start(f32[2,256,256]{2,1,0:T(8,128)S(1)} %get-tuple-element.9.half) | copy-start | bytes 1572868
  71.0 1.8 %copy-start.11 = (bf16[2,256,256]{2,1,0:T(8,128)(2,1)}, bf16[2,256,256]{2,1,0:T(8,128)(2,1)S(1)}, u32[]{:S(2)}) copy-start(bf16[2,256,256]{2,1,0:T(8,128)(2,1)S(1)} %get-tuple-element.7.probe) | copy-start | bytes 786436
  71.0 11.7 %copy-start.3 = (bf16[512,256]{1,0:T(8,128)(2,1)}, bf16[512,256]{1,0:T(8,128)(2,1)S(1)}, u32[]{:S(2)}) copy-start(bf16[512,256]{1,0:T(8,128)(2,1)S(1)} %collective-permute-done.2.up2) | copy-start | bytes 786436
  71.1 11.7 %copy-start.4 = (bf16[512,256]{1,0:T(8,128)(2,1)}, bf16[512,256]{1,0:T(8,128)(2,1)S(1)}, u32[]{:S(2)}) copy-start(bf16[512,256]{1,0:T(8,128)(2,1)S(1)} %collective-permute-done.1.up1) | copy-start | bytes 786436
  72.1 0.6 copy-start.5
  72.8 10.0 %copy-start.15 = (bf16[512,256]{1,0:T(8,128)(2,1)}, bf16[512,256]{1,0:T(8,128)(2,1)S(1)}, u32[]{:S(2)}) copy-start(bf16[512,256]{1,0:T(8,128)(2,1)S(1)} %collective-permute-done.6.vp3) | copy-start | bytes 786436
  72.8 9.9 %copy-start.16 = (bf16[512,256]{1,0:T(8,128)(2,1)}, bf16[512,256]{1,0:T(8,128)(2,1)S(1)}, u32[]{:S(2)}) copy-start(bf16[512,256]{1,0:T(8,128)(2,1)S(1)} %collective-permute-done.5.vp2) | copy-start | bytes 786436
  75.1 7.6 %copy-start.17 = (bf16[512,256]{1,0:T(8,128)(2,1)}, bf16[512,256]{1,0:T(8,128)(2,1)S(1)}, u32[]{:S(2)}) copy-start(bf16[512,256]{1,0:T(8,128)(2,1)S(1)} %collective-permute-done.4.vp1) | copy-start | bytes 786436
Sparse Core Ops, SparseCore 0:
  10.9 71.7 all-gather.1

commit v5 on v4

--- a/solution.py
+++ b/solution.py
@@ -279,8 +279,10 @@
         copies = [
             load(gathered.at[8 + t, rows], vall.at[rows, pl.ds(rmax * t, rmax)]) for t in range(2)
         ]
-        chunks = pl.ds(0, 2 * q + 2)
-        return copies + [load(gathered.at[chunks, rows], dinv.at[chunks, rows])]
+        for n in range(2):
+            chunks, block = pl.ds(0, 2 * q + 1 + n), pl.ds(part * q + rmax * n, rmax)
+            copies.append(load(gathered.at[chunks, block], dinv.at[chunks, block]))
+        return copies
 
     need_vj = [
         load(a, vall.at[pl.ds(at, part), pl.ds(2 * rmax, rmax)])
@@ -290,14 +292,16 @@
     need_u = [load(gathered.at[10 + t], ui.at[t]) for t in range(2)]
     need_u.append(load(trail_u, tu))
     need += [load_quarter(2), load_quarter(3)]
-    need_smalls = [load(a, b) for a, b in zip((probe, upper, half, reach), smalls)]
-    rest = [load(a, uj.at[pl.ds(at, part)]) for at, a in zip(spots(), (up0, up1, up2, up3))]
-    rest.append(load(trail_v, tv))
     for copy in need_vj:
         copy.wait()
     for q in range(4):
         for copy in need[q]:
             copy.wait()
+        if q == 1:
+            need_smalls = [load(a, b) for a, b in zip((probe, upper, half, reach), smalls)]
+        if q == 2:
+            rest = [load(a, uj.at[pl.ds(at, part)]) for at, a in zip(spots(), (up0, up1, up2, up3))]
+            rest.append(load(trail_v, tv))
         for n in range(2):
             at = part * q + rmax * n
             count = 2 * q + 1 + n
@@ -392,7 +396,7 @@
             pltpu.VMEM((2, rmax, rmax), F32),
             pltpu.VMEM((rmax, rmax), BF16),
             pltpu.VMEM((2, rmax, 2 * rmax), F32),
-            pltpu.SemaphoreType.DMA((28,)),
+            pltpu.SemaphoreType.DMA((32,)),
             pltpu.SemaphoreType.DMA((16,)),
         ],
         compiler_params=pltpu.CompilerParams(vmem_limit_bytes=56 * 1024 * 1024),
@@ -427,24 +431,25 @@
     times = (0, 2, 3, 1)
     swap = [(a * 4 + q, (times[a] ^ q) * 4 + a) for a in range(4) for q in range(4)]
     quarter = lax.ppermute(jnp.stack([col_v, col_u], axis=1), ("x", "z"), swap)
-    quarter = lax.all_to_all(quarter, ("y", "c"), split_axis=0, concat_axis=2, tiled=True)[0]
-
-    def spread(block):
-        return [block] + [
-            lax.ppermute(block, "x", [(a, (a + k) % 4) for a in range(4)]) for k in (1, 3, 2)
-        ]
-
-    vparts = spread(quarter[0])
-    uparts = spread(quarter[1])
-    vparts = [vparts[0], vparts[1], vparts[3], vparts[2]]
-    uparts = [uparts[0], uparts[1], uparts[3], uparts[2]]
-
     own_row = lax.dynamic_slice_in_dim(row_rank, x * trow, trow)
     own_col = lax.dynamic_slice_in_dim(col_rank, pcol, 1)
     turn = jnp.array(times, jnp.int32)[z]
     quarters = [(turn ^ lax.rem(x + 4 - k, 4))[None] for k in range(4)]
     ranks = jnp.concatenate([tile_rank[:, 0], new_rank[:, 0], own_row, own_col] + quarters)
     probe, upper, half = prepare(ranks, trail_u, trail_v, sketch)
+    quarter, probe, upper, half = lax.optimization_barrier((quarter, probe, upper, half))
+    quarter = lax.all_to_all(quarter, ("y", "c"), split_axis=0, concat_axis=2, tiled=True)[0]
+
+    def spread(block):
+        return [block] + [
+            lax.ppermute(block, "x", [(a, (a + k) % 4) for a in range(4)]) for k in (1, 3, 2)
+        ]
+
+    vparts = spread(quarter[0])
+    uparts = spread(quarter[1])
+    vparts = [vparts[0], vparts[1], vparts[3], vparts[2]]
+    uparts = [uparts[0], uparts[1], uparts[3], uparts[2]]
+
     reach = reach_of(ranks, sketch, uparts)
     fresh_u, fresh_v = tail(
         ranks, probe, upper, half, reach, gathered, vparts, uparts, trail_u, trail_v

time: 113 us -> 113 us (level)
  starting transfers between devices: 27.5 us -> 15.7 us
  waiting for transfers between devices: 16.2 us -> 27.9 us
    ppermute x6, waiting for transfers between devices: 8.58 us -> 20.4 us  [spread(): lax.ppermute(block, 'x', [(a, (a + k) % 4) for a in range(4)])]
    ppermute x6, starting transfers between devices: 26.8 us -> 15 us  [spread(): lax.ppermute(block, 'x', [(a, (a + k) % 4) for a in range(4)])]
  transfers between devices with their start and end apart: 8 -> 8, of which waited for: 3 -> 5; matrix products, arithmetic and copies ran while one was open for 3% -> 3% of each run, Pallas kernels for 4% -> 4%
where the time goes in v5:
time: 113 us
  Pallas kernels  29.4 us (26%)
  waiting for transfers between devices  27.9 us (25%)
  between operations  16.9 us (15%)
  blocking collectives  15.8 us (14%)
  starting transfers between devices  15.7 us (14%)
  local copies, waits for them, and re-layouts  5.91 us (5%)
    pallas_call x1, Pallas kernels, tail(): pl.pallas_call(tail_kernel, name='tail', out_shape=(tile, tile), in_specs...  23.2 us
    ppermute x6, waiting for transfers between devices, spread(): lax.ppermute(block, 'x', [(a, (a + k) % 4) for a in range(4)])  20.4 us
    all_to_all x1, blocking collectives, on_device(): lax.all_to_all(quarter, ('y', 'c'), split_axis=0, concat_axis=2, tiled=True)  15.8 us
    ppermute x6, starting transfers between devices, spread(): lax.ppermute(block, 'x', [(a, (a + k) % 4) for a in range(4)])  15 us
    all_gather x1, waiting for transfers between devices, on_device(): lax.all_gather(pack(diag_inv, row_v, row_u), ('z', 'y', 'c'), axis=1, til...  7.47 us
    unnamed x42, local copies, waits for them, and re-layouts  3.89 us
    pallas_call x1, Pallas kernels, prepare(): pl.pallas_call(prepare_kernel, name='prepare', grid=(2,), out_shape=(squa...  3.32 us
  transfers between devices with their start and end apart: 8, of which 5 were waited for; matrix products, arithmetic and copies ran while one was open for 3% of the time, Pallas kernels for 4%

profile of v5, /device:TPU:1, one launch (start us, length us, event | category | flops | bytes accessed | tf_op | source)
XLA Modules:
  0.0 112.7 jit_solution(15882152678762347020)
XLA Ops:
  7.2 0.0 copy-start.20
  7.2 0.0 all-gather.2.cloned.1.call-start
  7.3 1.9 %pack.1 = bf16[12,64,256]{2,1,0:T(8,128)(2,1)} custom-call(f32[64,2048]{1,0:T(8,128)} %diag.1, bf16[2,64,256]{2,1,0:T(8,128)(2,1)} %row_v.1, bf16[2,64,256]{2,1,0:T(8,128)(2,1)} %row_u.1), custom_call_target="tpu_custom_call" | custom-call | bytes 1100000 | tf_op jit(solution)/shard_map/pack/pallas_call | solution.py:150
  9.2 0.0 all-gather.2.cloned.1.call-update
  9.2 1.1 pad_maximum_fusion
  10.3 0.7 collective-permute-start
  11.1 0.6 dynamic_slice.11
  14.2 0.6 dynamic_slice.10
  14.8 0.1 dynamic_slice.9
  14.9 0.7 concatenate.3.ranks
  15.7 0.0 copy-start.7
  15.7 1.6 %copy-done.7 = bf16[2,1,2048,256]{3,2,1,0:T(8,128)(2,1)S(1)} copy-done((bf16[2,1,2048,256]{3,2,1,0:T(8,128)(2,1)S(1)}, bf16[2,1,2048,256]{3,2,1,0:T(8,128)(2,1)}, u32[]{:S(2)}) %copy-start.7) | copy-done | bytes 2097176
  17.2 1.6 %copy-done.8 = bf16[2,1,2048,256]{3,2,1,0:T(8,128)(2,1)S(1)} copy-done((bf16[2,1,2048,256]{3,2,1,0:T(8,128)(2,1)S(1)}, bf16[2,1,2048,256]{3,2,1,0:T(8,128)(2,1)}, u32[]{:S(2)}) %copy-start.8) | copy-done | bytes 2097176
  18.8 3.3 %prepare.1 = (bf16[2,256,256]{2,1,0:T(8,128)(2,1)S(1)}, f32[2,256,256]{2,1,0:T(8,128)S(1)}, f32[2,256,256]{2,1,0:T(8,128)S(1)}) custom-call(s32[11]{0:T(128)S(1)} %concatenate.3.ranks, bf16[2,2048,256]{2,1,0:T(8,128)(2,1)S(1)} %bitcast.28, bf16[2,2048,256]{2,1,0:T(8,128)(2,1)S(1)} %bitcast.30, bf16[2048,256]{1,0:T(8,128)(2,1)S(1)} %copy-done), custom_call_target="tpu_custom_call" | custom-call | flops 2000000000 | bytes 6000000 | tf_op jit(solution)/shard_map/prepare/pallas_call | solution.py:176
  22.2 0.0 collective-permute-done
  22.2 15.8 %all_to_all.15 = bf16[8,2,64,256]{3,2,1,0:T(8,128)(2,1)S(1)} all-to-all(bf16[8,2,64,256]{3,2,1,0:T(8,128)(2,1)S(1)} %collective-permute-done), channel_id=1, replica_groups=mesh['x'=4,'z'=4,'y'=4,'c'=2] {'y','c'}, dimensions={0} | all-to-all | bytes 1048576 | tf_op jit(solution)/shard_map/all_to_all | solution.py:441
  38.0 10.5 %collective-permute-start.3 = (bf16[512,256]{1,0:T(8,128)(2,1)S(1)}, bf16[512,256]{1,0:T(8,128)(2,1)S(1)}, u32[]{:S(2)}, u32[]{:S(2)}) collective-permute-start(bf16[512,256]{1,0:T(8,128)(2,1)S(1)} %bitcast.22), channel_id=1, source_target_pairs={{0,96},{32,0},{64,32},{96,64},{1,97},{33,1},{65,33},{97,65},{2,98}... | collective-permute-start | bytes 786440 | tf_op jit(solution)/shard_map/ppermute | solution.py:445
  48.6 0.4 collective-permute-start.2
  49.0 0.8 collective-permute-start.1
  49.8 1.9 %collective-permute-start.6 = (bf16[512,256]{1,0:T(8,128)(2,1)S(1)}, bf16[512,256]{1,0:T(8,128)(2,1)S(1)}, u32[]{:S(2)}, u32[]{:S(2)}) collective-permute-start(bf16[512,256]{1,0:T(8,128)(2,1)S(1)} %bitcast.34), channel_id=1, source_target_pairs={{0,96},{32,0},{64,32},{96,64},{1,97},{33,1},{65,33},{97,65},{2,98}... | collective-permute-start | bytes 786440 | tf_op jit(solution)/shard_map/ppermute | solution.py:445
  51.7 1.3 %collective-permute-start.5 = (bf16[512,256]{1,0:T(8,128)(2,1)S(1)}, bf16[512,256]{1,0:T(8,128)(2,1)S(1)}, u32[]{:S(2)}, u32[]{:S(2)}) collective-permute-start(bf16[512,256]{1,0:T(8,128)(2,1)S(1)} %bitcast.35), channel_id=1, source_target_pairs={{0,64},{32,96},{64,0},{96,32},{1,65},{33,97},{65,1},{97,33},{2,66}... | collective-permute-start | bytes 786440 | tf_op jit(solution)/shard_map/ppermute | solution.py:445
  53.0 6.2 %collective-permute-done.3.up3 = bf16[512,256]{1,0:T(8,128)(2,1)S(1)} collective-permute-done((bf16[512,256]{1,0:T(8,128)(2,1)S(1)}, bf16[512,256]{1,0:T(8,128)(2,1)S(1)}, u32[]{:S(2)}, u32[]{:S(2)}) %collective-permute-start.3) | collective-permute-done | bytes 262176 | tf_op jit(solution)/shard_map/ppermute | solution.py:445
  59.2 0.0 collective-permute-start.4
  59.3 0.0 collective-permute-done.2.up2
  59.3 6.1 %collective-permute-done.1.up1 = bf16[512,256]{1,0:T(8,128)(2,1)S(1)} collective-permute-done((bf16[512,256]{1,0:T(8,128)(2,1)S(1)}, bf16[512,256]{1,0:T(8,128)(2,1)S(1)}, u32[]{:S(2)}, u32[]{:S(2)}) %collective-permute-start.1) | collective-permute-done | bytes 262176 | tf_op jit(solution)/shard_map/ppermute | solution.py:445
  65.3 1.0 reach.1
  66.4 0.6 copy-done.5
  67.0 3.5 %collective-permute-done.6.vp3 = bf16[512,256]{1,0:T(8,128)(2,1)S(1)} collective-permute-done((bf16[512,256]{1,0:T(8,128)(2,1)S(1)}, bf16[512,256]{1,0:T(8,128)(2,1)S(1)}, u32[]{:S(2)}, u32[]{:S(2)}) %collective-permute-start.6) | collective-permute-done | bytes 262176 | tf_op jit(solution)/shard_map/ppermute | solution.py:445
  70.5 0.0 collective-permute-done.5.vp2
  70.5 4.7 %collective-permute-done.4.vp1 = bf16[512,256]{1,0:T(8,128)(2,1)S(1)} collective-permute-done((bf16[512,256]{1,0:T(8,128)(2,1)S(1)}, bf16[512,256]{1,0:T(8,128)(2,1)S(1)}, u32[]{:S(2)}, u32[]{:S(2)}) %collective-permute-start.4) | collective-permute-done | bytes 262176 | tf_op jit(solution)/shard_map/ppermute | solution.py:445
  75.2 7.5 %all-gather.2.cloned.1.call-done.gathered = bf16[12,2048,256]{2,1,0:T(8,128)(2,1)} async-done(((bf16[12,64,256]{2,1,0:T(8,128)(2,1)}), bf16[12,2048,256]{2,1,0:T(8,128)(2,1)}) %all-gather.2.cloned.1.call-update) | async-done | bytes 12582928 | tf_op jit(solution)/shard_map/all_gather | solution.py:429
  82.7 23.2 %tail.1 = (bf16[2,2048,256]{2,1,0:T(8,128)(2,1)}, bf16[2,2048,256]{2,1,0:T(8,128)(2,1)}) custom-call(s32[11]{0:T(128)} %copy-done.6, bf16[2,256,256]{2,1,0:T(8,128)(2,1)} %copy-done.11, f32[2,256,256]{2,1,0:T(8,128)} %copy-done.9, f32[2,256,256]{2,1,0:T(8,128)} %copy-done.10, bf16[256,256]{1,0:T(8,128)(2,1)} %copy-done.5, ...), custom_call_target="tpu_custom_call" | custom-call | flops 16000000000 | bytes 20000000 | tf_op jit(solution)/shard_map/tail/pallas_call | solution.py:376
  (38 shorter events, 0.1 us)
Async XLA Ops:
  7.2 3.9 %copy-start.20 = (s32[4]{0:T(128)S(1)}, s32[4]{0:T(128)}, u32[]{:S(2)}) copy-start(s32[4]{0:T(128)} %constant.45.clone) | copy-start | bytes 52
  7.2 7.1 %copy-start.18 = (s32[32]{0:T(128)S(1)}, s32[32]{0:T(128)}, u32[]{:S(2)}) copy-start(s32[32]{0:T(128)} %param.22) | copy-start | bytes 388
  7.2 7.6 %copy-start.19 = (s32[8]{0:T(128)S(1)}, s32[8]{0:T(128)}, u32[]{:S(2)}) copy-start(s32[8]{0:T(128)} %param.19) | copy-start | bytes 100
  7.2 7.7 %copy-start.14 = (s32[2,1]{0,1:T(1,128)S(1)}, s32[2,1]{0,1:T(1,128)}, u32[]{:S(2)}) copy-start(s32[2,1]{0,1:T(1,128)} %param.16) | copy-start | bytes 28
  7.2 7.7 %copy-start.13 = (s32[2,1]{0,1:T(1,128)S(1)}, s32[2,1]{0,1:T(1,128)}, u32[]{:S(2)}) copy-start(s32[2,1]{0,1:T(1,128)} %param.15) | copy-start | bytes 28
  7.2 8.4 %copy-start = (bf16[2048,256]{1,0:T(8,128)(2,1)S(1)}, bf16[2048,256]{1,0:T(8,128)(2,1)}, u32[]{:S(2)}) copy-start(bf16[2048,256]{1,0:T(8,128)(2,1)} %sk.3) | copy-start | bytes 3145732
  7.2 75.4 %all-gather.2.cloned.1.call-start = ((), (), s32[]{:S(2)}) async-start(), calls=%async_computation.1 | async-start | bytes 12976128 | tf_op jit(solution)/shard_map/all_gather | solution.py:429
  10.3 11.9 %collective-permute-start = (bf16[8,2,64,256]{3,2,1,0:T(8,128)(2,1)S(1)}, bf16[8,2,64,256]{3,2,1,0:T(8,128)(2,1)S(1)}, u32[]{:S(2)}, u32[]{:S(2)}) collective-permute-start(bf16[8,2,64,256]{3,2,1,0:T(8,128)(2,1)S(1)} %pad_maximum_fusion), channel_id=1, source_target_pairs={{0,0},{8,32},{16,64},{24,96},{32,72},{40,104},{48,8},{56,40},{64,1... | collective-permute-start | bytes 1572872 | tf_op jit(solution)/shard_map/ppermute | solution.py:433
  15.6 49.7 %copy-start.6 = (s32[11]{0:T(128)}, s32[11]{0:T(128)S(1)}, u32[]{:S(2)}) copy-start(s32[11]{0:T(128)S(1)} %concatenate.3.ranks) | copy-start | bytes 136
  15.7 1.6 %copy-start.7 = (bf16[2,1,2048,256]{3,2,1,0:T(8,128)(2,1)S(1)}, bf16[2,1,2048,256]{3,2,1,0:T(8,128)(2,1)}, u32[]{:S(2)}) copy-start(bf16[2,1,2048,256]{3,2,1,0:T(8,128)(2,1)} %param.13) | copy-start | bytes 6291460
  17.2 1.6 %copy-start.8 = (bf16[2,1,2048,256]{3,2,1,0:T(8,128)(2,1)S(1)}, bf16[2,1,2048,256]{3,2,1,0:T(8,128)(2,1)}, u32[]{:S(2)}) copy-start(bf16[2,1,2048,256]{3,2,1,0:T(8,128)(2,1)} %param.14) | copy-start | bytes 6291460
  22.2 15.8 %copy-start.10 = (f32[2,256,256]{2,1,0:T(8,128)}, f32[2,256,256]{2,1,0:T(8,128)S(1)}, u32[]{:S(2)}) copy-start(f32[2,256,256]{2,1,0:T(8,128)S(1)} %get-tuple-element.16.half) | copy-start | bytes 1572868
  22.2 15.9 %copy-start.11 = (bf16[2,256,256]{2,1,0:T(8,128)(2,1)}, bf16[2,256,256]{2,1,0:T(8,128)(2,1)S(1)}, u32[]{:S(2)}) copy-start(bf16[2,256,256]{2,1,0:T(8,128)(2,1)S(1)} %get-tuple-element.14.probe) | copy-start | bytes 786436
  22.2 44.2 %copy-start.9 = (f32[2,256,256]{2,1,0:T(8,128)}, f32[2,256,256]{2,1,0:T(8,128)S(1)}, u32[]{:S(2)}) copy-start(f32[2,256,256]{2,1,0:T(8,128)S(1)} %get-tuple-element.15.upper) | copy-start | bytes 1572868
  38.0 44.6 %copy-start.1 = (bf16[1,1,8,64,256]{4,3,1,2,0:T(8,128)(2,1)}, bf16[1,1,8,64,256]{4,3,1,2,0:T(8,128)(2,1)S(1)}, u32[]{:S(2)}) copy-start(bf16[1,1,8,64,256]{4,3,1,2,0:T(8,128)(2,1)S(1)} %get-tuple-element.25) | copy-start | bytes 786436
  38.0 44.6 %copy-start.12 = (bf16[1,1,8,64,256]{4,3,1,2,0:T(8,128)(2,1)}, bf16[1,1,8,64,256]{4,3,1,2,0:T(8,128)(2,1)S(1)}, u32[]{:S(2)}) copy-start(bf16[1,1,8,64,256]{4,3,1,2,0:T(8,128)(2,1)S(1)} %get-tuple-element.24) | copy-start | bytes 786436
  38.0 21.2 %collective-permute-start.3 = (bf16[512,256]{1,0:T(8,128)(2,1)S(1)}, bf16[512,256]{1,0:T(8,128)(2,1)S(1)}, u32[]{:S(2)}, u32[]{:S(2)}) collective-permute-start(bf16[512,256]{1,0:T(8,128)(2,1)S(1)} %bitcast.22), channel_id=1, source_target_pairs={{0,96},{32,0},{64,32},{96,64},{1,97},{33,1},{65,33},{97,65},{2,98}... | collective-permute-start | bytes 786440 | tf_op jit(solution)/shard_map/ppermute | solution.py:445
  48.6 10.7 %collective-permute-start.2 = (bf16[512,256]{1,0:T(8,128)(2,1)S(1)}, bf16[512,256]{1,0:T(8,128)(2,1)S(1)}, u32[]{:S(2)}, u32[]{:S(2)}) collective-permute-start(bf16[512,256]{1,0:T(8,128)(2,1)S(1)} %bitcast.23), channel_id=1, source_target_pairs={{0,64},{32,96},{64,0},{96,32},{1,65},{33,97},{65,1},{97,33},{2,66}... | collective-permute-start | bytes 786440 | tf_op jit(solution)/shard_map/ppermute | solution.py:445
  49.0 16.3 %collective-permute-start.1 = (bf16[512,256]{1,0:T(8,128)(2,1)S(1)}, bf16[512,256]{1,0:T(8,128)(2,1)S(1)}, u32[]{:S(2)}, u32[]{:S(2)}) collective-permute-start(bf16[512,256]{1,0:T(8,128)(2,1)S(1)} %bitcast.24), channel_id=1, source_target_pairs={{0,32},{32,64},{64,96},{96,0},{1,33},{33,65},{65,97},{97,1},{2,34}... | collective-permute-start | bytes 786440 | tf_op jit(solution)/shard_map/ppermute | solution.py:445
  49.8 20.7 %collective-permute-start.6 = (bf16[512,256]{1,0:T(8,128)(2,1)S(1)}, bf16[512,256]{1,0:T(8,128)(2,1)S(1)}, u32[]{:S(2)}, u32[]{:S(2)}) collective-permute-start(bf16[512,256]{1,0:T(8,128)(2,1)S(1)} %bitcast.34), channel_id=1, source_target_pairs={{0,96},{32,0},{64,32},{96,64},{1,97},{33,1},{65,33},{97,65},{2,98}... | collective-permute-start | bytes 786440 | tf_op jit(solution)/shard_map/ppermute | solution.py:445
  51.7 18.8 %collective-permute-start.5 = (bf16[512,256]{1,0:T(8,128)(2,1)S(1)}, bf16[512,256]{1,0:T(8,128)(2,1)S(1)}, u32[]{:S(2)}, u32[]{:S(2)}) collective-permute-start(bf16[512,256]{1,0:T(8,128)(2,1)S(1)} %bitcast.35), channel_id=1, source_target_pairs={{0,64},{32,96},{64,0},{96,32},{1,65},{33,97},{65,1},{97,33},{2,66}... | collective-permute-start | bytes 786440 | tf_op jit(solution)/shard_map/ppermute | solution.py:445
  59.2 23.4 %copy-start.2 = (bf16[512,256]{1,0:T(8,128)(2,1)}, bf16[512,256]{1,0:T(8,128)(2,1)S(1)}, u32[]{:S(2)}) copy-start(bf16[512,256]{1,0:T(8,128)(2,1)S(1)} %collective-permute-done.3.up3) | copy-start | bytes 786436
  59.2 15.9 %collective-permute-start.4 = (bf16[512,256]{1,0:T(8,128)(2,1)S(1)}, bf16[512,256]{1,0:T(8,128)(2,1)S(1)}, u32[]{:S(2)}, u32[]{:S(2)}) collective-permute-start(bf16[512,256]{1,0:T(8,128)(2,1)S(1)} %bitcast.36), channel_id=1, source_target_pairs={{0,32},{32,64},{64,96},{96,0},{1,33},{33,65},{65,97},{97,1},{2,34}... | collective-permute-start | bytes 786440 | tf_op jit(solution)/shard_map/ppermute | solution.py:445
  59.3 23.4 %copy-start.3 = (bf16[512,256]{1,0:T(8,128)(2,1)}, bf16[512,256]{1,0:T(8,128)(2,1)S(1)}, u32[]{:S(2)}) copy-start(bf16[512,256]{1,0:T(8,128)(2,1)S(1)} %collective-permute-done.2.up2) | copy-start | bytes 786436
  65.3 17.3 %copy-start.4 = (bf16[512,256]{1,0:T(8,128)(2,1)}, bf16[512,256]{1,0:T(8,128)(2,1)S(1)}, u32[]{:S(2)}) copy-start(bf16[512,256]{1,0:T(8,128)(2,1)S(1)} %collective-permute-done.1.up1) | copy-start | bytes 786436
  66.4 0.6 copy-start.5
  70.5 12.2 %copy-start.15 = (bf16[512,256]{1,0:T(8,128)(2,1)}, bf16[512,256]{1,0:T(8,128)(2,1)S(1)}, u32[]{:S(2)}) copy-start(bf16[512,256]{1,0:T(8,128)(2,1)S(1)} %collective-permute-done.6.vp3) | copy-start | bytes 786436
  70.5 12.2 %copy-start.16 = (bf16[512,256]{1,0:T(8,128)(2,1)}, bf16[512,256]{1,0:T(8,128)(2,1)S(1)}, u32[]{:S(2)}) copy-start(bf16[512,256]{1,0:T(8,128)(2,1)S(1)} %collective-permute-done.5.vp2) | copy-start | bytes 786436
  75.2 7.5 %copy-start.17 = (bf16[512,256]{1,0:T(8,128)(2,1)}, bf16[512,256]{1,0:T(8,128)(2,1)S(1)}, u32[]{:S(2)}) copy-start(bf16[512,256]{1,0:T(8,128)(2,1)S(1)} %collective-permute-done.4.vp1) | copy-start | bytes 786436
Sparse Core Ops, SparseCore 0:
  10.9 71.6 all-gather.1

commit v6 on v5

--- a/solution.py
+++ b/solution.py
@@ -135,22 +135,46 @@
     ]
 
 
-def pack_kernel(diag, row_v, row_u, out):
-    chunks = out.shape[0] - 4
-    rmax = out.shape[2]
-    for c in range(chunks):
-        out[c] = diag[:, rmax * c : rmax * (c + 1)].astype(BF16)
-    out[chunks : chunks + 2] = row_v[...]
-    out[chunks + 2 :] = row_u[...]
+def pack_kernel(diag, row_v, row_u, out, wide, narrow, sem):
+    chunks, _, rmax = narrow.shape
+    copies = [
+        pltpu.make_async_copy(row_v, out.at[pl.ds(chunks, 2)], sem.at[0]),
+        pltpu.make_async_copy(row_u, out.at[pl.ds(chunks + 2, 2)], sem.at[1]),
+    ]
+    loads = []
+    for k in range(4):
+        columns = pl.ds(2 * rmax * k, 2 * rmax)
+        loads.append(
+            pltpu.make_async_copy(diag.at[:, columns], wide.at[:, columns], sem.at[2 + k])
+        )
+    for copy in loads + copies:
+        copy.start()
+    for k in range(4):
+        loads[k].wait()
+        for c in (2 * k, 2 * k + 1):
+            narrow[c] = wide[:, rmax * c : rmax * (c + 1)].astype(BF16)
+        pair = pl.ds(2 * k, 2)
+        copies.append(pltpu.make_async_copy(narrow.at[pair], out.at[pair], sem.at[6 + k]))
+        copies[-1].start()
+    for copy in copies:
+        copy.wait()
 
 
 def pack(diag_inv, row_v, row_u):
     count, slab, rmax = row_v.shape
     chunks = diag_inv.shape[1] // rmax
+    hbm = pl.BlockSpec(memory_space=pl.ANY)
     return pl.pallas_call(
         pack_kernel,
         name="pack",
         out_shape=jax.ShapeDtypeStruct((chunks + 2 * count, slab, rmax), BF16),
+        in_specs=[hbm] * 3,
+        out_specs=hbm,
+        scratch_shapes=[
+            pltpu.VMEM(diag_inv.shape, F32),
+            pltpu.VMEM((chunks, slab, rmax), BF16),
+            pltpu.SemaphoreType.DMA((10,)),
+        ],
         cost_estimate=pl.CostEstimate(flops=0, bytes_accessed=1_100_000, transcendentals=0),
     )(diag_inv, row_v, row_u)
 

time: 113 us -> 116 us (1.027)
  Pallas kernels: 29.4 us -> 32.7 us
    pallas_call x1, Pallas kernels: 1.94 us -> 5.17 us  [pack(): pl.pallas_call(pack_kernel, name='pack', out_shape=jax.ShapeDtypeStruct((...]
where the time goes in v6:
time: 116 us
  Pallas kernels  32.7 us (28%)
  waiting for transfers between devices  27.9 us (24%)
  between operations  16.9 us (15%)
  blocking collectives  15.8 us (14%)
  starting transfers between devices  15.7 us (14%)
  local copies, waits for them, and re-layouts  5.92 us (5%)
    pallas_call x1, Pallas kernels, tail(): pl.pallas_call(tail_kernel, name='tail', out_shape=(tile, tile), in_specs...  23.1 us
    ppermute x6, waiting for transfers between devices, spread(): lax.ppermute(block, 'x', [(a, (a + k) % 4) for a in range(4)])  20.4 us
    all_to_all x1, blocking collectives, on_device(): lax.all_to_all(quarter, ('y', 'c'), split_axis=0, concat_axis=2, tiled=True)  15.8 us
    ppermute x6, starting transfers between devices, spread(): lax.ppermute(block, 'x', [(a, (a + k) % 4) for a in range(4)])  15 us
    all_gather x1, waiting for transfers between devices, on_device(): lax.all_gather(pack(diag_inv, row_v, row_u), ('z', 'y', 'c'), axis=1, til...  7.47 us
    pallas_call x1, Pallas kernels, pack(): pl.pallas_call(pack_kernel, name='pack', out_shape=jax.ShapeDtypeStruct((...  5.17 us
    unnamed x42, local copies, waits for them, and re-layouts  3.89 us
    pallas_call x1, Pallas kernels, prepare(): pl.pallas_call(prepare_kernel, name='prepare', grid=(2,), out_shape=(squa...  3.32 us
  transfers between devices with their start and end apart: 8, of which 5 were waited for; matrix products, arithmetic and copies ran while one was open for 3% of the time, Pallas kernels for 4%

profile of v6, /device:TPU:1, one launch (start us, length us, event | category | flops | bytes accessed | tf_op | source)
XLA Modules:
  0.0 115.9 jit_solution(14554350242695786387)
XLA Ops:
  7.2 0.0 copy-start.20
  7.2 0.0 all-gather.2.cloned.1.call-start
  7.3 5.2 %pack.1 = bf16[12,64,256]{2,1,0:T(8,128)(2,1)} custom-call(f32[64,2048]{1,0:T(8,128)} %diag.1, bf16[2,64,256]{2,1,0:T(8,128)(2,1)} %row_v.1, bf16[2,64,256]{2,1,0:T(8,128)(2,1)} %row_u.1), custom_call_target="tpu_custom_call" | custom-call | bytes 1100000 | tf_op jit(solution)/shard_map/pack/pallas_call | solution.py:167
  12.5 0.0 all-gather.2.cloned.1.call-update
  12.5 1.1 pad_maximum_fusion
  13.6 0.7 collective-permute-start
  14.3 0.6 dynamic_slice.11
  17.5 0.6 dynamic_slice.10
  18.1 0.1 dynamic_slice.9
  18.2 0.7 concatenate.3.ranks
  18.9 0.0 copy-start.7
  18.9 1.6 %copy-done.7 = bf16[2,1,2048,256]{3,2,1,0:T(8,128)(2,1)S(1)} copy-done((bf16[2,1,2048,256]{3,2,1,0:T(8,128)(2,1)S(1)}, bf16[2,1,2048,256]{3,2,1,0:T(8,128)(2,1)}, u32[]{:S(2)}) %copy-start.7) | copy-done | bytes 2097176
  20.5 1.6 %copy-done.8 = bf16[2,1,2048,256]{3,2,1,0:T(8,128)(2,1)S(1)} copy-done((bf16[2,1,2048,256]{3,2,1,0:T(8,128)(2,1)S(1)}, bf16[2,1,2048,256]{3,2,1,0:T(8,128)(2,1)}, u32[]{:S(2)}) %copy-start.8) | copy-done | bytes 2097176
  22.1 3.3 %prepare.1 = (bf16[2,256,256]{2,1,0:T(8,128)(2,1)S(1)}, f32[2,256,256]{2,1,0:T(8,128)S(1)}, f32[2,256,256]{2,1,0:T(8,128)S(1)}) custom-call(s32[11]{0:T(128)S(1)} %concatenate.3.ranks, bf16[2,2048,256]{2,1,0:T(8,128)(2,1)S(1)} %bitcast.28, bf16[2,2048,256]{2,1,0:T(8,128)(2,1)S(1)} %bitcast.30, bf16[2048,256]{1,0:T(8,128)(2,1)S(1)} %copy-done), custom_call_target="tpu_custom_call" | custom-call | flops 2000000000 | bytes 6000000 | tf_op jit(solution)/shard_map/prepare/pallas_call | solution.py:200
  25.4 0.0 collective-permute-done
  25.4 15.8 %all_to_all.15 = bf16[8,2,64,256]{3,2,1,0:T(8,128)(2,1)S(1)} all-to-all(bf16[8,2,64,256]{3,2,1,0:T(8,128)(2,1)S(1)} %collective-permute-done), channel_id=1, replica_groups=mesh['x'=4,'z'=4,'y'=4,'c'=2] {'y','c'}, dimensions={0} | all-to-all | bytes 1048576 | tf_op jit(solution)/shard_map/all_to_all | solution.py:465
  41.3 10.5 %collective-permute-start.3 = (bf16[512,256]{1,0:T(8,128)(2,1)S(1)}, bf16[512,256]{1,0:T(8,128)(2,1)S(1)}, u32[]{:S(2)}, u32[]{:S(2)}) collective-permute-start(bf16[512,256]{1,0:T(8,128)(2,1)S(1)} %bitcast.22), channel_id=1, source_target_pairs={{0,96},{32,0},{64,32},{96,64},{1,97},{33,1},{65,33},{97,65},{2,98}... | collective-permute-start | bytes 786440 | tf_op jit(solution)/shard_map/ppermute | solution.py:469
  51.8 0.4 collective-permute-start.2
  52.3 0.8 collective-permute-start.1
  53.0 1.9 %collective-permute-start.6 = (bf16[512,256]{1,0:T(8,128)(2,1)S(1)}, bf16[512,256]{1,0:T(8,128)(2,1)S(1)}, u32[]{:S(2)}, u32[]{:S(2)}) collective-permute-start(bf16[512,256]{1,0:T(8,128)(2,1)S(1)} %bitcast.34), channel_id=1, source_target_pairs={{0,96},{32,0},{64,32},{96,64},{1,97},{33,1},{65,33},{97,65},{2,98}... | collective-permute-start | bytes 786440 | tf_op jit(solution)/shard_map/ppermute | solution.py:469
  54.9 1.3 %collective-permute-start.5 = (bf16[512,256]{1,0:T(8,128)(2,1)S(1)}, bf16[512,256]{1,0:T(8,128)(2,1)S(1)}, u32[]{:S(2)}, u32[]{:S(2)}) collective-permute-start(bf16[512,256]{1,0:T(8,128)(2,1)S(1)} %bitcast.35), channel_id=1, source_target_pairs={{0,64},{32,96},{64,0},{96,32},{1,65},{33,97},{65,1},{97,33},{2,66}... | collective-permute-start | bytes 786440 | tf_op jit(solution)/shard_map/ppermute | solution.py:469
  56.2 6.3 %collective-permute-done.3.up3 = bf16[512,256]{1,0:T(8,128)(2,1)S(1)} collective-permute-done((bf16[512,256]{1,0:T(8,128)(2,1)S(1)}, bf16[512,256]{1,0:T(8,128)(2,1)S(1)}, u32[]{:S(2)}, u32[]{:S(2)}) %collective-permute-start.3) | collective-permute-done | bytes 262176 | tf_op jit(solution)/shard_map/ppermute | solution.py:469
  62.5 0.0 collective-permute-start.4
  62.5 0.0 collective-permute-done.2.up2
  62.5 6.0 %collective-permute-done.1.up1 = bf16[512,256]{1,0:T(8,128)(2,1)S(1)} collective-permute-done((bf16[512,256]{1,0:T(8,128)(2,1)S(1)}, bf16[512,256]{1,0:T(8,128)(2,1)S(1)}, u32[]{:S(2)}, u32[]{:S(2)}) %collective-permute-start.1) | collective-permute-done | bytes 262176 | tf_op jit(solution)/shard_map/ppermute | solution.py:469
  68.6 1.0 reach.1
  69.6 0.6 copy-done.5
  70.3 3.5 %collective-permute-done.6.vp3 = bf16[512,256]{1,0:T(8,128)(2,1)S(1)} collective-permute-done((bf16[512,256]{1,0:T(8,128)(2,1)S(1)}, bf16[512,256]{1,0:T(8,128)(2,1)S(1)}, u32[]{:S(2)}, u32[]{:S(2)}) %collective-permute-start.6) | collective-permute-done | bytes 262176 | tf_op jit(solution)/shard_map/ppermute | solution.py:469
  73.8 0.0 collective-permute-done.5.vp2
  73.8 4.6 %collective-permute-done.4.vp1 = bf16[512,256]{1,0:T(8,128)(2,1)S(1)} collective-permute-done((bf16[512,256]{1,0:T(8,128)(2,1)S(1)}, bf16[512,256]{1,0:T(8,128)(2,1)S(1)}, u32[]{:S(2)}, u32[]{:S(2)}) %collective-permute-start.4) | collective-permute-done | bytes 262176 | tf_op jit(solution)/shard_map/ppermute | solution.py:469
  78.4 7.5 %all-gather.2.cloned.1.call-done.gathered = bf16[12,2048,256]{2,1,0:T(8,128)(2,1)} async-done(((bf16[12,64,256]{2,1,0:T(8,128)(2,1)}), bf16[12,2048,256]{2,1,0:T(8,128)(2,1)}) %all-gather.2.cloned.1.call-update) | async-done | bytes 12582928 | tf_op jit(solution)/shard_map/all_gather | solution.py:453
  85.9 23.1 %tail.1 = (bf16[2,2048,256]{2,1,0:T(8,128)(2,1)}, bf16[2,2048,256]{2,1,0:T(8,128)(2,1)}) custom-call(s32[11]{0:T(128)} %copy-done.6, bf16[2,256,256]{2,1,0:T(8,128)(2,1)} %copy-done.11, f32[2,256,256]{2,1,0:T(8,128)} %copy-done.9, f32[2,256,256]{2,1,0:T(8,128)} %copy-done.10, bf16[256,256]{1,0:T(8,128)(2,1)} %copy-done.5, ...), custom_call_target="tpu_custom_call" | custom-call | flops 16000000000 | bytes 20000000 | tf_op jit(solution)/shard_map/tail/pallas_call | solution.py:400
  (38 shorter events, 0.1 us)
Async XLA Ops:
  7.2 7.1 %copy-start.20 = (s32[4]{0:T(128)S(1)}, s32[4]{0:T(128)}, u32[]{:S(2)}) copy-start(s32[4]{0:T(128)} %constant.45.clone) | copy-start | bytes 52
  7.2 10.3 %copy-start.18 = (s32[32]{0:T(128)S(1)}, s32[32]{0:T(128)}, u32[]{:S(2)}) copy-start(s32[32]{0:T(128)} %param.22) | copy-start | bytes 388
  7.2 10.9 %copy-start.19 = (s32[8]{0:T(128)S(1)}, s32[8]{0:T(128)}, u32[]{:S(2)}) copy-start(s32[8]{0:T(128)} %param.19) | copy-start | bytes 100
  7.2 11.0 %copy-start.14 = (s32[2,1]{0,1:T(1,128)S(1)}, s32[2,1]{0,1:T(1,128)}, u32[]{:S(2)}) copy-start(s32[2,1]{0,1:T(1,128)} %param.16) | copy-start | bytes 28
  7.2 10.9 %copy-start.13 = (s32[2,1]{0,1:T(1,128)S(1)}, s32[2,1]{0,1:T(1,128)}, u32[]{:S(2)}) copy-start(s32[2,1]{0,1:T(1,128)} %param.15) | copy-start | bytes 28
  7.2 11.7 %copy-start = (bf16[2048,256]{1,0:T(8,128)(2,1)S(1)}, bf16[2048,256]{1,0:T(8,128)(2,1)}, u32[]{:S(2)}) copy-start(bf16[2048,256]{1,0:T(8,128)(2,1)} %sk.3) | copy-start | bytes 3145732
  7.2 78.6 %all-gather.2.cloned.1.call-start = ((), (), s32[]{:S(2)}) async-start(), calls=%async_computation.1 | async-start | bytes 12976128 | tf_op jit(solution)/shard_map/all_gather | solution.py:453
  13.6 11.9 %collective-permute-start = (bf16[8,2,64,256]{3,2,1,0:T(8,128)(2,1)S(1)}, bf16[8,2,64,256]{3,2,1,0:T(8,128)(2,1)S(1)}, u32[]{:S(2)}, u32[]{:S(2)}) collective-permute-start(bf16[8,2,64,256]{3,2,1,0:T(8,128)(2,1)S(1)} %pad_maximum_fusion), channel_id=1, source_target_pairs={{0,0},{8,32},{16,64},{24,96},{32,72},{40,104},{48,8},{56,40},{64,1... | collective-permute-start | bytes 1572872 | tf_op jit(solution)/shard_map/ppermute | solution.py:457
  18.9 49.7 %copy-start.6 = (s32[11]{0:T(128)}, s32[11]{0:T(128)S(1)}, u32[]{:S(2)}) copy-start(s32[11]{0:T(128)S(1)} %concatenate.3.ranks) | copy-start | bytes 136
  18.9 1.6 %copy-start.7 = (bf16[2,1,2048,256]{3,2,1,0:T(8,128)(2,1)S(1)}, bf16[2,1,2048,256]{3,2,1,0:T(8,128)(2,1)}, u32[]{:S(2)}) copy-start(bf16[2,1,2048,256]{3,2,1,0:T(8,128)(2,1)} %param.13) | copy-start | bytes 6291460
  20.5 1.6 %copy-start.8 = (bf16[2,1,2048,256]{3,2,1,0:T(8,128)(2,1)S(1)}, bf16[2,1,2048,256]{3,2,1,0:T(8,128)(2,1)}, u32[]{:S(2)}) copy-start(bf16[2,1,2048,256]{3,2,1,0:T(8,128)(2,1)} %param.14) | copy-start | bytes 6291460
  25.4 15.8 %copy-start.10 = (f32[2,256,256]{2,1,0:T(8,128)}, f32[2,256,256]{2,1,0:T(8,128)S(1)}, u32[]{:S(2)}) copy-start(f32[2,256,256]{2,1,0:T(8,128)S(1)} %get-tuple-element.16.half) | copy-start | bytes 1572868
  25.4 15.9 %copy-start.11 = (bf16[2,256,256]{2,1,0:T(8,128)(2,1)}, bf16[2,256,256]{2,1,0:T(8,128)(2,1)S(1)}, u32[]{:S(2)}) copy-start(bf16[2,256,256]{2,1,0:T(8,128)(2,1)S(1)} %get-tuple-element.14.probe) | copy-start | bytes 786436
  25.4 44.2 %copy-start.9 = (f32[2,256,256]{2,1,0:T(8,128)}, f32[2,256,256]{2,1,0:T(8,128)S(1)}, u32[]{:S(2)}) copy-start(f32[2,256,256]{2,1,0:T(8,128)S(1)} %get-tuple-element.15.upper) | copy-start | bytes 1572868
  41.3 44.6 %copy-start.1 = (bf16[1,1,8,64,256]{4,3,1,2,0:T(8,128)(2,1)}, bf16[1,1,8,64,256]{4,3,1,2,0:T(8,128)(2,1)S(1)}, u32[]{:S(2)}) copy-start(bf16[1,1,8,64,256]{4,3,1,2,0:T(8,128)(2,1)S(1)} %get-tuple-element.25) | copy-start | bytes 786436
  41.3 44.6 %copy-start.12 = (bf16[1,1,8,64,256]{4,3,1,2,0:T(8,128)(2,1)}, bf16[1,1,8,64,256]{4,3,1,2,0:T(8,128)(2,1)S(1)}, u32[]{:S(2)}) copy-start(bf16[1,1,8,64,256]{4,3,1,2,0:T(8,128)(2,1)S(1)} %get-tuple-element.24) | copy-start | bytes 786436
  41.3 21.2 %collective-permute-start.3 = (bf16[512,256]{1,0:T(8,128)(2,1)S(1)}, bf16[512,256]{1,0:T(8,128)(2,1)S(1)}, u32[]{:S(2)}, u32[]{:S(2)}) collective-permute-start(bf16[512,256]{1,0:T(8,128)(2,1)S(1)} %bitcast.22), channel_id=1, source_target_pairs={{0,96},{32,0},{64,32},{96,64},{1,97},{33,1},{65,33},{97,65},{2,98}... | collective-permute-start | bytes 786440 | tf_op jit(solution)/shard_map/ppermute | solution.py:469
  51.8 10.7 %collective-permute-start.2 = (bf16[512,256]{1,0:T(8,128)(2,1)S(1)}, bf16[512,256]{1,0:T(8,128)(2,1)S(1)}, u32[]{:S(2)}, u32[]{:S(2)}) collective-permute-start(bf16[512,256]{1,0:T(8,128)(2,1)S(1)} %bitcast.23), channel_id=1, source_target_pairs={{0,64},{32,96},{64,0},{96,32},{1,65},{33,97},{65,1},{97,33},{2,66}... | collective-permute-start | bytes 786440 | tf_op jit(solution)/shard_map/ppermute | solution.py:469
  52.3 16.3 %collective-permute-start.1 = (bf16[512,256]{1,0:T(8,128)(2,1)S(1)}, bf16[512,256]{1,0:T(8,128)(2,1)S(1)}, u32[]{:S(2)}, u32[]{:S(2)}) collective-permute-start(bf16[512,256]{1,0:T(8,128)(2,1)S(1)} %bitcast.24), channel_id=1, source_target_pairs={{0,32},{32,64},{64,96},{96,0},{1,33},{33,65},{65,97},{97,1},{2,34}... | collective-permute-start | bytes 786440 | tf_op jit(solution)/shard_map/ppermute | solution.py:469
  53.0 20.7 %collective-permute-start.6 = (bf16[512,256]{1,0:T(8,128)(2,1)S(1)}, bf16[512,256]{1,0:T(8,128)(2,1)S(1)}, u32[]{:S(2)}, u32[]{:S(2)}) collective-permute-start(bf16[512,256]{1,0:T(8,128)(2,1)S(1)} %bitcast.34), channel_id=1, source_target_pairs={{0,96},{32,0},{64,32},{96,64},{1,97},{33,1},{65,33},{97,65},{2,98}... | collective-permute-start | bytes 786440 | tf_op jit(solution)/shard_map/ppermute | solution.py:469
  54.9 18.8 %collective-permute-start.5 = (bf16[512,256]{1,0:T(8,128)(2,1)S(1)}, bf16[512,256]{1,0:T(8,128)(2,1)S(1)}, u32[]{:S(2)}, u32[]{:S(2)}) collective-permute-start(bf16[512,256]{1,0:T(8,128)(2,1)S(1)} %bitcast.35), channel_id=1, source_target_pairs={{0,64},{32,96},{64,0},{96,32},{1,65},{33,97},{65,1},{97,33},{2,66}... | collective-permute-start | bytes 786440 | tf_op jit(solution)/shard_map/ppermute | solution.py:469
  62.5 23.4 %copy-start.2 = (bf16[512,256]{1,0:T(8,128)(2,1)}, bf16[512,256]{1,0:T(8,128)(2,1)S(1)}, u32[]{:S(2)}) copy-start(bf16[512,256]{1,0:T(8,128)(2,1)S(1)} %collective-permute-done.3.up3) | copy-start | bytes 786436
  62.5 15.9 %collective-permute-start.4 = (bf16[512,256]{1,0:T(8,128)(2,1)S(1)}, bf16[512,256]{1,0:T(8,128)(2,1)S(1)}, u32[]{:S(2)}, u32[]{:S(2)}) collective-permute-start(bf16[512,256]{1,0:T(8,128)(2,1)S(1)} %bitcast.36), channel_id=1, source_target_pairs={{0,32},{32,64},{64,96},{96,0},{1,33},{33,65},{65,97},{97,1},{2,34}... | collective-permute-start | bytes 786440 | tf_op jit(solution)/shard_map/ppermute | solution.py:469
  62.5 23.4 %copy-start.3 = (bf16[512,256]{1,0:T(8,128)(2,1)}, bf16[512,256]{1,0:T(8,128)(2,1)S(1)}, u32[]{:S(2)}) copy-start(bf16[512,256]{1,0:T(8,128)(2,1)S(1)} %collective-permute-done.2.up2) | copy-start | bytes 786436
  68.6 17.3 %copy-start.4 = (bf16[512,256]{1,0:T(8,128)(2,1)}, bf16[512,256]{1,0:T(8,128)(2,1)S(1)}, u32[]{:S(2)}) copy-start(bf16[512,256]{1,0:T(8,128)(2,1)S(1)} %collective-permute-done.1.up1) | copy-start | bytes 786436
  69.6 0.6 copy-start.5
  73.7 12.1 %copy-start.15 = (bf16[512,256]{1,0:T(8,128)(2,1)}, bf16[512,256]{1,0:T(8,128)(2,1)S(1)}, u32[]{:S(2)}) copy-start(bf16[512,256]{1,0:T(8,128)(2,1)S(1)} %collective-permute-done.6.vp3) | copy-start | bytes 786436
  73.8 12.1 %copy-start.16 = (bf16[512,256]{1,0:T(8,128)(2,1)}, bf16[512,256]{1,0:T(8,128)(2,1)S(1)}, u32[]{:S(2)}) copy-start(bf16[512,256]{1,0:T(8,128)(2,1)S(1)} %collective-permute-done.5.vp2) | copy-start | bytes 786436
  78.4 7.5 %copy-start.17 = (bf16[512,256]{1,0:T(8,128)(2,1)}, bf16[512,256]{1,0:T(8,128)(2,1)S(1)}, u32[]{:S(2)}) copy-start(bf16[512,256]{1,0:T(8,128)(2,1)S(1)} %collective-permute-done.4.vp1) | copy-start | bytes 786436
Sparse Core Ops, SparseCore 0:
  12.6 73.2 all-gather.1
